TPU v7x, 128 devices: a whole 4x4x4 slice. The times are simulated.
128 devices in a mesh: dp: 64 (over z, y, x_hi, core), mp: 2 (over x_lo).
Axes of the slice: x: 4 (x_hi: 2, x_lo: 2; x = x_hi * 2 + x_lo), y: 4, z: 4, core: 2. Of those that a mesh axis runs over, the one named last changes fastest.
Arguments:
- hidden_rows: bfloat16 [16384, 8192], P(('dp', 'mp')), may hold values from -6 to 6
- key_grads: bfloat16 [16384, 1024], P('dp', 'mp'), may hold values from -6 to 6
- loss_mask: int32 [16384], P('dp'), may hold values 0 or 1
- key_weight: bfloat16 [8192, 1024], P(None, 'mp'), may hold values from -0.1875 to 0.1875
- error_buf: bfloat16 [64, 8192, 1024], P('dp', None, 'mp'), may hold values from -6 to 6
- right_factor: float32 [1024, 64], P('mp'), may hold values from -6 to 6
Outputs:
- input_grad: bfloat16 [16384, 8192], P(('dp', 'mp'))
- update: bfloat16 [8192, 1024], P(None, 'mp')
- new_error: bfloat16 [64, 8192, 1024], P('dp', None, 'mp')
- new_factor: float32 [1024, 64], P('mp')
All inputs are finite; a program needn't handle non-finite values. No bound on the sum of `loss_mask` on one device may be relied on, other than what follows from the above.
Results may differ from a plain program's by a relative error of at most 0.00115.
Values may be sent and summed in bfloat16 or wider, within the bound.
No kernel may reach another device: no remote copies, remote signals or barrier semaphores. Data moves between devices by JAX's collectives and lax.ppermute only.
A program may use at most 256 MiB of HBM per device.

v0:
```python
import jax
import jax.numpy as jnp
from jax import lax
from jax.sharding import PartitionSpec as P


def orthonormal(left_sum, gram_matrix):
    factor_low = jnp.linalg.cholesky(gram_matrix)
    return jax.scipy.linalg.solve_triangular(factor_low, left_sum.T, lower=True).T


def local(hidden_rows, key_grads, loss_mask, key_weight, error_buf, right_factor):
    highest = lax.Precision.HIGHEST
    masked = key_grads * loss_mask[:, None].astype(jnp.bfloat16)
    token_count = masked.shape[0]
    token_slab = masked
    weight_grad = lax.dot_general(
        lax.all_gather(hidden_rows, "mp", axis=0, tiled=True),
        token_slab,
        (((0,), (0,)), ((), ())),
        preferred_element_type=jnp.float32,
    ) * token_count ** (-0.5)
    token_slab = masked
    input_grad = lax.psum_scatter(
        lax.dot_general(
            token_slab, key_weight, (((1,), (1,)), ((), ())), preferred_element_type=jnp.float32
        ),
        "mp",
        scatter_dimension=0,
        tiled=True,
    ).astype(jnp.bfloat16)
    merged = weight_grad + error_buf[0].astype(jnp.float32)
    left_part = jnp.dot(merged, right_factor, precision=highest)
    left_sum = lax.psum(left_part, "mp")
    left_sum = lax.psum(left_sum, "dp")
    gram_matrix = jnp.dot(left_sum.T, left_sum, precision=highest)
    ortho_basis = orthonormal(left_sum, gram_matrix)
    right_part = lax.dot_general(
        merged,
        ortho_basis,
        (((0,), (0,)), ((), ())),
        precision=highest,
        preferred_element_type=jnp.float32,
    )
    new_factor = lax.psum(right_part, "dp") / lax.axis_size("dp")
    estimate = jnp.dot(ortho_basis, new_factor.T, precision=highest)
    new_error = (merged - estimate).astype(jnp.bfloat16)[None]
    return (input_grad, estimate.astype(jnp.bfloat16), new_error, new_factor)


def solution(mesh):
    placed = (
        P(("dp", "mp"), None),
        P("dp", "mp"),
        P("dp"),
        P(None, "mp"),
        P("dp", None, "mp"),
        P("mp", None),
    )
    return jax.shard_map(
        local,
        mesh=mesh,
        in_specs=placed,
        out_specs=(P(("dp", "mp"), None), P(None, "mp"), P("dp", None, "mp"), P("mp", None)),
        check_vma=False,
    )
```

profile of v0, /device:TPU:1, one launch (start us, length us, event | category | flops | bytes accessed | tf_op | source)
XLA Modules:
  0.0 1535.0 jit_solution(16070821971087726351)
XLA Ops:
  7.2 0.0 all-gather.2.cloned.1.call-start
  7.2 0.7 all-gather.2.cloned.1.call-update
  7.9 0.0 all-reduce.4.cloned.1.call-start
  8.0 0.7 convert_element_type.19
  8.7 12.0 copy.10
  20.6 51.6 %all-gather.2.cloned.1.call-done = bf16[256,8192]{1,0:T(8,128)(2,1)} async-done(((bf16[128,8192]{1,0:T(8,128)(2,1)}), bf16[256,8192]{1,0:T(8,128)(2,1)}) %all-gather.2.cloned.1.call-update) | async-done | bytes 4194320 | tf_op jit(solution)/shard_map/all_gather | solution.py:18
  72.2 7.2 convert_add_fusion
  79.3 5.7 copy-done.2
  85.1 12.4 fusion.11
  97.5 0.0 all-reduce.4.cloned.1.call-update
  97.5 0.0 all-reduce.6.cloned.1.call-start
  97.6 70.6 %all-reduce.4.cloned.1.call-done = f32[8192,64]{0,1:T(8,128)} async-done(((f32[8192,64]{0,1:T(8,128)}), f32[8192,64]{0,1:T(8,128)}) %all-reduce.4.cloned.1.call-update) | async-done | bytes 2097168 | tf_op jit(solution)/shard_map/psum | solution.py:34
  168.2 0.2 all-reduce.8.cloned.1.call-start
  168.4 643.3 %all-reduce.6.cloned.1.call-done = f32[8192,64]{0,1:T(8,128)} async-done(((f32[8192,64]{0,1:T(8,128)}), f32[8192,64]{0,1:T(8,128)}) %all-reduce.6.cloned.1.call-update) | async-done | bytes 2097168 | tf_op jit(solution)/shard_map/psum | solution.py:35
  811.7 4.0 fusion.12
  815.7 0.1 copy.11
  815.8 5.8 cholesky.16
  821.7 0.6 compare_reduce_fusion
  822.4 0.7 fusion.6
  823.0 4.9 custom-call.7
  827.9 3.5 fusion.7
  831.4 20.3 %fusion.13 = f32[512,64]{0,1:T(8,128)} fusion(f32[8192,512]{0,1:T(8,128)} %copy-done.2, f32[64,8192]{1,0:T(8,128)S(1)} %fusion.7), kind=kOutput, calls=%fused_computation.22 | convolution fusion | flops 3221225472 | bytes 19005440 | tf_op jit(solution)/shard_map/dot_general | solution.py:38
  851.8 0.3 reduce-scatter.2.cloned.1.call-start
  852.0 9.0 fusion.2
  861.0 560.4 %all-reduce.8.cloned.1.call-done = f32[512,64]{0,1:T(8,128)} async-done(((f32[512,64]{0,1:T(8,128)}), f32[512,64]{0,1:T(8,128)}) %all-reduce.8.cloned.1.call-update) | async-done | bytes 131088 | tf_op jit(solution)/shard_map/psum | solution.py:45
  1421.4 0.9 broadcast_multiply_fusion
  1422.3 16.6 %fusion.10 = (bf16[8192,512]{1,0:T(8,128)(2,1)}, f32[8192,512]{1,0:T(8,128)}) fusion(f32[64,8192]{1,0:T(8,128)S(1)} %fusion.7, f32[512,64]{0,1:T(8,128)S(1)} %broadcast_multiply_fusion), kind=kOutput, calls=%fused_computation.19 | convolution fusion | flops 3225419776 | bytes 27394048 | tf_op jit(solution)/shard_map/dot_general | solution.py:46
  1439.0 17.7 %copy.12 = f32[8192,512]{0,1:T(8,128)} copy(f32[8192,512]{1,0:T(8,128)} %get-tuple-element.9) | data formatting | bytes 33554432 | tf_op jit(solution)/shard_map/dot_general | solution.py:46
  1456.6 15.5 %fusion = bf16[1,8192,512]{1,2,0:T(8,128)(2,1)} fusion(f32[8192,512]{0,1:T(8,128)} %copy-done.2, f32[8192,512]{0,1:T(8,128)} %copy.12), kind=kLoop, calls=%fused_computation.2 | loop fusion | flops 8388608 | bytes 41943040 | tf_op jit(solution)/shard_map/broadcast_in_dim | solution.py:47
  1472.1 12.0 copy.13
  1484.1 40.6 %reduce-scatter.2.cloned.1.call-done = f32[128,8192]{1,0:T(8,128)} async-done(((f32[256,8192]{1,0:T(8,128)}), f32[128,8192]{1,0:T(8,128)}) %reduce-scatter.2.cloned.1.call-update) | async-done | bytes 4194320 | tf_op jit(solution)/shard_map/reduce_scatter | solution.py:24
  1524.7 3.8 convert_element_type.20
  (14 shorter events, 0.1 us)
Async XLA Ops:
  7.2 77.9 %copy-start = (f32[512,64]{0,1:T(8,128)S(1)}, f32[512,64]{0,1:T(8,128)}, u32[]{:S(2)}) copy-start(f32[512,64]{0,1:T(8,128)} %param.11) | copy-start | bytes 393220
  7.2 65.0 %all-gather.2.cloned.1.call-start = ((), (), s32[]{:S(2)}) async-start(), calls=%async_computation.2 | async-start | bytes 6291456 | tf_op jit(solution)/shard_map/all_gather | solution.py:18
  7.9 160.2 %all-reduce.4.cloned.1.call-start = ((), (), s32[]{:S(2)}) async-start(), calls=%async_computation.3 | async-start | bytes 4194304 | tf_op jit(solution)/shard_map/psum | solution.py:34
  8.6 63.5 %copy-start.3 = (bf16[256,512]{1,0:T(8,128)(2,1)S(1)}, bf16[256,512]{1,0:T(8,128)(2,1)}, u32[]{:S(2)}) copy-start(bf16[256,512]{1,0:T(8,128)(2,1)} %param.7) | copy-start | bytes 786436
  79.3 5.7 copy-start.2
  97.5 714.2 %all-reduce.6.cloned.1.call-start = ((), (), s32[]{:S(2)}) async-start(), calls=%async_computation.4 | async-start | bytes 4194304 | tf_op jit(solution)/shard_map/psum | solution.py:35
  168.2 1253.2 %all-reduce.8.cloned.1.call-start = ((), (), s32[]{:S(2)}) async-start(), calls=%async_computation.5 | async-start | bytes 262144 | tf_op jit(solution)/shard_map/psum | solution.py:45
  851.8 672.9 %reduce-scatter.2.cloned.1.call-start = ((), (), s32[]{:S(2)}) async-start(), calls=%async_computation.1 | async-start | bytes 12582912 | tf_op jit(solution)/shard_map/reduce_scatter | solution.py:24
  1422.3 16.7 %copy-start.4 = (f32[512,64]{0,1:T(8,128)}, f32[512,64]{0,1:T(8,128)S(1)}, u32[]{:S(2)}) copy-start(f32[512,64]{0,1:T(8,128)S(1)} %broadcast_multiply_fusion) | copy-start | bytes 393220
  1456.6 71.8 %copy-start.1 = (f32[512,64]{0,1:T(8,128)S(1)}, f32[512,64]{0,1:T(8,128)}, u32[]{:S(2)}) copy-start(f32[512,64]{0,1:T(8,128)} %param.11) | copy-start | bytes 393220
Sparse Core Ops, SparseCore 0:
  9.7 62.4 all-gather.1
  97.7 70.4 all-reduce.3
  170.8 640.8 all-reduce.5
  851.9 569.4 all-reduce.7
  1423.8 100.8 reduce-scatter.1
where the time goes:
time: 1540 us; the launch traced here: 1530 us
  waiting for transfers between devices  1370 us (89%)
  matrix products  73.1 us (5%)
  local copies, waits for them, and re-layouts  47.4 us (3%)
  other arithmetic  32.9 us (2%)
    psum x1, waiting for transfers between devices, local(): left_sum = lax.psum(left_sum, 'dp')  643 us
    psum x1, waiting for transfers between devices, local(): new_factor = lax.psum(right_part, 'dp') / lax.axis_size('dp')  560 us
    psum x1, waiting for transfers between devices, local(): left_sum = lax.psum(left_part, 'mp')  70.6 us
    all_gather x1, waiting for transfers between devices, local(): lax.all_gather(hidden_rows, 'mp', axis=0, tiled=True)  51.6 us
    reduce_scatter x1, waiting for transfers between devices, local(): lax.psum_scatter(lax.dot_general(token_slab, key_weight, (((1,), (1,)), (...  40.6 us
  transfers between devices with their start and end apart: 5, of which 5 were waited for; matrix products, arithmetic and copies ran while one was open for 5% of the time, Pallas kernels for 0%

commit v1 on v0

v1 whole, which is shorter than its diff:
```python
import functools

import jax
import jax.numpy as jnp
import numpy as np
from jax import lax
from jax.experimental import pallas as pl
from jax.experimental.pallas import tpu as pltpu
from jax.sharding import Mesh
from jax.sharding import PartitionSpec as P

AXES = ("z", "y", "xh", "core", "xl")
SIZES = (4, 4, 2, 2, 2)
BF = jnp.bfloat16
F32 = jnp.float32
HIGHEST = lax.Precision.HIGHEST
BLK = 512
VMEM_LIMIT = 40 * 1024 * 1024


def permutation(z=0, y=0, x=0, core=0, flip=None):
    pairs = []
    for source in range(128):
        cz, cy, ch, cc, cl = (int(v) for v in np.unravel_index(source, SIZES))
        cx = ch * 2 + cl
        cx = (cx + x) % 4 if flip is None else flip[cx]
        target = ((cz + z) % 4, (cy + y) % 4, cx // 2, (cc + core) % 2, cx % 2)
        pairs.append((source, int(np.ravel_multi_index(target, SIZES))))
    return pairs


OTHER_CORE = permutation(core=1)
PARTNER = permutation(flip=(1, 0, 3, 2))
WRAP = permutation(flip=(3, 2, 1, 0))


def send(array, pairs):
    return lax.ppermute(array, AXES, pairs)


def sum_of_four(array, axis):
    ahead = send(array, permutation(**{axis: 1}))
    behind = send(array, permutation(**{axis: 3}))
    across = send(array, permutation(**{axis: 2}))
    return (array + across) + (ahead + behind)


def split3(value, axis):
    a = lax.reduce_precision(value, 8, 7)
    b = lax.reduce_precision(value - a, 8, 7)
    c = value - a - b
    return jnp.concatenate([a.astype(BF), b.astype(BF), c.astype(BF)], axis=axis)


def kernel_split3(value):
    a = value.astype(BF)
    rest = value - a.astype(F32)
    b = rest.astype(BF)
    c = (rest - b.astype(F32)).astype(BF)
    return a, b, c


def dot(a, b, contract):
    return lax.dot_general(a, b, ((contract[:1], contract[1:]), ((), ())), preferred_element_type=F32)


def left_kernel(core_ref, err, hid_lo, hid_hi, rfs, toks, keep, away):
    step = pl.program_id(0)
    halves = []
    for half, hid in ((0, hid_lo), (1, hid_hi)):
        wide = dot(err[half], rfs[...], (1, 0)) + dot(hid[...], toks[...], (0, 0))
        halves.append(wide[:, :64] + wide[:, 64:128] + wide[:, 128:192])
    both = jnp.concatenate(halves, axis=1)

    @pl.when(step < 4)
    def _():
        away[...] = both

    @pl.when(step >= 4)
    def _():
        keep[...] = both


def first4(i, core):
    return (jnp.minimum(i, 3), 0)


def last4(i, core):
    return (jnp.maximum(i - 4, 0), 0)


def left_part(core, err, hidden, rfs, toks):
    def block(i, c):
        return ((1 - c[0]) * 4 + i) % 8

    return pl.pallas_call(
        left_kernel,
        out_shape=(jax.ShapeDtypeStruct((2048, 128), F32), jax.ShapeDtypeStruct((2048, 128), F32)),
        grid_spec=pltpu.PrefetchScalarGridSpec(
            num_scalar_prefetch=1,
            grid=(8,),
            in_specs=[
                pl.BlockSpec((2, BLK, 512), lambda i, c: (0, block(i, c), 0)),
                pl.BlockSpec((128, BLK), lambda i, c: (0, block(i, c))),
                pl.BlockSpec((128, BLK), lambda i, c: (0, block(i, c) + 8)),
                pl.BlockSpec((512, 192), lambda i, c: (0, 0)),
                pl.BlockSpec((128, 192), lambda i, c: (0, 0)),
            ],
            out_specs=[pl.BlockSpec((BLK, 128), last4), pl.BlockSpec((BLK, 128), first4)],
        ),
        compiler_params=pltpu.CompilerParams(vmem_limit_bytes=VMEM_LIMIT),
        cost_estimate=pl.CostEstimate(flops=3 * 10**9, bytes_accessed=13 * 2**20, transcendentals=0),
        name="left_part",
    )(core, err, hidden, hidden, rfs, toks)


def right_kernel(core_ref, mine, other, err, own_lo, own_hi, oa_lo, oa_hi, ob_lo, ob_hi, masked, right, gram, z_acc, w_acc, g_acc):
    step = pl.program_id(0)

    @pl.when(step == 0)
    def _():
        z_acc[...] = jnp.zeros_like(z_acc)
        w_acc[...] = jnp.zeros_like(w_acc)
        g_acc[...] = jnp.zeros_like(g_acc)

    packed = jnp.where(step < 4, mine[...], other[...])
    for half, hids in ((0, (own_lo, oa_lo, ob_lo)), (1, (own_hi, oa_hi, ob_hi))):
        terms = jnp.concatenate(kernel_split3(packed[:, half * 64 : half * 64 + 64]), axis=1)
        rows = jnp.concatenate([h[...] for h in hids], axis=0)
        z_acc[...] += dot(rows, terms, (1, 0))
        w_acc[...] += dot(terms, err[half], (0, 0))
        g_acc[...] += dot(terms, terms, (0, 0))

    @pl.when(step == 7)
    def _():
        z = z_acc[...]
        z = (z[:, :64] + z[:, 64:128] + z[:, 128:192]) * (1.0 / 16.0)
        wide = w_acc[...] + dot(jnp.concatenate(kernel_split3(z), axis=1), masked[...], (0, 0))
        right[...] = wide[:64] + wide[64:128] + wide[128:192]
        g = g_acc[...]
        g = g[:64] + g[64:128] + g[128:192]
        gram[...] = g[:, :64] + g[:, 64:128] + g[:, 128:192]


def right_part(core, mine, other, err, own, other_a, other_b, masked):
    def block(i, c):
        return (c[0] * 4 + i) % 8

    def lo(i, c):
        return (0, block(i, c))

    def hi(i, c):
        return (0, block(i, c) + 8)

    return pl.pallas_call(
        right_kernel,
        out_shape=(jax.ShapeDtypeStruct((64, 512), F32), jax.ShapeDtypeStruct((64, 64), F32)),
        grid_spec=pltpu.PrefetchScalarGridSpec(
            num_scalar_prefetch=1,
            grid=(8,),
            in_specs=[
                pl.BlockSpec((BLK, 128), first4),
                pl.BlockSpec((BLK, 128), last4),
                pl.BlockSpec((2, BLK, 512), lambda i, c: (0, block(i, c), 0)),
                pl.BlockSpec((128, BLK), lo),
                pl.BlockSpec((128, BLK), hi),
                pl.BlockSpec((64, BLK), lo),
                pl.BlockSpec((64, BLK), hi),
                pl.BlockSpec((64, BLK), lo),
                pl.BlockSpec((64, BLK), hi),
                pl.BlockSpec((256, 512), lambda i, c: (0, 0)),
            ],
            out_specs=[pl.BlockSpec((64, 512), lambda i, c: (0, 0)), pl.BlockSpec((64, 64), lambda i, c: (0, 0))],
            scratch_shapes=[pltpu.VMEM((256, 192), F32), pltpu.VMEM((192, 512), F32), pltpu.VMEM((192, 192), F32)],
        ),
        compiler_params=pltpu.CompilerParams(vmem_limit_bytes=VMEM_LIMIT),
        cost_estimate=pl.CostEstimate(flops=4 * 10**9, bytes_accessed=14 * 2**20, transcendentals=0),
        name="right_part",
    )(core, mine, other, err, own, own, other_a, other_a, other_b, other_b, masked)


def final_kernel(core_ref, mine, other, err, own_lo, own_hi, oa_lo, oa_hi, ob_lo, ob_hi, masked, factor, update, new_error):
    step = pl.program_id(0)
    packed = jnp.where(step < 4, mine[...], other[...])
    n1 = factor[...].astype(BF)
    n2 = (factor[...] - n1.astype(F32)).astype(BF)
    factors = jnp.concatenate([n1, n2, n1], axis=0)
    for half, hids in ((0, (own_lo, oa_lo, ob_lo)), (1, (own_hi, oa_hi, ob_hi))):
        basis = packed[:, half * 64 : half * 64 + 64]
        o1 = basis.astype(BF)
        o2 = (basis - o1.astype(F32)).astype(BF)
        estimate = dot(jnp.concatenate([o1, o1, o2], axis=1), factors, (1, 0))
        rows = jnp.concatenate([h[...] for h in hids], axis=0)
        merged = dot(rows, masked[...], (0, 0)) * (1.0 / 16.0) + err[half].astype(F32)
        update[half] = estimate.astype(BF)
        new_error[half] = (merged - estimate).astype(BF)


def final_part(core, mine, other, err, own, other_a, other_b, masked, factor):
    def block(i, c):
        return (c[0] * 4 + i) % 8

    def lo(i, c):
        return (0, block(i, c))

    def hi(i, c):
        return (0, block(i, c) + 8)

    def rows(i, c):
        return (0, block(i, c), 0)

    return pl.pallas_call(
        final_kernel,
        out_shape=(jax.ShapeDtypeStruct((2, 4096, 512), BF), jax.ShapeDtypeStruct((2, 4096, 512), BF)),
        grid_spec=pltpu.PrefetchScalarGridSpec(
            num_scalar_prefetch=1,
            grid=(8,),
            in_specs=[
                pl.BlockSpec((BLK, 128), first4),
                pl.BlockSpec((BLK, 128), last4),
                pl.BlockSpec((2, BLK, 512), rows),
                pl.BlockSpec((128, BLK), lo),
                pl.BlockSpec((128, BLK), hi),
                pl.BlockSpec((64, BLK), lo),
                pl.BlockSpec((64, BLK), hi),
                pl.BlockSpec((64, BLK), lo),
                pl.BlockSpec((64, BLK), hi),
                pl.BlockSpec((256, 512), lambda i, c: (0, 0)),
                pl.BlockSpec((64, 512), lambda i, c: (0, 0)),
            ],
            out_specs=[pl.BlockSpec((2, BLK, 512), rows), pl.BlockSpec((2, BLK, 512), rows)],
        ),
        compiler_params=pltpu.CompilerParams(vmem_limit_bytes=VMEM_LIMIT),
        cost_estimate=pl.CostEstimate(flops=4 * 10**9, bytes_accessed=30 * 2**20, transcendentals=0),
        name="final_part",
    )(core, mine, other, err, own, own, other_a, other_a, other_b, other_b, masked, factor)


def input_kernel(place_ref, near, far, weight_near, weight_far, out_own, out_other):
    value = dot(near[...], weight_near[...], (1, 1)) + dot(far[...], weight_far[...], (1, 1))
    value = value.astype(BF)
    out_own[...] = value[:128]
    out_other[...] = value[128:]


def input_part(place, near, far, key_weight, weight_far):
    size = weight_far.shape[0]
    steps = size // BLK
    out = jax.ShapeDtypeStruct((128, size), BF)
    return pl.pallas_call(
        input_kernel,
        out_shape=(out, out),
        grid_spec=pltpu.PrefetchScalarGridSpec(
            num_scalar_prefetch=1,
            grid=(steps,),
            in_specs=[
                pl.BlockSpec((256, 512), lambda i, p: (0, 0)),
                pl.BlockSpec((256, 512), lambda i, p: (0, 0)),
                pl.BlockSpec((BLK, 512), lambda i, p: (p[0] + i, 0)),
                pl.BlockSpec((BLK, 512), lambda i, p: (i, 0)),
            ],
            out_specs=[pl.BlockSpec((128, BLK), lambda i, p: (0, i))] * 2,
        ),
        compiler_params=pltpu.CompilerParams(vmem_limit_bytes=VMEM_LIMIT),
        cost_estimate=pl.CostEstimate(flops=size * 524288, bytes_accessed=size * 2560, transcendentals=0),
        name="input_part",
    )(place, near, far, key_weight, weight_far)


def local(hidden_rows, key_grads, loss_mask, key_weight, error_buf, right_factor):
    core = lax.axis_index("core")
    xl = lax.axis_index("xl")
    core_arg = core.astype(jnp.int32)[None]
    err = error_buf.reshape(2, 4096, 512)

    masked = key_grads * loss_mask[:, None].astype(BF)
    masked_own = lax.dynamic_slice(masked, (xl * 128, 0), (128, 512))
    masked_other = lax.dynamic_slice(masked, ((1 - xl) * 128, 0), (128, 512))
    rfs = split3(right_factor, 1)
    wide_own = dot(masked_own, rfs, (1, 0))
    wide_other = dot(masked_other, rfs, (1, 0))
    tok_own = wide_own[:, :64] + wide_own[:, 64:128] + wide_own[:, 128:]
    tok_other = wide_other[:, :64] + wide_other[:, 64:128] + wide_other[:, 128:]
    tok = (tok_own + send(tok_other, PARTNER)) * (1.0 / 16.0)
    masked_far = send(masked_other, PARTNER)

    weight_half = lax.dynamic_slice(key_weight, (core * 4096, 0), (4096, 512))
    hidden_a, hidden_b = hidden_rows[:64], hidden_rows[64:]
    hidden_a, tok = lax.optimization_barrier((hidden_a, tok))
    far_hidden_a = send(hidden_a, PARTNER)
    far_weight = [send(weight_half[:1024], WRAP)]

    keep, away = left_part(core_arg, err, hidden_rows, rfs, split3(tok, 1))
    piece = keep + send(away, OTHER_CORE)
    piece = lax.all_to_all(piece.reshape(16, 128, 128), ("z", "y"), 0, 0, tiled=True)
    piece = jnp.sum(piece, axis=0)
    piece = sum_of_four(piece, "x")

    hidden_b, weight_b, weight_c, weight_d, piece = lax.optimization_barrier(
        (hidden_b, weight_half[1024:2048], weight_half[2048:3072], weight_half[3072:], piece)
    )
    far_hidden_b = send(hidden_b, PARTNER)
    far_weight += [send(weight_b, WRAP), send(weight_c, WRAP), send(weight_d, PARTNER)]

    mine = lax.all_to_all(jnp.broadcast_to(piece[None], (16, 128, 128)), ("z", "y"), 0, 0, tiled=True)
    mine = mine.reshape(2048, 128)
    other = send(mine, OTHER_CORE)

    masked_both = jnp.concatenate([masked_own, masked_other], axis=0)
    right, gram = right_part(core_arg, mine, other, err, hidden_rows, far_hidden_a, far_hidden_b, masked_both)
    keep = lax.dynamic_slice(right, (core * 32, 0), (32, 512))
    away = lax.dynamic_slice(right, ((1 - core) * 32, 0), (32, 512))
    total = keep + send(away, OTHER_CORE)
    total = sum_of_four(total, "y")
    total = sum_of_four(total, "z")
    total = total + send(total, permutation(x=2))
    total_other = send(total, OTHER_CORE)
    right = jnp.where(core == 0, jnp.concatenate([total, total_other]), jnp.concatenate([total_other, total]))

    factor_low = jnp.linalg.cholesky(gram)
    inverse = jax.scipy.linalg.solve_triangular(factor_low, jnp.eye(64, dtype=F32), lower=True)
    empty = jnp.zeros((64, 64), F32)
    twice = jnp.concatenate([jnp.concatenate([inverse.T, empty], 1), jnp.concatenate([empty, inverse.T], 1)], 0)
    basis_mine = jnp.dot(mine, twice, precision=HIGHEST)
    basis_other = jnp.dot(other, twice, precision=HIGHEST)

    tokens_here = jnp.stack([masked_own, masked_far])
    tokens_there = send(tokens_here, OTHER_CORE)
    near = jnp.concatenate([tokens_here[0], tokens_there[0]], axis=0)
    far = jnp.concatenate([tokens_here[1], tokens_there[1]], axis=0)
    grads_own, grads_other = [], []
    for number, weight_far in enumerate(far_weight):
        place = core_arg * 8 + number * 2
        grad_own, grad_other = input_part(place, near, far, key_weight, weight_far)
        grads_own.append(grad_own)
        grads_other.append(send(grad_other, OTHER_CORE))
    input_grad = jnp.where(
        core == 0,
        jnp.concatenate(grads_own + grads_other, axis=1),
        jnp.concatenate(grads_other + grads_own, axis=1),
    )

    factor = jnp.dot(inverse, right, precision=HIGHEST) * (1.0 / 64.0)
    update, new_error = final_part(
        core_arg, basis_mine, basis_other, err, hidden_rows, far_hidden_a, far_hidden_b, masked_both, factor
    )
    return input_grad, update.reshape(8192, 512), new_error.reshape(1, 8192, 512), factor.T


def solution(mesh):
    fine = Mesh(mesh.devices.reshape(SIZES), AXES)
    dp = ("z", "y", "xh", "core")
    placed = (
        P(AXES, None),
        P(dp, "xl"),
        P(dp),
        P(None, "xl"),
        P(dp, None, "xl"),
        P("xl", None),
    )
    return jax.shard_map(
        local,
        mesh=fine,
        in_specs=placed,
        out_specs=(P(AXES, None), P(None, "xl"), P(dp, None, "xl"), P("xl", None)),
        check_vma=False,
    )
```

time: 1540 us -> 236 us (0.15)
  waiting for transfers between devices: 1370 us -> 58 us
  matrix products: 73.1 us -> 4.96 us
  starting transfers between devices: 0.6 us -> 61.9 us
  Pallas kernels: 0 us -> 40.6 us
    psum x3 -> x0, waiting for transfers between devices: 1270 us -> none  [the longest x1 643 us: local(): left_sum = lax.psum(left_sum, 'dp')]
    dot_general x6 -> x5, matrix products: 69.6 us -> 3.99 us  [the longest x1 2.25 us: local(): basis_mine = jnp.dot(mine, twice, precision=HIGHEST)]
    all_gather x1 -> x0, waiting for transfers between devices: 51.6 us -> none  [local(): lax.all_gather(hidden_rows, 'mp', axis=0, tiled=True)]
    ppermute x0 -> x27, starting transfers between devices: none -> 49.7 us  [send(): return lax.ppermute(array, AXES, pairs)]
    ppermute x0 -> x27, waiting for transfers between devices: none -> 43 us  [send(): return lax.ppermute(array, AXES, pairs)]
    reduce_scatter x1 -> x0, waiting for transfers between devices: 40.6 us -> none  [local(): lax.psum_scatter(lax.dot_general(token_slab, key_weight, (((1,), (1,)), (...]
    pallas_call x0 -> x7, Pallas kernels: none -> 40.6 us  [the longest x1 13.3 us: final_part(): pl.pallas_call(final_kernel, out_shape=(jax.ShapeDtypeStruct((2, 4096, 51...]
    dot_general x2 -> x0, local copies, waits for them, and re-layouts: 17.7 us -> none  [the longest x1 17.7 us: local(): estimate = jnp.dot(ortho_basis, new_factor.T, precision=highest)]
  transfers between devices with their start and end apart: 5 -> 29, of which waited for: 5 -> 10; matrix products, arithmetic and copies ran while one was open for 5% -> 17% of each run, Pallas kernels for 0% -> 4%
where the time goes in v1:
time: 236 us; the launch traced here: 235 us
  starting transfers between devices  61.9 us (26%)
  waiting for transfers between devices  58 us (25%)
  Pallas kernels  40.6 us (17%)
  local copies, waits for them, and re-layouts  38.4 us (16%)
  other arithmetic  29.7 us (13%)
  matrix products  4.96 us (2%)
    ppermute x27, starting transfers between devices, send(): return lax.ppermute(array, AXES, pairs)  49.7 us
    ppermute x27, waiting for transfers between devices, send(): return lax.ppermute(array, AXES, pairs)  43 us
    unnamed x57, local copies, waits for them, and re-layouts  27.1 us
    all_to_all x1, waiting for transfers between devices, local(): lax.all_to_all(piece.reshape(16, 128, 128), ('z', 'y'), 0, 0, tiled=True)  15 us
    pallas_call x1, Pallas kernels, final_part(): pl.pallas_call(final_kernel, out_shape=(jax.ShapeDtypeStruct((2, 4096, 51...  13.3 us
    pallas_call x1, Pallas kernels, right_part(): pl.pallas_call(right_kernel, out_shape=(jax.ShapeDtypeStruct((64, 512), F...  10.2 us
    pallas_call x4, Pallas kernels, input_part(): pl.pallas_call(input_kernel, out_shape=(out, out), grid_spec=pltpu.Prefet...  9.59 us
    another operation x3, other arithmetic, local(): factor_low = jnp.linalg.cholesky(gram)  8.64 us
  transfers between devices with their start and end apart: 29, of which 10 were waited for; matrix products, arithmetic and copies ran while one was open for 17% of the time, Pallas kernels for 4%

profile of v1, /device:TPU:1, one launch (start us, length us, event | category | flops | bytes accessed | tf_op | source)
XLA Modules:
  0.0 234.6 jit_solution(5561072629684432704)
XLA Ops:
  5.2 2.1 collective-permute-start.3
  9.3 3.4 %copy-done.3 = bf16[1,8192,512]{2,1,0:T(8,128)(2,1)S(1)} copy-done((bf16[1,8192,512]{2,1,0:T(8,128)(2,1)S(1)}, bf16[1,8192,512]{2,1,0:T(8,128)(2,1)}, u32[]{:S(2)}) %copy-start.3) | copy-done | bytes 8388632
  12.7 7.4 %left_part.1 = (f32[2048,128]{1,0:T(8,128)S(1)}, f32[2048,128]{1,0:T(8,128)S(1)}) custom-call(s32[1]{0:T(128)} %bitcast.core_ref, bf16[2,4096,512]{2,1,0:T(8,128)(2,1)S(1)} %bitcast.32, bf16[128,8192]{1,0:T(8,128)(2,1)S(1)} %copy-done.2, bf16[128,8192]{1,0:T(8,128)(2,1)S(1)} %copy-done.2, bf16[512,192]{1,0:T(8,128)(2,1)S(1)} %pad_maximum_fusion.4.rfs, ...), custom_call_target="tpu_custom_call" | custom-call | flops 3000000000 | bytes 13631488 | tf_op jit(solution)/shard_map/left_part/pallas_call | solution.py:96
  20.1 2.0 collective-permute-start.4
  22.1 2.3 collective-permute-done.4
  25.5 7.9 %all-to-all-start = ((f32[16,128,128]{2,1,0:T(8,128)}), f32[16,128,128]{2,1,0:T(8,128)S(1)}, u32[]{:S(2)}, u32[]{:S(2)}) async-start(f32[16,128,128]{2,1,0:T(8,128)} %bitcast.6), calls=%async_computation | async-start | bytes 2097152 | tf_op jit(solution)/shard_map/all_to_all | solution.py:295
  34.6 15.0 %all-to-all-done = f32[16,128,128]{2,1,0:T(8,128)S(1)} async-done(((f32[16,128,128]{2,1,0:T(8,128)}), f32[16,128,128]{2,1,0:T(8,128)S(1)}, u32[]{:S(2)}, u32[]{:S(2)}) %all-to-all-start) | async-done | bytes 1048608 | tf_op jit(solution)/shard_map/all_to_all | solution.py:295
  50.3 2.5 %collective-permute-start.7 = (f32[128,128]{1,0:T(8,128)}, f32[128,128]{1,0:T(8,128)S(1)}, u32[]{:S(2)}, u32[]{:S(2)}) collective-permute-start(f32[128,128]{1,0:T(8,128)} %reduce_sum.9), channel_id=1, source_target_pairs={{0,5},{1,0},{2,7},{3,2},{4,1},{5,4},{6,3},{7,6},{8,13},{9,8},{10,1... | collective-permute-start | bytes 196616 | tf_op jit(solution)/shard_map/ppermute | solution.py:38
  54.5 4.3 %constant_dynamic-slice_fusion.4 = (bf16[1024,512]{1,0:T(8,128)(2,1)}, bf16[1024,512]{1,0:T(8,128)(2,1)}, bf16[1024,512]{1,0:T(8,128)(2,1)}, bf16[1024,512]{1,0:T(8,128)(2,1)}) fusion(bf16[8192,512]{1,0:T(8,128)(2,1)} %weight_near.7, s32[]{:T(128)S(6)} %add.119, s32[]{:T(128)S(6)} %add.118, s32[]{:T(128)S(6)} %add.117, s32[]{:T(128)S(6)} %select_n.38), kind=kLoop, calls=%fused_computation.74 | loop fusion | bytes 8388624 | tf_op jit(solution)/shard_map/slice | solution.py:300
  59.9 1.8 collective-permute-start.8
  63.4 3.7 %collective-permute-start.1 = (bf16[2,128,512]{2,1,0:T(8,128)(2,1)}, bf16[2,128,512]{2,1,0:T(8,128)(2,1)}, u32[]{:S(2)}, u32[]{:S(2)}) collective-permute-start(bf16[2,128,512]{2,1,0:T(8,128)(2,1)} %pad_maximum_fusion.2), channel_id=1, source_target_pairs={{0,2},{1,3},{2,0},{3,1},{4,6},{5,7},{6,4},{7,5},{8,10},{9,11},{10,... | collective-permute-start | bytes 786440 | tf_op jit(solution)/shard_map/ppermute | solution.py:38
  68.2 4.3 %all-to-all-start.1 = ((f32[16,128,128]{2,1,0:T(8,128)}), f32[16,128,128]{2,1,0:T(8,128)}, u32[]{:S(2)}, u32[]{:S(2)}) async-start(f32[16,128,128]{2,1,0:T(8,128)} %broadcast_in_dim.6), calls=%async_computation.1 | async-start | bytes 2097152 | tf_op jit(solution)/shard_map/all_to_all | solution.py:305
  76.1 5.9 %collective-permute-done.2.weight_far = bf16[1024,512]{1,0:T(8,128)(2,1)S(1)} collective-permute-done((bf16[1024,512]{1,0:T(8,128)(2,1)}, bf16[1024,512]{1,0:T(8,128)(2,1)S(1)}, u32[]{:S(2)}, u32[]{:S(2)}) %collective-permute-start.2) | collective-permute-done | bytes 1048608 | tf_op jit(solution)/shard_map/ppermute | solution.py:38
  82.0 3.4 %copy-done = bf16[8192,512]{1,0:T(8,128)(2,1)S(1)} copy-done((bf16[8192,512]{1,0:T(8,128)(2,1)S(1)}, bf16[8192,512]{1,0:T(8,128)(2,1)}, u32[]{:S(2)}) %copy-start) | copy-done | bytes 8388632
  87.7 7.4 %collective-permute-start.11 = (bf16[128,1024]{1,0:T(8,128)(2,1)}, bf16[128,1024]{1,0:T(8,128)(2,1)}, u32[]{:S(2)}, u32[]{:S(2)}) collective-permute-start(bf16[128,1024]{1,0:T(8,128)(2,1)} %get-tuple-element.35), channel_id=1, source_target_pairs={{0,2},{1,3},{2,0},{3,1},{4,6},{5,7},{6,4},{7,5},{8,10},{9,11},{10,... | collective-permute-start | bytes 786440 | tf_op jit(solution)/shard_map/ppermute | solution.py:38
  95.1 9.5 %collective-permute-done.8.weight_far = bf16[1024,512]{1,0:T(8,128)(2,1)} collective-permute-done((bf16[1024,512]{1,0:T(8,128)(2,1)}, bf16[1024,512]{1,0:T(8,128)(2,1)}, u32[]{:S(2)}, u32[]{:S(2)}) %collective-permute-start.8) | collective-permute-done | bytes 1048608 | tf_op jit(solution)/shard_map/ppermute | solution.py:38
  104.6 2.7 %input_part.5 = (bf16[128,1024]{1,0:T(8,128)(2,1)S(1)}, bf16[128,1024]{1,0:T(8,128)(2,1)}) custom-call(s32[1]{0:T(128)S(6)} %add.94.place_ref, bf16[256,512]{1,0:T(8,128)(2,1)S(1)} %get-tuple-element.68.near, bf16[256,512]{1,0:T(8,128)(2,1)S(1)} %pad_maximum_fusion.3.far, bf16[8192,512]{1,0:T(8,128)(2,1)S(1)} %copy-done, ...), custom_call_target="tpu_custom_call" | custom-call | flops 536870912 | bytes 2621440 | tf_op jit(solution)/shard_map/input_part/pallas_call | solution.py:250
  107.9 7.4 %collective-permute-start.12 = (bf16[128,1024]{1,0:T(8,128)(2,1)}, bf16[128,1024]{1,0:T(8,128)(2,1)}, u32[]{:S(2)}, u32[]{:S(2)}) collective-permute-start(bf16[128,1024]{1,0:T(8,128)(2,1)} %get-tuple-element.36), channel_id=1, source_target_pairs={{0,2},{1,3},{2,0},{3,1},{4,6},{5,7},{6,4},{7,5},{8,10},{9,11},{10,... | collective-permute-start | bytes 786440 | tf_op jit(solution)/shard_map/ppermute | solution.py:38
  115.6 11.4 %collective-permute-done.9.weight_far = bf16[1024,512]{1,0:T(8,128)(2,1)} collective-permute-done((bf16[1024,512]{1,0:T(8,128)(2,1)}, bf16[1024,512]{1,0:T(8,128)(2,1)}, u32[]{:S(2)}, u32[]{:S(2)}) %collective-permute-start.9) | collective-permute-done | bytes 1048608 | tf_op jit(solution)/shard_map/ppermute | solution.py:38
  127.0 3.4 %copy-done.1 = bf16[8192,512]{1,0:T(8,128)(2,1)S(1)} copy-done((bf16[8192,512]{1,0:T(8,128)(2,1)S(1)}, bf16[8192,512]{1,0:T(8,128)(2,1)}, u32[]{:S(2)}) %copy-start.1) | copy-done | bytes 8388632
  131.4 2.7 %input_part.6 = (bf16[128,1024]{1,0:T(8,128)(2,1)S(1)}, bf16[128,1024]{1,0:T(8,128)(2,1)}) custom-call(s32[1]{0:T(128)S(6)} %add.104.place_ref, bf16[256,512]{1,0:T(8,128)(2,1)S(1)} %copy-done.5, bf16[256,512]{1,0:T(8,128)(2,1)S(1)} %pad_maximum_fusion.3.far, bf16[8192,512]{1,0:T(8,128)(2,1)S(1)} %copy-done.1, ...), custom_call_target="tpu_custom_call" | custom-call | flops 536870912 | bytes 2621440 | tf_op jit(solution)/shard_map/input_part/pallas_call | solution.py:250
  134.0 3.9 %collective-permute-start.13 = (bf16[128,1024]{1,0:T(8,128)(2,1)}, bf16[128,1024]{1,0:T(8,128)(2,1)}, u32[]{:S(2)}, u32[]{:S(2)}) collective-permute-start(bf16[128,1024]{1,0:T(8,128)(2,1)} %get-tuple-element.37), channel_id=1, source_target_pairs={{0,2},{1,3},{2,0},{3,1},{4,6},{5,7},{6,4},{7,5},{8,10},{9,11},{10,... | collective-permute-start | bytes 786440 | tf_op jit(solution)/shard_map/ppermute | solution.py:38
  137.9 2.7 %input_part.7 = (bf16[128,1024]{1,0:T(8,128)(2,1)S(1)}, bf16[128,1024]{1,0:T(8,128)(2,1)}) custom-call(s32[1]{0:T(128)S(6)} %add.105.place_ref, bf16[256,512]{1,0:T(8,128)(2,1)S(1)} %copy-done.5, bf16[256,512]{1,0:T(8,128)(2,1)S(1)} %pad_maximum_fusion.3.far, bf16[8192,512]{1,0:T(8,128)(2,1)S(1)} %copy-done.1, ...), custom_call_target="tpu_custom_call" | custom-call | flops 536870912 | bytes 2621440 | tf_op jit(solution)/shard_map/input_part/pallas_call | solution.py:250
  158.1 9.7 %collective-permute-done.17.ob_lo.ob_hi = bf16[64,8192]{1,0:T(8,128)(2,1)} collective-permute-done((bf16[64,8192]{1,0:T(8,128)(2,1)}, bf16[64,8192]{1,0:T(8,128)(2,1)}, u32[]{:S(2)}, u32[]{:S(2)}) %collective-permute-start.17) | collective-permute-done | bytes 1048608 | tf_op jit(solution)/shard_map/ppermute | solution.py:38
  167.8 10.2 %right_part.1 = (f32[64,512]{1,0:T(8,128)S(1)}, f32[64,64]{1,0:T(8,128)S(1)}) custom-call(s32[1]{0:T(128)} %bitcast.core_ref, f32[2048,128]{1,0:T(8,128)} %bitcast.7.mine, f32[2048,128]{1,0:T(8,128)S(1)} %collective-permute-done.15.other, bf16[2,4096,512]{2,1,0:T(8,128)(2,1)} %bitcast.30, bf16[128,8192]{1,0:T(8,128)(2,1)S(1)} %copy-done.2, ...), custom_call_target="tpu_custom_call" | custom-call | flops 4000000000 | bytes 14680064 | tf_op jit(solution)/shard_map/right_part/pallas_call | solution.py:155
  181.5 7.2 %cholesky.17 = f32[64,64]{1,0:T(8,128)} custom-call(f32[64,64]{1,0:T(8,128)} %fusion.19), custom_call_target="Cholesky" | custom-call | tf_op jit(solution)/shard_map/jit(cholesky)/cholesky | solution.py:320
  193.8 1.8 collective-permute-start.19
  195.6 1.9 fusion.12
  197.6 6.3 %custom-call.7 = f32[1,64,64]{1,2,0:T(8,128)} custom-call(f32[1,64,64]{2,1,0:T(8,128)} %fusion.12), custom_call_target="InvertDiagBlocksLowerTriangular" | custom-call | tf_op jit(solution)/shard_map/jit(_solve_triangular)/triangular_solve | solution.py:321
  211.9 2.3 fusion.11.mine
  215.9 3.9 %collective-permute-start.26 = (f32[32,512]{1,0:T(8,128)S(1)}, f32[32,512]{1,0:T(8,128)S(1)}, u32[]{:S(2)}, u32[]{:S(2)}) collective-permute-start(f32[32,512]{1,0:T(8,128)S(1)} %add.116), channel_id=1, source_target_pairs={{0,2},{1,3},{2,0},{3,1},{4,6},{5,7},{6,4},{7,5},{8,10},{9,11},{10,... | collective-permute-start | bytes 196616 | tf_op jit(solution)/shard_map/ppermute | solution.py:38
  221.2 13.3 %final_part.1 = (bf16[2,4096,512]{2,1,0:T(8,128)(2,1)}, bf16[2,4096,512]{2,1,0:T(8,128)(2,1)}) custom-call(s32[1]{0:T(128)} %bitcast.core_ref, f32[2048,128]{1,0:T(8,128)S(1)} %fusion.11.mine, f32[2048,128]{1,0:T(8,128)S(1)} %fusion.10.other, bf16[2,4096,512]{2,1,0:T(8,128)(2,1)} %bitcast.31, bf16[128,8192]{1,0:T(8,128)(2,1)S(1)} %copy-done.2, ...), custom_call_target="tpu_custom_call" | custom-call | flops 4000000000 | bytes 31457280 | tf_op jit(solution)/shard_map/final_part/pallas_call | solution.py:212
  (132 shorter events, 59.9 us)
Async XLA Ops:
  4.7 28.6 %copy-start.20 = (bf16[128,512]{1,0:T(8,128)(2,1)}, bf16[128,512]{1,0:T(8,128)(2,1)S(1)}, u32[]{:S(2)}) copy-start(bf16[128,512]{1,0:T(8,128)(2,1)S(1)} %get-tuple-element.65) | copy-start | bytes 393220
  5.2 3.9 %collective-permute-start.3 = (f32[128,64]{1,0:T(8,128)S(1)}, f32[128,64]{1,0:T(8,128)S(1)}, u32[]{:S(2)}, u32[]{:S(2)}) collective-permute-start(f32[128,64]{1,0:T(8,128)S(1)} %slice_add_fusion), channel_id=1, source_target_pairs={{0,1},{1,0},{2,3},{3,2},{4,5},{5,4},{6,7},{7,6},{8,9},{9,8},{10,11... | collective-permute-start | bytes 98312 | tf_op jit(solution)/shard_map/ppermute | solution.py:38
  20.1 4.3 %collective-permute-start.4 = (f32[2048,128]{1,0:T(8,128)S(1)}, f32[2048,128]{1,0:T(8,128)S(1)}, u32[]{:S(2)}, u32[]{:S(2)}) collective-permute-start(f32[2048,128]{1,0:T(8,128)S(1)} %get-tuple-element.28), channel_id=1, source_target_pairs={{0,2},{1,3},{2,0},{3,1},{4,6},{5,7},{6,4},{7,5},{8,10},{9,11},{10,... | collective-permute-start | bytes 3145736 | tf_op jit(solution)/shard_map/ppermute | solution.py:38
  25.5 24.2 %all-to-all-start = ((f32[16,128,128]{2,1,0:T(8,128)}), f32[16,128,128]{2,1,0:T(8,128)S(1)}, u32[]{:S(2)}, u32[]{:S(2)}) async-start(f32[16,128,128]{2,1,0:T(8,128)} %bitcast.6), calls=%async_computation | async-start | bytes 2097152 | tf_op jit(solution)/shard_map/all_to_all | solution.py:295
  33.3 29.3 %collective-permute-start = (bf16[128,512]{1,0:T(8,128)(2,1)S(1)}, bf16[128,512]{1,0:T(8,128)(2,1)S(1)}, u32[]{:S(2)}, u32[]{:S(2)}) collective-permute-start(bf16[128,512]{1,0:T(8,128)(2,1)S(1)} %get-tuple-element.65), channel_id=1, source_target_pairs={{0,1},{1,0},{2,3},{3,2},{4,5},{5,4},{6,7},{7,6},{8,9},{9,8},{10,11... | collective-permute-start | bytes 393224 | tf_op jit(solution)/shard_map/ppermute | solution.py:38
  50.3 9.5 %collective-permute-start.7 = (f32[128,128]{1,0:T(8,128)}, f32[128,128]{1,0:T(8,128)S(1)}, u32[]{:S(2)}, u32[]{:S(2)}) collective-permute-start(f32[128,128]{1,0:T(8,128)} %reduce_sum.9), channel_id=1, source_target_pairs={{0,5},{1,0},{2,7},{3,2},{4,1},{5,4},{6,3},{7,6},{8,13},{9,8},{10,1... | collective-permute-start | bytes 196616 | tf_op jit(solution)/shard_map/ppermute | solution.py:38
  52.8 7.0 %collective-permute-start.6 = (f32[128,128]{1,0:T(8,128)}, f32[128,128]{1,0:T(8,128)S(1)}, u32[]{:S(2)}, u32[]{:S(2)}) collective-permute-start(f32[128,128]{1,0:T(8,128)} %reduce_sum.9), channel_id=1, source_target_pairs={{0,1},{1,4},{2,3},{3,6},{4,5},{5,0},{6,7},{7,2},{8,9},{9,12},{10,1... | collective-permute-start | bytes 196616 | tf_op jit(solution)/shard_map/ppermute | solution.py:38
  52.8 7.0 %collective-permute-start.5 = (f32[128,128]{1,0:T(8,128)}, f32[128,128]{1,0:T(8,128)S(1)}, u32[]{:S(2)}, u32[]{:S(2)}) collective-permute-start(f32[128,128]{1,0:T(8,128)} %reduce_sum.9), channel_id=1, source_target_pairs={{0,4},{1,5},{2,6},{3,7},{4,0},{5,1},{6,2},{7,3},{8,12},{9,13},{10,... | collective-permute-start | bytes 196616 | tf_op jit(solution)/shard_map/ppermute | solution.py:38
  58.9 23.1 %collective-permute-start.2 = (bf16[1024,512]{1,0:T(8,128)(2,1)}, bf16[1024,512]{1,0:T(8,128)(2,1)S(1)}, u32[]{:S(2)}, u32[]{:S(2)}) collective-permute-start(bf16[1024,512]{1,0:T(8,128)(2,1)} %get-tuple-element.49), channel_id=1, source_target_pairs={{0,5},{1,4},{2,7},{3,6},{4,1},{5,0},{6,3},{7,2},{8,13},{9,12},{10,... | collective-permute-start | bytes 3145736 | tf_op jit(solution)/shard_map/ppermute | solution.py:38
  59.9 44.7 %collective-permute-start.8 = (bf16[1024,512]{1,0:T(8,128)(2,1)}, bf16[1024,512]{1,0:T(8,128)(2,1)}, u32[]{:S(2)}, u32[]{:S(2)}) collective-permute-start(bf16[1024,512]{1,0:T(8,128)(2,1)} %get-tuple-element.29), channel_id=1, source_target_pairs={{0,5},{1,4},{2,7},{3,6},{4,1},{5,0},{6,3},{7,2},{8,13},{9,12},{10,... | collective-permute-start | bytes 3145736 | tf_op jit(solution)/shard_map/ppermute | solution.py:38
  61.7 65.3 %collective-permute-start.9 = (bf16[1024,512]{1,0:T(8,128)(2,1)}, bf16[1024,512]{1,0:T(8,128)(2,1)}, u32[]{:S(2)}, u32[]{:S(2)}) collective-permute-start(bf16[1024,512]{1,0:T(8,128)(2,1)} %get-tuple-element.31), channel_id=1, source_target_pairs={{0,5},{1,4},{2,7},{3,6},{4,1},{5,0},{6,3},{7,2},{8,13},{9,12},{10,... | collective-permute-start | bytes 3145736 | tf_op jit(solution)/shard_map/ppermute | solution.py:38
  62.6 75.3 %collective-permute-start.10 = (bf16[1024,512]{1,0:T(8,128)(2,1)}, bf16[1024,512]{1,0:T(8,128)(2,1)}, u32[]{:S(2)}, u32[]{:S(2)}) collective-permute-start(bf16[1024,512]{1,0:T(8,128)(2,1)} %get-tuple-element.33), channel_id=1, source_target_pairs={{0,1},{1,0},{2,3},{3,2},{4,5},{5,4},{6,7},{7,6},{8,9},{9,8},{10,11... | collective-permute-start | bytes 3145736 | tf_op jit(solution)/shard_map/ppermute | solution.py:38
  63.4 9.1 %collective-permute-start.1 = (bf16[2,128,512]{2,1,0:T(8,128)(2,1)}, bf16[2,128,512]{2,1,0:T(8,128)(2,1)}, u32[]{:S(2)}, u32[]{:S(2)}) collective-permute-start(bf16[2,128,512]{2,1,0:T(8,128)(2,1)} %pad_maximum_fusion.2), channel_id=1, source_target_pairs={{0,2},{1,3},{2,0},{3,1},{4,6},{5,7},{6,4},{7,5},{8,10},{9,11},{10,... | collective-permute-start | bytes 786440 | tf_op jit(solution)/shard_map/ppermute | solution.py:38
  68.2 75.2 %all-to-all-start.1 = ((f32[16,128,128]{2,1,0:T(8,128)}), f32[16,128,128]{2,1,0:T(8,128)}, u32[]{:S(2)}, u32[]{:S(2)}) async-start(f32[16,128,128]{2,1,0:T(8,128)} %broadcast_in_dim.6), calls=%async_computation.1 | async-start | bytes 2097152 | tf_op jit(solution)/shard_map/all_to_all | solution.py:305
  76.1 28.5 %copy-start.4 = (bf16[256,512]{1,0:T(8,128)(2,1)}, bf16[256,512]{1,0:T(8,128)(2,1)S(1)}, u32[]{:S(2)}) copy-start(bf16[256,512]{1,0:T(8,128)(2,1)S(1)} %get-tuple-element.68.near) | copy-start | bytes 786436
  87.7 53.7 %collective-permute-start.11 = (bf16[128,1024]{1,0:T(8,128)(2,1)}, bf16[128,1024]{1,0:T(8,128)(2,1)}, u32[]{:S(2)}, u32[]{:S(2)}) collective-permute-start(bf16[128,1024]{1,0:T(8,128)(2,1)} %get-tuple-element.35), channel_id=1, source_target_pairs={{0,2},{1,3},{2,0},{3,1},{4,6},{5,7},{6,4},{7,5},{8,10},{9,11},{10,... | collective-permute-start | bytes 786440 | tf_op jit(solution)/shard_map/ppermute | solution.py:38
  107.9 35.5 %collective-permute-start.12 = (bf16[128,1024]{1,0:T(8,128)(2,1)}, bf16[128,1024]{1,0:T(8,128)(2,1)}, u32[]{:S(2)}, u32[]{:S(2)}) collective-permute-start(bf16[128,1024]{1,0:T(8,128)(2,1)} %get-tuple-element.36), channel_id=1, source_target_pairs={{0,2},{1,3},{2,0},{3,1},{4,6},{5,7},{6,4},{7,5},{8,10},{9,11},{10,... | collective-permute-start | bytes 786440 | tf_op jit(solution)/shard_map/ppermute | solution.py:38
  115.3 42.7 %collective-permute-start.16 = (bf16[64,8192]{1,0:T(8,128)(2,1)}, bf16[64,8192]{1,0:T(8,128)(2,1)S(1)}, u32[]{:S(2)}, u32[]{:S(2)}) collective-permute-start(bf16[64,8192]{1,0:T(8,128)(2,1)} %get-tuple-element.40), channel_id=1, source_target_pairs={{0,1},{1,0},{2,3},{3,2},{4,5},{5,4},{6,7},{7,6},{8,9},{9,8},{10,11... | collective-permute-start | bytes 3145736 | tf_op jit(solution)/shard_map/ppermute | solution.py:38
  134.0 12.0 %collective-permute-start.13 = (bf16[128,1024]{1,0:T(8,128)(2,1)}, bf16[128,1024]{1,0:T(8,128)(2,1)}, u32[]{:S(2)}, u32[]{:S(2)}) collective-permute-start(bf16[128,1024]{1,0:T(8,128)(2,1)} %get-tuple-element.37), channel_id=1, source_target_pairs={{0,2},{1,3},{2,0},{3,1},{4,6},{5,7},{6,4},{7,5},{8,10},{9,11},{10,... | collective-permute-start | bytes 786440 | tf_op jit(solution)/shard_map/ppermute | solution.py:38
  141.3 6.4 %collective-permute-start.14 = (bf16[128,1024]{1,0:T(8,128)(2,1)}, bf16[128,1024]{1,0:T(8,128)(2,1)}, u32[]{:S(2)}, u32[]{:S(2)}) collective-permute-start(bf16[128,1024]{1,0:T(8,128)(2,1)} %get-tuple-element.38), channel_id=1, source_target_pairs={{0,2},{1,3},{2,0},{3,1},{4,6},{5,7},{6,4},{7,5},{8,10},{9,11},{10,... | collective-permute-start | bytes 786440 | tf_op jit(solution)/shard_map/ppermute | solution.py:38
  143.1 24.7 %collective-permute-start.17 = (bf16[64,8192]{1,0:T(8,128)(2,1)}, bf16[64,8192]{1,0:T(8,128)(2,1)}, u32[]{:S(2)}, u32[]{:S(2)}) collective-permute-start(bf16[64,8192]{1,0:T(8,128)(2,1)} %get-tuple-element.41), channel_id=1, source_target_pairs={{0,1},{1,0},{2,3},{3,2},{4,5},{5,4},{6,7},{7,6},{8,9},{9,8},{10,11... | collective-permute-start | bytes 3145736 | tf_op jit(solution)/shard_map/ppermute | solution.py:38
  143.4 24.3 %collective-permute-start.15 = (f32[2048,128]{1,0:T(8,128)}, f32[2048,128]{1,0:T(8,128)S(1)}, u32[]{:S(2)}, u32[]{:S(2)}) collective-permute-start(f32[2048,128]{1,0:T(8,128)} %bitcast.7.mine), channel_id=1, source_target_pairs={{0,2},{1,3},{2,0},{3,1},{4,6},{5,7},{6,4},{7,5},{8,10},{9,11},{10,... | collective-permute-start | bytes 3145736 | tf_op jit(solution)/shard_map/ppermute | solution.py:38
  189.5 2.2 collective-permute-start.18
  192.3 11.5 %collective-permute-start.21 = (f32[32,512]{1,0:T(8,128)}, f32[32,512]{1,0:T(8,128)S(1)}, u32[]{:S(2)}, u32[]{:S(2)}) collective-permute-start(f32[32,512]{1,0:T(8,128)} %dynamic-slice_add_fusion), channel_id=1, source_target_pairs={{0,24},{1,25},{2,26},{3,27},{4,28},{5,29},{6,30},{7,31},{8,0},{9,1... | collective-permute-start | bytes 196616 | tf_op jit(solution)/shard_map/ppermute | solution.py:38
  192.9 11.0 %collective-permute-start.20 = (f32[32,512]{1,0:T(8,128)}, f32[32,512]{1,0:T(8,128)S(1)}, u32[]{:S(2)}, u32[]{:S(2)}) collective-permute-start(f32[32,512]{1,0:T(8,128)} %dynamic-slice_add_fusion), channel_id=1, source_target_pairs={{0,8},{1,9},{2,10},{3,11},{4,12},{5,13},{6,14},{7,15},{8,16},{9,17... | collective-permute-start | bytes 196616 | tf_op jit(solution)/shard_map/ppermute | solution.py:38
  193.8 10.0 %collective-permute-start.19 = (f32[32,512]{1,0:T(8,128)}, f32[32,512]{1,0:T(8,128)}, u32[]{:S(2)}, u32[]{:S(2)}) collective-permute-start(f32[32,512]{1,0:T(8,128)} %dynamic-slice_add_fusion), channel_id=1, source_target_pairs={{0,16},{1,17},{2,18},{3,19},{4,20},{5,21},{6,22},{7,23},{8,24},{9,... | collective-permute-start | bytes 196616 | tf_op jit(solution)/shard_map/ppermute | solution.py:38
  203.8 16.0 %copy-start.7 = (f32[2048,128]{1,0:T(8,128)S(1)}, f32[2048,128]{1,0:T(8,128)}, u32[]{:S(2)}) copy-start(f32[2048,128]{1,0:T(8,128)} %copy-done.6) | copy-start | bytes 3145732
  204.8 4.1 %collective-permute-start.24 = (f32[32,512]{1,0:T(8,128)S(1)}, f32[32,512]{1,0:T(8,128)S(1)}, u32[]{:S(2)}, u32[]{:S(2)}) collective-permute-start(f32[32,512]{1,0:T(8,128)S(1)} %add_add_fusion.1), channel_id=1, source_target_pairs={{0,96},{1,97},{2,98},{3,99},{4,100},{5,101},{6,102},{7,103},{8,104... | collective-permute-start | bytes 196616 | tf_op jit(solution)/shard_map/ppermute | solution.py:38
  206.0 4.3 %collective-permute-start.23 = (f32[32,512]{1,0:T(8,128)S(1)}, f32[32,512]{1,0:T(8,128)S(1)}, u32[]{:S(2)}, u32[]{:S(2)}) collective-permute-start(f32[32,512]{1,0:T(8,128)S(1)} %add_add_fusion.1), channel_id=1, source_target_pairs={{0,32},{1,33},{2,34},{3,35},{4,36},{5,37},{6,38},{7,39},{8,40},{9,... | collective-permute-start | bytes 196616 | tf_op jit(solution)/shard_map/ppermute | solution.py:38
  206.4 4.8 %collective-permute-start.22 = (f32[32,512]{1,0:T(8,128)S(1)}, f32[32,512]{1,0:T(8,128)S(1)}, u32[]{:S(2)}, u32[]{:S(2)}) collective-permute-start(f32[32,512]{1,0:T(8,128)S(1)} %add_add_fusion.1), channel_id=1, source_target_pairs={{0,64},{1,65},{2,66},{3,67},{4,68},{5,69},{6,70},{7,71},{8,72},{9,... | collective-permute-start | bytes 196616 | tf_op jit(solution)/shard_map/ppermute | solution.py:38
  211.2 4.7 %collective-permute-start.25 = (f32[32,512]{1,0:T(8,128)S(1)}, f32[32,512]{1,0:T(8,128)S(1)}, u32[]{:S(2)}, u32[]{:S(2)}) collective-permute-start(f32[32,512]{1,0:T(8,128)S(1)} %add_add_fusion), channel_id=1, source_target_pairs={{0,4},{1,5},{2,6},{3,7},{4,0},{5,1},{6,2},{7,3},{8,12},{9,13},{10,... | collective-permute-start | bytes 196616 | tf_op jit(solution)/shard_map/ppermute | solution.py:38
  215.9 5.0 %collective-permute-start.26 = (f32[32,512]{1,0:T(8,128)S(1)}, f32[32,512]{1,0:T(8,128)S(1)}, u32[]{:S(2)}, u32[]{:S(2)}) collective-permute-start(f32[32,512]{1,0:T(8,128)S(1)} %add.116), channel_id=1, source_target_pairs={{0,2},{1,3},{2,0},{3,1},{4,6},{5,7},{6,4},{7,5},{8,10},{9,11},{10,... | collective-permute-start | bytes 196616 | tf_op jit(solution)/shard_map/ppermute | solution.py:38
  (20 other events, 116.1 us)

commit v2 on v0

v2 whole, which is shorter than its diff:
```python
import functools

import jax
import jax.numpy as jnp
import numpy as np
from jax import lax
from jax.experimental import pallas as pl
from jax.experimental.pallas import tpu as pltpu
from jax.sharding import Mesh
from jax.sharding import PartitionSpec as P

AXES = ("z", "y", "xh", "core", "xl")
SIZES = (4, 4, 2, 2, 2)
BF = jnp.bfloat16
F32 = jnp.float32
HIGHEST = lax.Precision.HIGHEST
BLK = 512
AHEAD = 4
SLOTS = 16
COUNT = 8192 // BLK
HALF = COUNT // 2


def permutation(z=0, y=0, x=0, core=0, flip=None):
    pairs = []
    for source in range(128):
        cz, cy, ch, cc, cl = (int(v) for v in np.unravel_index(source, SIZES))
        cx = ch * 2 + cl
        cx = (cx + x) % 4 if flip is None else flip[cx]
        target = ((cz + z) % 4, (cy + y) % 4, cx // 2, (cc + core) % 2, cx % 2)
        pairs.append((source, int(np.ravel_multi_index(target, SIZES))))
    return pairs


OTHER_CORE = permutation(core=1)
PARTNER = permutation(flip=(1, 0, 3, 2))
WRAP = permutation(flip=(3, 2, 1, 0))


def send(array, pairs):
    return lax.ppermute(array, AXES, pairs)


def sum_of_four(array, axis):
    ahead = send(array, permutation(**{axis: 1}))
    behind = send(array, permutation(**{axis: 3}))
    across = send(array, permutation(**{axis: 2}))
    return (array + across) + (ahead + behind)


def kernel_split3(value):
    a = value.astype(BF)
    rest = value - a.astype(F32)
    b = rest.astype(BF)
    c = (rest - b.astype(F32)).astype(BF)
    return a, b, c


def stack3(value):
    return jnp.concatenate(kernel_split3(value), axis=0)


def sum3(value):
    return value[:64] + value[64:128] + value[128:192]


def dot(a, b, contract):
    return lax.dot_general(a, b, ((contract[:1], contract[1:]), ((), ())), preferred_element_type=F32)


def start(copies):
    for copy in copies:
        copy.start()


def wait(copies):
    for copy in copies:
        copy.wait()


def call(kernel, name, operands, outs, scratch, limit, aliases=None, hbm=False):
    anywhere = pl.BlockSpec(memory_space=pl.ANY)
    far = [pltpu.with_memory_space_constraint(array, pltpu.HBM) for array in operands[1:]]
    return pl.pallas_call(
        kernel,
        out_shape=[(pltpu.HBM if hbm else jax.ShapeDtypeStruct)(shape, dtype) for shape, dtype in outs],
        in_specs=[pl.BlockSpec(memory_space=pltpu.SMEM)] + [pl.BlockSpec(memory_space=pltpu.HBM)] * len(far),
        out_specs=[anywhere] * len(outs),
        scratch_shapes=scratch,
        input_output_aliases=aliases or {},
        compiler_params=pltpu.CompilerParams(vmem_limit_bytes=limit * 2**20),
        cost_estimate=pl.CostEstimate(flops=1024, bytes_accessed=1024, transcendentals=0),
        name=name,
    )(operands[0], *far)


def rows_of(block):
    return pl.ds(pl.multiple_of(block * BLK, BLK), BLK)


def error_loads(err, v_err, sems, places):
    return [pltpu.make_async_copy(err.at[rows_of(p), :], v_err.at[p], sems.at[j]) for j, p in enumerate(places)]


class Group:
    def __init__(self, copies):
        self.copies = copies

    def start(self):
        start(self.copies)

    def wait(self):
        wait(self.copies)


def hidden_loads(hidden, v_hid, sems, places):
    groups = []
    for j, place in enumerate(places):
        copies, row = [], 0
        for number, part in enumerate(hidden):
            size = part.shape[0]
            copies.append(
                pltpu.make_async_copy(part.at[:, rows_of(place)], v_hid.at[place, pl.ds(row, size), :], sems.at[j, number])
            )
            row += size
        groups.append(Group(copies))
    return groups


def factor_loads(mine, other, v_left, sems, places):
    return [
        pltpu.make_async_copy((mine, other)[j // HALF].at[pl.ds(2 * (j % HALF), 2)], v_left.at[p], sems.at[j])
        for j, p in enumerate(places)
    ]


def token_kernel(
    xl_ref, grads, mask, factor_t, own, other, tok_own, tok_other, terms_t, v_grads, v_mask, v_factor, v_tok, v_masked, v_terms, sems
):
    loads = [
        pltpu.make_async_copy(grads, v_grads, sems.at[0]),
        pltpu.make_async_copy(mask, v_mask, sems.at[1]),
        pltpu.make_async_copy(factor_t, v_factor, sems.at[2]),
    ]
    start(loads)
    wait(loads)
    flags = jnp.broadcast_to(v_mask[...].astype(F32), (128, 256)).T[:, :1]
    masked = (v_grads[...].astype(F32) * flags).astype(BF)
    terms = stack3(v_factor[...])
    tok = sum3(dot(terms, masked, (1, 1))) * (1.0 / 16.0)
    first = xl_ref[0] == 0
    v_tok[0] = jnp.where(first, tok[:, 128:], tok[:, :128])
    v_tok[1] = jnp.where(first, tok[:, :128], tok[:, 128:])
    v_terms[...] = terms
    v_masked[0] = jnp.where(first, masked[:128], masked[128:])
    v_masked[1] = jnp.where(first, masked[128:], masked[:128])
    stores = [
        pltpu.make_async_copy(v_tok.at[0], tok_other, sems.at[3]),
        pltpu.make_async_copy(v_tok.at[1], tok_own, sems.at[4]),
        pltpu.make_async_copy(v_terms, terms_t, sems.at[5]),
        pltpu.make_async_copy(v_masked.at[0], own, sems.at[6]),
        pltpu.make_async_copy(v_masked.at[1], other, sems.at[7]),
    ]
    start(stores)
    wait(stores)


def token_part(xl, grads, mask, factor_t):
    return call(
        token_kernel,
        "token_part",
        (xl, grads, mask, factor_t),
        [((128, 512), BF), ((128, 512), BF), ((64, 128), F32), ((64, 128), F32), ((192, 512), BF)],
        [
            pltpu.VMEM((256, 512), BF),
            pltpu.VMEM((1, 256), jnp.int32),
            pltpu.VMEM((64, 512), F32),
            pltpu.VMEM((2, 64, 128), F32),
            pltpu.VMEM((2, 128, 512), BF),
            pltpu.VMEM((192, 512), BF),
            pltpu.SemaphoreType.DMA((8,)),
        ],
        8,
        hbm=True,
    )


def parcel_kernel(firsts, core_ref, after, hidden, key_weight, *refs):
    count = len(firsts)
    parcels, v_parcels, sems = refs[:count], refs[count : 2 * count], refs[2 * count]
    picks, drops = [], []
    for k, (kind, first) in enumerate(firsts):
        rows = parcels[k].shape[0]
        if kind == "hidden":
            source = hidden.at[pl.ds(first, rows), :]
        else:
            source = key_weight.at[pl.ds(pl.multiple_of(core_ref[0] * 4096 + first, 64), rows), :]
        picks.append(pltpu.make_async_copy(source, v_parcels[k], sems.at[0, k]))
        drops.append(pltpu.make_async_copy(v_parcels[k], parcels[k], sems.at[1, k]))
    start(picks)
    for pick, drop in zip(picks, drops):
        pick.wait()
        drop.start()
    wait(drops)


def parcel_part(core, after, hidden, key_weight, parcels):
    shapes = [((rows, 8192 if kind == "hidden" else 512), BF) for kind, _, rows in parcels]
    return call(
        functools.partial(parcel_kernel, [(kind, first) for kind, first, _ in parcels]),
        "parcel_part",
        (core, after, hidden, key_weight),
        shapes,
        [*[pltpu.VMEM(shape, dtype) for shape, dtype in shapes], pltpu.SemaphoreType.DMA((2, len(shapes)))],
        10,
        hbm=True,
    )


def left_kernel(
    core_ref, err, hidden, terms_t, tok_own, tok_far, keep, away, v_err, v_hid, v_terms, v_tok, v_out, sems, sem_err, sem_hid, sem_out
):
    small = [
        pltpu.make_async_copy(terms_t, v_terms, sems.at[0]),
        pltpu.make_async_copy(tok_own, v_tok.at[0], sems.at[1]),
        pltpu.make_async_copy(tok_far, v_tok.at[1], sems.at[2]),
    ]
    places = [(1 - core_ref[0]) * HALF + j if j < HALF else core_ref[0] * HALF + j - HALF for j in range(COUNT)]
    loads = list(zip(error_loads(err, v_err, sem_err, places), hidden_loads([hidden], v_hid, sem_hid, places)))
    start(small)
    for j in range(AHEAD):
        start(loads[j])
    wait(small)
    toks = stack3(v_tok[0] + v_tok[1])
    stores = []
    for j in range(COUNT):
        wait(loads[j])
        if j + AHEAD < COUNT:
            start(loads[j + AHEAD])
        value = sum3(dot(v_terms[...], v_err[places[j]], (1, 1)) + dot(toks, v_hid[places[j]], (1, 0)))
        v_out[j, 0] = value[:, :256]
        v_out[j, 1] = value[:, 256:]
        target = away if j < HALF else keep
        stores.append(pltpu.make_async_copy(v_out.at[j], target.at[pl.ds(2 * (j % HALF), 2)], sem_out.at[j]))
        stores[j].start()
    wait(stores)


def left_part(core, err, hidden, terms_t, tok_own, tok_far):
    return call(
        left_kernel,
        "left_part",
        (core, err, hidden, terms_t, tok_own, tok_far),
        [((16, 64, 256), F32), ((16, 64, 256), F32)],
        [
            pltpu.VMEM((COUNT, BLK, 512), BF),
            pltpu.VMEM((COUNT, 128, BLK), BF),
            pltpu.VMEM((192, 512), BF),
            pltpu.VMEM((2, 64, 128), F32),
            pltpu.VMEM((COUNT, 2, 64, 256), F32),
            pltpu.SemaphoreType.DMA((3,)),
            pltpu.SemaphoreType.DMA((COUNT,)),
            pltpu.SemaphoreType.DMA((COUNT, 1)),
            pltpu.SemaphoreType.DMA((COUNT,)),
        ],
        28,
    )


def right_kernel(count, core_ref, mine, other, err, masked_own, masked_other, *refs):
    hidden = refs[:count]
    keep, away, gram, v_left, v_err, v_hid = refs[count : count + 6]
    v_masked, v_keep, v_away, v_gram, sems, sem_left, sem_err, sem_hid = refs[count + 6 :]
    places = [core_ref[0] * HALF + j if j < HALF else (1 - core_ref[0]) * HALF + j - HALF for j in range(COUNT)]
    loads = list(
        zip(
            factor_loads(mine, other, v_left, sem_left, places),
            error_loads(err, v_err, sem_err, places),
            hidden_loads(hidden, v_hid, sem_hid, places),
        )
    )
    late = [
        pltpu.make_async_copy(masked_own, v_masked.at[pl.ds(0, 128), :], sems.at[0]),
        pltpu.make_async_copy(masked_other, v_masked.at[pl.ds(128, 128), :], sems.at[4]),
    ]
    for j in range(AHEAD):
        start(loads[j])
    start(late)
    w_sum, g_sum, z_sum = 0.0, 0.0, 0.0
    for j in range(COUNT):
        wait(loads[j])
        if j + AHEAD < COUNT:
            start(loads[j + AHEAD])
        terms = stack3(jnp.concatenate([v_left[places[j], 0], v_left[places[j], 1]], axis=1))
        w_sum = w_sum + dot(terms, v_err[places[j]], (1, 0))
        g_sum = g_sum + dot(terms, terms, (1, 1))
        z_sum = z_sum + dot(terms, v_hid[places[j]], (1, 1))
    wait(late)
    z = sum3(z_sum) * (1.0 / 16.0)
    right = sum3(w_sum + dot(stack3(z), v_masked[...], (1, 0)))
    first = core_ref[0] == 0
    v_keep[...] = jnp.where(first, right[:32], right[32:])
    v_away[...] = jnp.where(first, right[32:], right[:32])
    g = sum3(g_sum)
    v_gram[...] = g[:, :64] + g[:, 64:128] + g[:, 128:192]
    stores = [
        pltpu.make_async_copy(v_away, away, sems.at[1]),
        pltpu.make_async_copy(v_keep, keep, sems.at[2]),
        pltpu.make_async_copy(v_gram, gram, sems.at[3]),
    ]
    start(stores)
    wait(stores)


def right_part(core, mine, other, err, hidden, masked_own, masked_other):
    return call(
        functools.partial(right_kernel, len(hidden)),
        "right_part",
        (core, mine, other, err, masked_own, masked_other, *hidden),
        [((32, 512), F32), ((32, 512), F32), ((64, 64), F32)],
        [
            pltpu.VMEM((COUNT, 2, 64, 256), F32),
            pltpu.VMEM((COUNT, BLK, 512), BF),
            pltpu.VMEM((COUNT, 256, BLK), BF),
            pltpu.VMEM((256, 512), BF),
            pltpu.VMEM((32, 512), F32),
            pltpu.VMEM((32, 512), F32),
            pltpu.VMEM((64, 64), F32),
            pltpu.SemaphoreType.DMA((5,)),
            pltpu.SemaphoreType.DMA((COUNT,)),
            pltpu.SemaphoreType.DMA((COUNT,)),
            pltpu.SemaphoreType.DMA((COUNT, len(hidden))),
        ],
        28,
    )


def final_kernel(
    count, core_ref, masked_own, masked_other, total, total_other, inverse, grad_far, grad_base, mine, other, err, *refs
):
    hidden, refs = refs[:count], refs[count:]
    update, new_error, factor, grad = refs[:4]
    v_left, v_err, v_hid, v_masked, v_right, v_inv, v_factor, v_update, v_new, v_grad = refs[4:14]
    sems, sem_left, sem_err, sem_hid, sem_out = refs[14:]
    core = core_ref[0]
    places = [core * HALF + j if j < HALF else (1 - core) * HALF + j - HALF for j in range(COUNT)]
    loads = list(
        zip(
            factor_loads(mine, other, v_left, sem_left, places),
            error_loads(err, v_err, sem_err, places),
            hidden_loads(hidden, v_hid, sem_hid, places),
        )
    )
    small = [
        pltpu.make_async_copy(inverse, v_inv, sems.at[0]),
        pltpu.make_async_copy(total, v_right.at[pl.ds(pl.multiple_of(core * 32, 32), 32), :], sems.at[1]),
        pltpu.make_async_copy(total_other, v_right.at[pl.ds(pl.multiple_of((1 - core) * 32, 32), 32), :], sems.at[2]),
        pltpu.make_async_copy(masked_own, v_masked.at[pl.ds(0, 128), :], sems.at[3]),
        pltpu.make_async_copy(masked_other, v_masked.at[pl.ds(128, 128), :], sems.at[7]),
    ]
    grad_in = pltpu.make_async_copy(grad_far, v_grad, sems.at[4])
    start(small)
    for j in range(AHEAD):
        start(loads[j])
    wait(small)
    v_factor[...] = jnp.dot(v_inv[...], v_right[...], precision=HIGHEST, preferred_element_type=F32) * (1.0 / 64.0)
    coefficients = lax.dot_general(
        v_inv[...], v_factor[...], (((0,), (0,)), ((), ())), precision=HIGHEST, preferred_element_type=F32
    )
    y1, y2, y3 = kernel_split3(coefficients)
    ys = jnp.concatenate([y1, y1, y1, y2, y2, y3], axis=0)
    stores = [pltpu.make_async_copy(v_factor, factor, sems.at[5])]
    stores[0].start()
    for j in range(COUNT):
        place = places[j]
        wait(loads[j])
        if j + AHEAD < COUNT:
            start(loads[j + AHEAD])
        elif j + AHEAD == COUNT:
            grad_in.start()
        l1, l2, l3 = kernel_split3(jnp.concatenate([v_left[place, 0], v_left[place, 1]], axis=1))
        estimate = dot(jnp.concatenate([l1, l2, l3, l1, l2, l1], axis=0), ys, (0, 0))
        merged = dot(v_hid[place], v_masked[...], (0, 0)) * (1.0 / 16.0) + v_err[place].astype(F32)
        slot = j % SLOTS
        if j >= SLOTS:
            wait(stores[2 * (j - SLOTS) + 1 : 2 * (j - SLOTS) + 3])
        v_update[slot] = estimate.astype(BF)
        v_new[slot] = (merged - estimate).astype(BF)
        for k, (source, target) in enumerate(((v_update, update), (v_new, new_error))):
            copy = pltpu.make_async_copy(source.at[slot], target.at[rows_of(place), :], sem_out.at[k, slot])
            copy.start()
            stores.append(copy)
    grad_in.wait()
    columns = pl.ds(pl.multiple_of((1 - core) * 4096, 4096), 4096)
    stores.append(pltpu.make_async_copy(v_grad, grad.at[:, columns], sems.at[6]))
    stores[-1].start()
    wait(stores[:1] + stores[2 * (COUNT - SLOTS) + 1 :])


def final_part(core, masked_own, masked_other, total, total_other, inverse, grad_far, grad_base, mine, other, err, hidden):
    return call(
        functools.partial(final_kernel, len(hidden)),
        "final_part",
        (core, masked_own, masked_other, total, total_other, inverse, grad_far, grad_base, mine, other, err, *hidden),
        [((8192, 512), BF), ((8192, 512), BF), ((64, 512), F32), ((128, 8192), BF)],
        [
            pltpu.VMEM((COUNT, 2, 64, 256), F32),
            pltpu.VMEM((COUNT, BLK, 512), BF),
            pltpu.VMEM((COUNT, 256, BLK), BF),
            pltpu.VMEM((256, 512), BF),
            pltpu.VMEM((64, 512), F32),
            pltpu.VMEM((64, 64), F32),
            pltpu.VMEM((64, 512), F32),
            pltpu.VMEM((SLOTS, BLK, 512), BF),
            pltpu.VMEM((SLOTS, BLK, 512), BF),
            pltpu.VMEM((128, 4096), BF),
            pltpu.SemaphoreType.DMA((8,)),
            pltpu.SemaphoreType.DMA((COUNT,)),
            pltpu.SemaphoreType.DMA((COUNT,)),
            pltpu.SemaphoreType.DMA((COUNT, len(hidden))),
            pltpu.SemaphoreType.DMA((2, SLOTS)),
        ],
        44,
        aliases={7: 3},
    )


def input_kernel(count, core_ref, near_own, near_other, far_own, far_other, key_weight, *refs):
    pieces = refs[:count]
    grad, grad_other, v_near, v_far, v_wnear, v_wfar, v_own, v_other, sems, sem_near, sem_far, sem_out = refs[count:]
    core = core_ref[0]
    small = [
        pltpu.make_async_copy(near_own, v_near.at[pl.ds(0, 128), :], sems.at[0]),
        pltpu.make_async_copy(near_other, v_near.at[pl.ds(128, 128), :], sems.at[1]),
        pltpu.make_async_copy(far_own, v_far.at[pl.ds(0, 128), :], sems.at[2]),
        pltpu.make_async_copy(far_other, v_far.at[pl.ds(128, 128), :], sems.at[3]),
    ]
    loads, fars, ends, row = [], [], [], 0
    for j in range(4):
        place = pl.ds(pl.multiple_of(core * 4096 + j * 1024, 1024), 1024)
        loads.append(pltpu.make_async_copy(key_weight.at[place, :], v_wnear.at[j], sem_near.at[j]))
    for number, piece in enumerate(pieces):
        size = piece.shape[0]
        fars.append(pltpu.make_async_copy(piece, v_wfar.at[pl.ds(row, size), :], sem_far.at[number]))
        row += size
        ends.append(row)
    start(small)
    begun = 0
    for j in range(4):
        loads[j].start()
        while begun < count and (0 if begun == 0 else ends[begun - 1]) < (j + 1) * 1024:
            fars[begun].start()
            begun += 1
    wait(small)
    stores, waited = [], 0
    for j in range(4):
        loads[j].wait()
        while waited < count and (0 if waited == 0 else ends[waited - 1]) < (j + 1) * 1024:
            fars[waited].wait()
            waited += 1
        value = dot(v_near[...], v_wnear[j], (1, 1))
        value = (value + dot(v_far[...], v_wfar[pl.ds(j * 1024, 1024), :], (1, 1))).astype(BF)
        v_own[j] = value[:128]
        v_other[j] = value[128:]
        place = pl.ds(pl.multiple_of(core * 4096 + j * 1024, 1024), 1024)
        stores.append(pltpu.make_async_copy(v_own.at[j], grad.at[:, place], sem_out.at[0, j]))
        stores.append(pltpu.make_async_copy(v_other.at[j], grad_other.at[:, pl.ds(j * 1024, 1024)], sem_out.at[1, j]))
        start(stores[-2:])
    wait(stores)


def input_part(core, near_own, near_other, far_own, far_other, key_weight, pieces):
    return call(
        functools.partial(input_kernel, len(pieces)),
        "input_part",
        (core, near_own, near_other, far_own, far_other, key_weight, *pieces),
        [((128, 8192), BF), ((128, 4096), BF)],
        [
            pltpu.VMEM((256, 512), BF),
            pltpu.VMEM((256, 512), BF),
            pltpu.VMEM((4, 1024, 512), BF),
            pltpu.VMEM((4096, 512), BF),
            pltpu.VMEM((4, 128, 1024), BF),
            pltpu.VMEM((4, 128, 1024), BF),
            pltpu.SemaphoreType.DMA((4,)),
            pltpu.SemaphoreType.DMA((4,)),
            pltpu.SemaphoreType.DMA((len(pieces),)),
            pltpu.SemaphoreType.DMA((2, 4)),
        ],
        18,
    )


def local(hidden_rows, key_grads, loss_mask, key_weight, error_buf, right_factor):
    core = lax.axis_index("core")
    core_arg = core.astype(jnp.int32)[None]
    xl_arg = lax.axis_index("xl").astype(jnp.int32)[None]
    err = error_buf.reshape(8192, 512)
    barrier = lax.optimization_barrier

    def weight_rows(first, rows):
        return lax.dynamic_slice(key_weight, (core * 4096 + first, 0), (rows, 512))

    masked_own, masked_other, tok_own, tok_other, terms_t = token_part(
        xl_arg, key_grads, loss_mask.reshape(1, 256), right_factor.T
    )

    tok_far = send(tok_other, PARTNER)

    hidden_0, weight_0, hidden_1, weight_1, hidden_2, weight_2, weight_3, weight_4 = parcel_part(
        core_arg,
        masked_own,
        hidden_rows,
        key_weight,
        [
            ("hidden", 0, 48),
            ("weight", 0, 576),
            ("hidden", 48, 48),
            ("weight", 576, 768),
            ("hidden", 96, 32),
            ("weight", 1344, 512),
            ("weight", 1856, 1152),
            ("weight", 3008, 1088),
        ],
    )
    tok_far, hidden_0 = barrier((tok_far, hidden_0))
    far_hidden_0 = send(hidden_0, PARTNER)
    far_weight_0 = send(weight_0, WRAP)

    keep, away = left_part(core_arg, err, hidden_rows, terms_t, tok_own, tok_far)
    keep, away, far_hidden_0, far_weight_0, hidden_1, weight_1, masked_own, masked_other = barrier(
        (keep, away, far_hidden_0, far_weight_0, hidden_1, weight_1, masked_own, masked_other)
    )
    piece = keep + send(away, OTHER_CORE)
    masked_far = send(masked_other, PARTNER)
    far_hidden_1 = send(hidden_1, PARTNER)
    far_weight_1 = send(weight_1, WRAP)
    piece = lax.all_to_all(piece, ("z", "y"), 0, 0, tiled=True)
    piece = jnp.sum(piece, axis=0)
    piece, far_hidden_1, far_weight_1, masked_far = barrier((piece, far_hidden_1, far_weight_1, masked_far))
    piece = sum_of_four(piece, "x")

    piece, hidden_2, weight_2, masked_own, masked_far = barrier((piece, hidden_2, weight_2, masked_own, masked_far))
    far_hidden_2 = send(hidden_2, PARTNER)
    far_weight_2 = send(weight_2, WRAP)
    near_other = send(masked_own, OTHER_CORE)
    far_other = send(masked_far, OTHER_CORE)
    mine = lax.all_to_all(jnp.broadcast_to(piece[None], (16, 64, 256)), ("z", "y"), 0, 0, tiled=True)
    mine, far_hidden_2, far_weight_2, weight_3, weight_4, near_other, far_other = barrier(
        (mine, far_hidden_2, far_weight_2, weight_3, weight_4, near_other, far_other)
    )
    far_weight_3 = send(weight_3, WRAP)
    far_weight_4 = send(weight_4, PARTNER)
    other = send(mine, OTHER_CORE)

    hidden = [hidden_rows, far_hidden_0, far_hidden_1, far_hidden_2]
    keep, away, gram = right_part(core_arg, mine, other, err, hidden, masked_own, masked_other)
    total = keep + send(away, OTHER_CORE)
    total, gram = barrier((total, gram))
    factor_low = jnp.linalg.cholesky(gram)
    total = sum_of_four(total, "y")
    total, factor_low, far_weight_3, far_weight_4 = barrier((total, factor_low, far_weight_3, far_weight_4))
    pieces = [far_weight_0, far_weight_1, far_weight_2, far_weight_3, far_weight_4]
    grad, grad_other = input_part(core_arg, masked_own, near_other, masked_far, far_other, key_weight, pieces)
    total = sum_of_four(total, "z")
    total, factor_low, grad_other = barrier((total, factor_low, grad_other))
    inverse = jax.scipy.linalg.solve_triangular(factor_low, jnp.eye(64, dtype=F32), lower=True)
    grad_far = send(grad_other, OTHER_CORE)
    total = total + send(total, permutation(x=2))
    total_other = send(total, OTHER_CORE)

    update, new_error, factor, input_grad = final_part(
        core_arg, masked_own, masked_other, total, total_other, inverse, grad_far, grad, mine, other, err, hidden
    )
    return input_grad, update, new_error[None], factor.T


def solution(mesh):
    fine = Mesh(mesh.devices.reshape(SIZES), AXES)
    dp = ("z", "y", "xh", "core")
    placed = (
        P(AXES, None),
        P(dp, "xl"),
        P(dp),
        P(None, "xl"),
        P(dp, None, "xl"),
        P("xl", None),
    )
    return jax.shard_map(
        local,
        mesh=fine,
        in_specs=placed,
        out_specs=(P(AXES, None), P(None, "xl"), P(dp, None, "xl"), P("xl", None)),
        check_vma=False,
    )
```

time: 1540 us -> 161 us (0.10)
  waiting for transfers between devices: 1370 us -> 43.6 us
  matrix products: 73.1 us -> 0.82 us
  starting transfers between devices: 0.6 us -> 49.9 us
  Pallas kernels: 0 us -> 48.4 us
  local copies, waits for them, and re-layouts: 47.4 us -> 3.19 us
  other arithmetic: 32.9 us -> 13.4 us
    psum x3 -> x0, waiting for transfers between devices: 1270 us -> none  [the longest x1 643 us: local(): left_sum = lax.psum(left_sum, 'dp')]
    dot_general x6 -> x0, matrix products: 69.6 us -> none  [the longest x1 20.3 us: local(): lax.dot_general(merged, ortho_basis, (((0,), (0,)), ((), ())), precision=...]
    all_gather x1 -> x0, waiting for transfers between devices: 51.6 us -> none  [local(): lax.all_gather(hidden_rows, 'mp', axis=0, tiled=True)]
    pallas_call x0 -> x6, Pallas kernels: none -> 48.4 us  [call(): pl.pallas_call(kernel, out_shape=[(pltpu.HBM if hbm else jax.ShapeDtypeSt...]
    reduce_scatter x1 -> x0, waiting for transfers between devices: 40.6 us -> none  [local(): lax.psum_scatter(lax.dot_general(token_slab, key_weight, (((1,), (1,)), (...]
    ppermute x0 -> x27, starting transfers between devices: none -> 35.8 us  [send(): return lax.ppermute(array, AXES, pairs)]
    ppermute x0 -> x27, waiting for transfers between devices: none -> 27.7 us  [send(): return lax.ppermute(array, AXES, pairs)]
    unnamed x12 -> x36, local copies, waits for them, and re-layouts: 29.7 us -> 2.05 us
  transfers between devices with their start and end apart: 5 -> 29, of which waited for: 5 -> 15; matrix products, arithmetic and copies ran while one was open for 5% -> 8% of each run, Pallas kernels for 0% -> 19%
where the time goes in v2:
time: 161 us; the launch traced here: 160 us
  starting transfers between devices  49.9 us (31%)
  Pallas kernels  48.4 us (30%)
  waiting for transfers between devices  43.6 us (27%)
  other arithmetic  13.4 us (8%)
  local copies, waits for them, and re-layouts  3.19 us (2%)
    pallas_call x6, Pallas kernels, call(): pl.pallas_call(kernel, out_shape=[(pltpu.HBM if hbm else jax.ShapeDtypeSt...  48.4 us
    ppermute x27, starting transfers between devices, send(): return lax.ppermute(array, AXES, pairs)  35.8 us
    ppermute x27, waiting for transfers between devices, send(): return lax.ppermute(array, AXES, pairs)  27.7 us
    all_to_all x1, waiting for transfers between devices, local(): piece = lax.all_to_all(piece, ('z', 'y'), 0, 0, tiled=True)  13.5 us
    all_to_all x1, starting transfers between devices, local(): piece = lax.all_to_all(piece, ('z', 'y'), 0, 0, tiled=True)  7.77 us
    another operation x3, other arithmetic, local(): factor_low = jnp.linalg.cholesky(gram)  6.52 us
    all_to_all x1, starting transfers between devices, local(): lax.all_to_all(jnp.broadcast_to(piece[None], (16, 64, 256)), ('z', 'y'),...  6.33 us
    another operation x2, other arithmetic, local(): jax.scipy.linalg.solve_triangular(factor_low, jnp.eye(64, dtype=F32), low...  4.9 us
  transfers between devices with their start and end apart: 29, of which 15 were waited for; matrix products, arithmetic and copies ran while one was open for 8% of the time, Pallas kernels for 19%

profile of v2, /device:TPU:1, one launch (start us, length us, event | category | flops | bytes accessed | tf_op | source)
XLA Modules:
  0.0 160.4 jit_solution(14405838153675821758)
XLA Ops:
  0.6 2.3 %token_part.1 = (bf16[128,512]{1,0:T(8,128)(2,1)}, bf16[128,512]{1,0:T(8,128)(2,1)}, f32[64,128]{1,0:T(8,128)}, f32[64,128]{1,0:T(8,128)}, bf16[192,512]{1,0:T(8,128)(2,1)}) custom-call(s32[1]{0:T(128)} %bitcast.2.xl_ref, bf16[256,512]{1,0:T(8,128)(2,1)} %grads.1, s32[1,256]{1,0:T(1,128)} %bitcast.20, f32[64,512]{1,0:T(8,128)} %bitcast.19), custom_call_target="tpu_custom_call" | custom-call | flops 1024 | bytes 1024 | tf_op jit(solution)/shard_map/token_part/pallas_call | solution.py:84
  3.0 2.1 %collective-permute-start = (f32[64,128]{1,0:T(8,128)}, f32[64,128]{1,0:T(8,128)S(1)}, u32[]{:S(2)}, u32[]{:S(2)}) collective-permute-start(f32[64,128]{1,0:T(8,128)} %get-tuple-element.65), channel_id=1, source_target_pairs={{0,1},{1,0},{2,3},{3,2},{4,5},{5,4},{6,7},{7,6},{8,9},{9,8},{10,11... | collective-permute-start | bytes 98312 | tf_op jit(solution)/shard_map/ppermute | solution.py:41
  5.1 5.4 %parcel_part.1 = (bf16[48,8192]{1,0:T(8,128)(2,1)}, bf16[576,512]{1,0:T(8,128)(2,1)}, bf16[48,8192]{1,0:T(8,128)(2,1)}, bf16[768,512]{1,0:T(8,128)(2,1)}, bf16[3...) custom-call(s32[1]{0:T(128)} %bitcast.core_ref, ...), custom_call_target="tpu_custom_call" | custom-call | flops 1024 | bytes 1024 | tf_op jit(solution)/shard_map/parcel_part/pallas_call | solution.py:84
  10.6 2.7 %collective-permute-start.2 = (bf16[576,512]{1,0:T(8,128)(2,1)}, bf16[576,512]{1,0:T(8,128)(2,1)S(1)}, u32[]{:S(2)}, u32[]{:S(2)}) collective-permute-start(bf16[576,512]{1,0:T(8,128)(2,1)} %get-tuple-element.72), channel_id=1, source_target_pairs={{0,5},{1,4},{2,7},{3,6},{4,1},{5,0},{6,3},{7,2},{8,13},{9,12},{10,... | collective-permute-start | bytes 1769480 | tf_op jit(solution)/shard_map/ppermute | solution.py:41
  13.3 10.2 %left_part.1 = (f32[16,64,256]{2,1,0:T(8,128)S(1)}, f32[16,64,256]{2,1,0:T(8,128)S(1)}) custom-call(s32[1]{0:T(128)} %bitcast.core_ref, bf16[8192,512]{1,0:T(8,128)(2,1)} %bitcast.16, bf16[128,8192]{1,0:T(8,128)(2,1)} %refs_0_.3, bf16[192,512]{1,0:T(8,128)(2,1)} %get-tuple-element.63.terms_t, f32[64,128]{1,0:T(8,128)} %get-tuple-element.64.tok_own, ...), custom_call_target="tpu_custom_call" | custom-call | flops 1024 | bytes 1024 | tf_op jit(solution)/shard_map/left_part/pallas_call | solution.py:84
  23.5 2.1 %collective-permute-done.2.refs_0_ = bf16[576,512]{1,0:T(8,128)(2,1)S(1)} collective-permute-done((bf16[576,512]{1,0:T(8,128)(2,1)}, bf16[576,512]{1,0:T(8,128)(2,1)S(1)}, u32[]{:S(2)}, u32[]{:S(2)}) %collective-permute-start.2) | collective-permute-done | bytes 589856 | tf_op jit(solution)/shard_map/ppermute | solution.py:41
  25.6 3.3 %collective-permute-done.1.refs_1_ = bf16[48,8192]{1,0:T(8,128)(2,1)S(1)} collective-permute-done((bf16[48,8192]{1,0:T(8,128)(2,1)}, bf16[48,8192]{1,0:T(8,128)(2,1)S(1)}, u32[]{:S(2)}, u32[]{:S(2)}) %collective-permute-start.1) | collective-permute-done | bytes 786464 | tf_op jit(solution)/shard_map/ppermute | solution.py:41
  28.9 1.9 %collective-permute-start.3 = (f32[16,64,256]{2,1,0:T(8,128)S(1)}, f32[16,64,256]{2,1,0:T(8,128)S(1)}, u32[]{:S(2)}, u32[]{:S(2)}) collective-permute-start(f32[16,64,256]{2,1,0:T(8,128)S(1)} %get-tuple-element.77), channel_id=1, source_target_pairs={{0,2},{1,3},{2,0},{3,1},{4,6},{5,7},{6,4},{7,5},{8,10},{9,11},{10,... | collective-permute-start | bytes 3145736 | tf_op jit(solution)/shard_map/ppermute | solution.py:41
  30.7 2.3 %collective-permute-done.3 = f32[16,64,256]{2,1,0:T(8,128)S(1)} collective-permute-done((f32[16,64,256]{2,1,0:T(8,128)S(1)}, f32[16,64,256]{2,1,0:T(8,128)S(1)}, u32[]{:S(2)}, u32[]{:S(2)}) %collective-permute-start.3) | collective-permute-done | bytes 1048608 | tf_op jit(solution)/shard_map/ppermute | solution.py:41
  33.0 1.1 add.48
  34.2 7.8 %all-to-all-start = ((f32[16,64,256]{2,1,0:T(8,128)}), f32[16,64,256]{2,1,0:T(8,128)S(1)}, u32[]{:S(2)}, u32[]{:S(2)}) async-start(f32[16,64,256]{2,1,0:T(8,128)} %add.48), calls=%async_computation | async-start | bytes 2097152 | tf_op jit(solution)/shard_map/all_to_all | solution.py:538
  42.3 2.5 %collective-permute-start.5 = (bf16[768,512]{1,0:T(8,128)(2,1)}, bf16[768,512]{1,0:T(8,128)(2,1)S(1)}, u32[]{:S(2)}, u32[]{:S(2)}) collective-permute-start(bf16[768,512]{1,0:T(8,128)(2,1)} %get-tuple-element.79), channel_id=1, source_target_pairs={{0,5},{1,4},{2,7},{3,6},{4,1},{5,0},{6,3},{7,2},{8,13},{9,12},{10,... | collective-permute-start | bytes 2359304 | tf_op jit(solution)/shard_map/ppermute | solution.py:41
  44.8 13.5 %all-to-all-done = f32[16,64,256]{2,1,0:T(8,128)S(1)} async-done(((f32[16,64,256]{2,1,0:T(8,128)}), f32[16,64,256]{2,1,0:T(8,128)S(1)}, u32[]{:S(2)}, u32[]{:S(2)}) %all-to-all-start) | async-done | bytes 1048608 | tf_op jit(solution)/shard_map/all_to_all | solution.py:538
  58.3 5.1 %collective-permute-done.6.far_own = bf16[128,512]{1,0:T(8,128)(2,1)S(1)} collective-permute-done((bf16[128,512]{1,0:T(8,128)(2,1)S(1)}, bf16[128,512]{1,0:T(8,128)(2,1)S(1)}, u32[]{:S(2)}, u32[]{:S(2)}) %collective-permute-start.6) | collective-permute-done | bytes 131104 | tf_op jit(solution)/shard_map/ppermute | solution.py:41
  63.5 1.9 %collective-permute-start.9 = (f32[64,256]{1,0:T(8,128)S(1)}, f32[64,256]{1,0:T(8,128)S(1)}, u32[]{:S(2)}, u32[]{:S(2)}) collective-permute-start(f32[64,256]{1,0:T(8,128)S(1)} %reduce_sum.9), channel_id=1, source_target_pairs={{0,5},{1,0},{2,7},{3,2},{4,1},{5,4},{6,3},{7,6},{8,13},{9,8},{10,1... | collective-permute-start | bytes 196616 | tf_op jit(solution)/shard_map/ppermute | solution.py:41
  65.4 2.1 %collective-permute-start.7 = (f32[64,256]{1,0:T(8,128)S(1)}, f32[64,256]{1,0:T(8,128)S(1)}, u32[]{:S(2)}, u32[]{:S(2)}) collective-permute-start(f32[64,256]{1,0:T(8,128)S(1)} %reduce_sum.9), channel_id=1, source_target_pairs={{0,4},{1,5},{2,6},{3,7},{4,0},{5,1},{6,2},{7,3},{8,12},{9,13},{10,... | collective-permute-start | bytes 196616 | tf_op jit(solution)/shard_map/ppermute | solution.py:41
  67.5 2.9 %collective-permute-done.8 = f32[64,256]{1,0:T(8,128)S(1)} collective-permute-done((f32[64,256]{1,0:T(8,128)S(1)}, f32[64,256]{1,0:T(8,128)S(1)}, u32[]{:S(2)}, u32[]{:S(2)}) %collective-permute-start.8) | collective-permute-done | bytes 65568 | tf_op jit(solution)/shard_map/ppermute | solution.py:41
  71.5 6.3 %all-to-all-start.1 = ((f32[16,64,256]{2,1,0:T(8,128)}), f32[16,64,256]{2,1,0:T(8,128)S(1)}, u32[]{:S(2)}, u32[]{:S(2)}) async-start(f32[16,64,256]{2,1,0:T(8,128)} %broadcast_in_dim.19), calls=%async_computation.1 | async-start | bytes 2097152 | tf_op jit(solution)/shard_map/all_to_all | solution.py:548
  78.2 2.1 %collective-permute-start.11 = (bf16[512,512]{1,0:T(8,128)(2,1)S(1)}, bf16[512,512]{1,0:T(8,128)(2,1)S(1)}, u32[]{:S(2)}, u32[]{:S(2)}) collective-permute-start(bf16[512,512]{1,0:T(8,128)(2,1)S(1)} %copy-done.17), channel_id=1, source_target_pairs={{0,5},{1,4},{2,7},{3,6},{4,1},{5,0},{6,3},{7,2},{8,13},{9,12},{10,... | collective-permute-start | bytes 1572872 | tf_op jit(solution)/shard_map/ppermute | solution.py:41
  80.4 4.1 %collective-permute-start.13 = (bf16[128,512]{1,0:T(8,128)(2,1)S(1)}, bf16[128,512]{1,0:T(8,128)(2,1)S(1)}, u32[]{:S(2)}, u32[]{:S(2)}) collective-permute-start(bf16[128,512]{1,0:T(8,128)(2,1)S(1)} %collective-permute-done.6.far_own), channel_id=1, source_target_pairs={{0,2},{1,3},{2,0},{3,1},{4,6},{5,7},{6,4},{7,5},{8,10},{9,11},{10,... | collective-permute-start | bytes 393224 | tf_op jit(solution)/shard_map/ppermute | solution.py:41
  85.8 2.2 %collective-permute-done.10.refs_3_ = bf16[32,8192]{1,0:T(8,128)(2,1)S(1)} collective-permute-done((bf16[32,8192]{1,0:T(8,128)(2,1)}, bf16[32,8192]{1,0:T(8,128)(2,1)S(1)}, u32[]{:S(2)}, u32[]{:S(2)}) %collective-permute-start.10) | collective-permute-done | bytes 524320 | tf_op jit(solution)/shard_map/ppermute | solution.py:41
  88.0 1.3 collective-permute-done.11.refs_2_
  89.3 2.3 %all-to-all-done.1.mine = f32[16,64,256]{2,1,0:T(8,128)S(1)} async-done(((f32[16,64,256]{2,1,0:T(8,128)}), f32[16,64,256]{2,1,0:T(8,128)S(1)}, u32[]{:S(2)}, u32[]{:S(2)}) %all-to-all-start.1) | async-done | bytes 1048608 | tf_op jit(solution)/shard_map/all_to_all | solution.py:548
  91.7 4.8 %collective-permute-start.14 = (f32[16,64,256]{2,1,0:T(8,128)S(1)}, f32[16,64,256]{2,1,0:T(8,128)S(1)}, u32[]{:S(2)}, u32[]{:S(2)}) collective-permute-start(f32[16,64,256]{2,1,0:T(8,128)S(1)} %all-to-all-done.1.mine), channel_id=1, source_target_pairs={{0,2},{1,3},{2,0},{3,1},{4,6},{5,7},{6,4},{7,5},{8,10},{9,11},{10,... | collective-permute-start | bytes 3145736 | tf_op jit(solution)/shard_map/ppermute | solution.py:41
  96.4 2.3 %collective-permute-start.19 = (bf16[1152,512]{1,0:T(8,128)(2,1)}, bf16[1152,512]{1,0:T(8,128)(2,1)}, u32[]{:S(2)}, u32[]{:S(2)}) collective-permute-start(bf16[1152,512]{1,0:T(8,128)(2,1)} %get-tuple-element.102), channel_id=1, source_target_pairs={{0,5},{1,4},{2,7},{3,6},{4,1},{5,0},{6,3},{7,2},{8,13},{9,12},{10,... | collective-permute-start | bytes 3538952 | tf_op jit(solution)/shard_map/ppermute | solution.py:41
  99.7 8.4 %right_part.1 = (f32[32,512]{1,0:T(8,128)S(1)}, f32[32,512]{1,0:T(8,128)S(1)}, f32[64,64]{1,0:T(8,128)S(1)}) custom-call(s32[1]{0:T(128)} %bitcast.core_ref, f32[16,64,256]{2,1,0:T(8,128)} %copy-done, f32[16,64,256]{2,1,0:T(8,128)} %copy-done.1, bf16[8192,512]{1,0:T(8,128)(2,1)} %bitcast.17, bf16[128,512]{1,0:T(8,128)(2,1)} %get-tuple-element.86.after.masked_own.near_own, ...), custom_call_target="tpu_custom_call" | custom-call | flops 1024 | bytes 1024 | tf_op jit(solution)/shard_map/right_part/pallas_call | solution.py:84
  112.2 5.8 %cholesky.20 = f32[64,64]{1,0:T(8,128)S(1)} custom-call(f32[64,64]{1,0:T(8,128)S(1)} %fusion.2), custom_call_target="Cholesky" | custom-call | tf_op jit(solution)/shard_map/jit(cholesky)/cholesky | solution.py:560
  119.4 5.4 %collective-permute-done.20.refs_4_ = bf16[1088,512]{1,0:T(8,128)(2,1)} collective-permute-done((bf16[1088,512]{1,0:T(8,128)(2,1)}, bf16[1088,512]{1,0:T(8,128)(2,1)}, u32[]{:S(2)}, u32[]{:S(2)}) %collective-permute-start.20) | collective-permute-done | bytes 1114144 | tf_op jit(solution)/shard_map/ppermute | solution.py:41
  128.0 6.7 %input_part.1 = (bf16[128,8192]{1,0:T(8,128)(2,1)}, bf16[128,4096]{1,0:T(8,128)(2,1)S(1)}) custom-call(s32[1]{0:T(128)} %bitcast.core_ref, bf16[128,512]{1,0:T(8,128)(2,1)} %get-tuple-element.86.after.masked_own.near_own, bf16[128,512]{1,0:T(8,128)(2,1)} %copy-done.14, bf16[128,512]{1,0:T(8,128)(2,1)} %copy-done.12, bf16[128,512]{1,0:T(8,128)(2,1)} %copy-done.13, ...), custom_call_target="tpu_custom_call" | custom-call | flops 1024 | bytes 1024 | tf_op jit(solution)/shard_map/input_part/pallas_call | solution.py:84
  134.8 1.7 %collective-permute-start.26 = (bf16[128,4096]{1,0:T(8,128)(2,1)S(1)}, bf16[128,4096]{1,0:T(8,128)(2,1)S(1)}, u32[]{:S(2)}, u32[]{:S(2)}) collective-permute-start(bf16[128,4096]{1,0:T(8,128)(2,1)S(1)} %get-tuple-element.116), channel_id=1, source_target_pairs={{0,2},{1,3},{2,0},{3,1},{4,6},{5,7},{6,4},{7,5},{8,10},{9,11},{10,... | collective-permute-start | bytes 3145736 | tf_op jit(solution)/shard_map/ppermute | solution.py:41
  137.3 4.9 %custom-call.7 = f32[1,64,64]{1,2,0:T(8,128)S(1)} custom-call(f32[1,64,64]{2,1,0:T(8,128)S(1)} %select_bitcast_fusion), custom_call_target="InvertDiagBlocksLowerTriangular" | custom-call | tf_op jit(solution)/shard_map/jit(_solve_triangular)/triangular_solve | solution.py:567
  144.8 15.4 %final_part.1 = (bf16[8192,512]{1,0:T(8,128)(2,1)}, bf16[8192,512]{1,0:T(8,128)(2,1)}, f32[64,512]{1,0:T(8,128)}, bf16[128,8192]{1,0:T(8,128)(2,1)}) custom-call(s32[1]{0:T(128)} %bitcast.core_ref, bf16[128,512]{1,0:T(8,128)(2,1)} %get-tuple-element.86.after.masked_own.near_own, ...), custom_call_target="tpu_custom_call", output_to_operand_aliasing={{3}: (7, {})} | custom-call | flops 1024 | bytes 1024 | tf_op jit(solution)/shard_map/final_part/pallas_call | solution.py:84
  (85 shorter events, 16.2 us)
Async XLA Ops:
  3.0 7.5 %collective-permute-start = (f32[64,128]{1,0:T(8,128)}, f32[64,128]{1,0:T(8,128)S(1)}, u32[]{:S(2)}, u32[]{:S(2)}) collective-permute-start(f32[64,128]{1,0:T(8,128)} %get-tuple-element.65), channel_id=1, source_target_pairs={{0,1},{1,0},{2,3},{3,2},{4,5},{5,4},{6,7},{7,6},{8,9},{9,8},{10,11... | collective-permute-start | bytes 98312 | tf_op jit(solution)/shard_map/ppermute | solution.py:41
  10.5 18.4 %collective-permute-start.1 = (bf16[48,8192]{1,0:T(8,128)(2,1)}, bf16[48,8192]{1,0:T(8,128)(2,1)S(1)}, u32[]{:S(2)}, u32[]{:S(2)}) collective-permute-start(bf16[48,8192]{1,0:T(8,128)(2,1)} %get-tuple-element.71), channel_id=1, source_target_pairs={{0,1},{1,0},{2,3},{3,2},{4,5},{5,4},{6,7},{7,6},{8,9},{9,8},{10,11... | collective-permute-start | bytes 2359304 | tf_op jit(solution)/shard_map/ppermute | solution.py:41
  10.6 15.0 %collective-permute-start.2 = (bf16[576,512]{1,0:T(8,128)(2,1)}, bf16[576,512]{1,0:T(8,128)(2,1)S(1)}, u32[]{:S(2)}, u32[]{:S(2)}) collective-permute-start(bf16[576,512]{1,0:T(8,128)(2,1)} %get-tuple-element.72), channel_id=1, source_target_pairs={{0,5},{1,4},{2,7},{3,6},{4,1},{5,0},{6,3},{7,2},{8,13},{9,12},{10,... | collective-permute-start | bytes 1769480 | tf_op jit(solution)/shard_map/ppermute | solution.py:41
  28.9 4.2 %collective-permute-start.3 = (f32[16,64,256]{2,1,0:T(8,128)S(1)}, f32[16,64,256]{2,1,0:T(8,128)S(1)}, u32[]{:S(2)}, u32[]{:S(2)}) collective-permute-start(f32[16,64,256]{2,1,0:T(8,128)S(1)} %get-tuple-element.77), channel_id=1, source_target_pairs={{0,2},{1,3},{2,0},{3,1},{4,6},{5,7},{6,4},{7,5},{8,10},{9,11},{10,... | collective-permute-start | bytes 3145736 | tf_op jit(solution)/shard_map/ppermute | solution.py:41
  34.2 24.1 %all-to-all-start = ((f32[16,64,256]{2,1,0:T(8,128)}), f32[16,64,256]{2,1,0:T(8,128)S(1)}, u32[]{:S(2)}, u32[]{:S(2)}) async-start(f32[16,64,256]{2,1,0:T(8,128)} %add.48), calls=%async_computation | async-start | bytes 2097152 | tf_op jit(solution)/shard_map/all_to_all | solution.py:538
  41.9 42.5 %copy-start.4 = (bf16[128,512]{1,0:T(8,128)(2,1)S(1)}, bf16[128,512]{1,0:T(8,128)(2,1)}, u32[]{:S(2)}) copy-start(bf16[128,512]{1,0:T(8,128)(2,1)} %get-tuple-element.86.after.masked_own.near_own) | copy-start | bytes 393220
  41.9 21.5 %collective-permute-start.4 = (bf16[48,8192]{1,0:T(8,128)(2,1)}, bf16[48,8192]{1,0:T(8,128)(2,1)S(1)}, u32[]{:S(2)}, u32[]{:S(2)}) collective-permute-start(bf16[48,8192]{1,0:T(8,128)(2,1)} %get-tuple-element.78), channel_id=1, source_target_pairs={{0,1},{1,0},{2,3},{3,2},{4,5},{5,4},{6,7},{7,6},{8,9},{9,8},{10,11... | collective-permute-start | bytes 2359304 | tf_op jit(solution)/shard_map/ppermute | solution.py:41
  42.3 21.2 %collective-permute-start.5 = (bf16[768,512]{1,0:T(8,128)(2,1)}, bf16[768,512]{1,0:T(8,128)(2,1)S(1)}, u32[]{:S(2)}, u32[]{:S(2)}) collective-permute-start(bf16[768,512]{1,0:T(8,128)(2,1)} %get-tuple-element.79), channel_id=1, source_target_pairs={{0,5},{1,4},{2,7},{3,6},{4,1},{5,0},{6,3},{7,2},{8,13},{9,12},{10,... | collective-permute-start | bytes 2359304 | tf_op jit(solution)/shard_map/ppermute | solution.py:41
  44.8 18.7 %collective-permute-start.6 = (bf16[128,512]{1,0:T(8,128)(2,1)S(1)}, bf16[128,512]{1,0:T(8,128)(2,1)S(1)}, u32[]{:S(2)}, u32[]{:S(2)}) collective-permute-start(bf16[128,512]{1,0:T(8,128)(2,1)S(1)} %copy-done.9), channel_id=1, source_target_pairs={{0,1},{1,0},{2,3},{3,2},{4,5},{5,4},{6,7},{7,6},{8,9},{9,8},{10,11... | collective-permute-start | bytes 393224 | tf_op jit(solution)/shard_map/ppermute | solution.py:41
  63.5 44.7 %copy-start.12 = (bf16[128,512]{1,0:T(8,128)(2,1)}, bf16[128,512]{1,0:T(8,128)(2,1)S(1)}, u32[]{:S(2)}) copy-start(bf16[128,512]{1,0:T(8,128)(2,1)S(1)} %collective-permute-done.6.far_own) | copy-start | bytes 393220
  63.5 4.0 %collective-permute-start.9 = (f32[64,256]{1,0:T(8,128)S(1)}, f32[64,256]{1,0:T(8,128)S(1)}, u32[]{:S(2)}, u32[]{:S(2)}) collective-permute-start(f32[64,256]{1,0:T(8,128)S(1)} %reduce_sum.9), channel_id=1, source_target_pairs={{0,5},{1,0},{2,7},{3,2},{4,1},{5,4},{6,3},{7,6},{8,13},{9,8},{10,1... | collective-permute-start | bytes 196616 | tf_op jit(solution)/shard_map/ppermute | solution.py:41
  65.4 5.0 %collective-permute-start.8 = (f32[64,256]{1,0:T(8,128)S(1)}, f32[64,256]{1,0:T(8,128)S(1)}, u32[]{:S(2)}, u32[]{:S(2)}) collective-permute-start(f32[64,256]{1,0:T(8,128)S(1)} %reduce_sum.9), channel_id=1, source_target_pairs={{0,1},{1,4},{2,3},{3,6},{4,5},{5,0},{6,7},{7,2},{8,9},{9,12},{10,1... | collective-permute-start | bytes 196616 | tf_op jit(solution)/shard_map/ppermute | solution.py:41
  65.4 5.0 %collective-permute-start.7 = (f32[64,256]{1,0:T(8,128)S(1)}, f32[64,256]{1,0:T(8,128)S(1)}, u32[]{:S(2)}, u32[]{:S(2)}) collective-permute-start(f32[64,256]{1,0:T(8,128)S(1)} %reduce_sum.9), channel_id=1, source_target_pairs={{0,4},{1,5},{2,6},{3,7},{4,0},{5,1},{6,2},{7,3},{8,12},{9,13},{10,... | collective-permute-start | bytes 196616 | tf_op jit(solution)/shard_map/ppermute | solution.py:41
  71.5 20.1 %all-to-all-start.1 = ((f32[16,64,256]{2,1,0:T(8,128)}), f32[16,64,256]{2,1,0:T(8,128)S(1)}, u32[]{:S(2)}, u32[]{:S(2)}) async-start(f32[16,64,256]{2,1,0:T(8,128)} %broadcast_in_dim.19), calls=%async_computation.1 | async-start | bytes 2097152 | tf_op jit(solution)/shard_map/all_to_all | solution.py:548
  77.9 10.1 %collective-permute-start.10 = (bf16[32,8192]{1,0:T(8,128)(2,1)}, bf16[32,8192]{1,0:T(8,128)(2,1)S(1)}, u32[]{:S(2)}, u32[]{:S(2)}) collective-permute-start(bf16[32,8192]{1,0:T(8,128)(2,1)} %get-tuple-element.88), channel_id=1, source_target_pairs={{0,1},{1,0},{2,3},{3,2},{4,5},{5,4},{6,7},{7,6},{8,9},{9,8},{10,11... | collective-permute-start | bytes 1572872 | tf_op jit(solution)/shard_map/ppermute | solution.py:41
  78.2 11.1 %collective-permute-start.11 = (bf16[512,512]{1,0:T(8,128)(2,1)S(1)}, bf16[512,512]{1,0:T(8,128)(2,1)S(1)}, u32[]{:S(2)}, u32[]{:S(2)}) collective-permute-start(bf16[512,512]{1,0:T(8,128)(2,1)S(1)} %copy-done.17), channel_id=1, source_target_pairs={{0,5},{1,4},{2,7},{3,6},{4,1},{5,0},{6,3},{7,2},{8,13},{9,12},{10,... | collective-permute-start | bytes 1572872 | tf_op jit(solution)/shard_map/ppermute | solution.py:41
  80.4 5.0 %collective-permute-start.13 = (bf16[128,512]{1,0:T(8,128)(2,1)S(1)}, bf16[128,512]{1,0:T(8,128)(2,1)S(1)}, u32[]{:S(2)}, u32[]{:S(2)}) collective-permute-start(bf16[128,512]{1,0:T(8,128)(2,1)S(1)} %collective-permute-done.6.far_own), channel_id=1, source_target_pairs={{0,2},{1,3},{2,0},{3,1},{4,6},{5,7},{6,4},{7,5},{8,10},{9,11},{10,... | collective-permute-start | bytes 393224 | tf_op jit(solution)/shard_map/ppermute | solution.py:41
  84.4 1.3 collective-permute-start.12
  85.4 22.8 %copy-start.13 = (bf16[128,512]{1,0:T(8,128)(2,1)}, bf16[128,512]{1,0:T(8,128)(2,1)S(1)}, u32[]{:S(2)}) copy-start(bf16[128,512]{1,0:T(8,128)(2,1)S(1)} %collective-permute-done.13.far_other) | copy-start | bytes 393220
  91.7 7.1 %collective-permute-start.14 = (f32[16,64,256]{2,1,0:T(8,128)S(1)}, f32[16,64,256]{2,1,0:T(8,128)S(1)}, u32[]{:S(2)}, u32[]{:S(2)}) collective-permute-start(f32[16,64,256]{2,1,0:T(8,128)S(1)} %all-to-all-done.1.mine), channel_id=1, source_target_pairs={{0,2},{1,3},{2,0},{3,1},{4,6},{5,7},{6,4},{7,5},{8,10},{9,11},{10,... | collective-permute-start | bytes 3145736 | tf_op jit(solution)/shard_map/ppermute | solution.py:41
  96.4 29.1 %collective-permute-start.19 = (bf16[1152,512]{1,0:T(8,128)(2,1)}, bf16[1152,512]{1,0:T(8,128)(2,1)}, u32[]{:S(2)}, u32[]{:S(2)}) collective-permute-start(bf16[1152,512]{1,0:T(8,128)(2,1)} %get-tuple-element.102), channel_id=1, source_target_pairs={{0,5},{1,4},{2,7},{3,6},{4,1},{5,0},{6,3},{7,2},{8,13},{9,12},{10,... | collective-permute-start | bytes 3538952 | tf_op jit(solution)/shard_map/ppermute | solution.py:41
  98.7 26.1 %collective-permute-start.20 = (bf16[1088,512]{1,0:T(8,128)(2,1)}, bf16[1088,512]{1,0:T(8,128)(2,1)}, u32[]{:S(2)}, u32[]{:S(2)}) collective-permute-start(bf16[1088,512]{1,0:T(8,128)(2,1)} %get-tuple-element.103), channel_id=1, source_target_pairs={{0,1},{1,0},{2,3},{3,2},{4,5},{5,4},{6,7},{7,6},{8,9},{9,8},{10,11... | collective-permute-start | bytes 3342344 | tf_op jit(solution)/shard_map/ppermute | solution.py:41
  108.2 1.4 collective-permute-start.15
  109.6 9.8 %collective-permute-start.18 = (f32[32,512]{1,0:T(8,128)S(1)}, f32[32,512]{1,0:T(8,128)S(1)}, u32[]{:S(2)}, u32[]{:S(2)}) collective-permute-start(f32[32,512]{1,0:T(8,128)S(1)} %add.52), channel_id=1, source_target_pairs={{0,24},{1,25},{2,26},{3,27},{4,28},{5,29},{6,30},{7,31},{8,0},{9,1... | collective-permute-start | bytes 196616 | tf_op jit(solution)/shard_map/ppermute | solution.py:41
  110.3 9.1 %collective-permute-start.17 = (f32[32,512]{1,0:T(8,128)S(1)}, f32[32,512]{1,0:T(8,128)S(1)}, u32[]{:S(2)}, u32[]{:S(2)}) collective-permute-start(f32[32,512]{1,0:T(8,128)S(1)} %add.52), channel_id=1, source_target_pairs={{0,8},{1,9},{2,10},{3,11},{4,12},{5,13},{6,14},{7,15},{8,16},{9,17... | collective-permute-start | bytes 196616 | tf_op jit(solution)/shard_map/ppermute | solution.py:41
  111.1 8.3 %collective-permute-start.16 = (f32[32,512]{1,0:T(8,128)S(1)}, f32[32,512]{1,0:T(8,128)S(1)}, u32[]{:S(2)}, u32[]{:S(2)}) collective-permute-start(f32[32,512]{1,0:T(8,128)S(1)} %add.52), channel_id=1, source_target_pairs={{0,16},{1,17},{2,18},{3,19},{4,20},{5,21},{6,22},{7,23},{8,24},{9,... | collective-permute-start | bytes 196616 | tf_op jit(solution)/shard_map/ppermute | solution.py:41
  125.5 9.2 %collective-permute-start.23 = (f32[32,512]{1,0:T(8,128)S(1)}, f32[32,512]{1,0:T(8,128)S(1)}, u32[]{:S(2)}, u32[]{:S(2)}) collective-permute-start(f32[32,512]{1,0:T(8,128)S(1)} %add_add_fusion.1), channel_id=1, source_target_pairs={{0,96},{1,97},{2,98},{3,99},{4,100},{5,101},{6,102},{7,103},{8,104... | collective-permute-start | bytes 196616 | tf_op jit(solution)/shard_map/ppermute | solution.py:41
  126.2 8.6 %collective-permute-start.22 = (f32[32,512]{1,0:T(8,128)S(1)}, f32[32,512]{1,0:T(8,128)S(1)}, u32[]{:S(2)}, u32[]{:S(2)}) collective-permute-start(f32[32,512]{1,0:T(8,128)S(1)} %add_add_fusion.1), channel_id=1, source_target_pairs={{0,32},{1,33},{2,34},{3,35},{4,36},{5,37},{6,38},{7,39},{8,40},{9,... | collective-permute-start | bytes 196616 | tf_op jit(solution)/shard_map/ppermute | solution.py:41
  127.0 7.8 %collective-permute-start.21 = (f32[32,512]{1,0:T(8,128)S(1)}, f32[32,512]{1,0:T(8,128)S(1)}, u32[]{:S(2)}, u32[]{:S(2)}) collective-permute-start(f32[32,512]{1,0:T(8,128)S(1)} %add_add_fusion.1), channel_id=1, source_target_pairs={{0,64},{1,65},{2,66},{3,67},{4,68},{5,69},{6,70},{7,71},{8,72},{9,... | collective-permute-start | bytes 196616 | tf_op jit(solution)/shard_map/ppermute | solution.py:41
  134.8 9.0 %collective-permute-start.26 = (bf16[128,4096]{1,0:T(8,128)(2,1)S(1)}, bf16[128,4096]{1,0:T(8,128)(2,1)S(1)}, u32[]{:S(2)}, u32[]{:S(2)}) collective-permute-start(bf16[128,4096]{1,0:T(8,128)(2,1)S(1)} %get-tuple-element.116), channel_id=1, source_target_pairs={{0,2},{1,3},{2,0},{3,1},{4,6},{5,7},{6,4},{7,5},{8,10},{9,11},{10,... | collective-permute-start | bytes 3145736 | tf_op jit(solution)/shard_map/ppermute | solution.py:41
  136.5 5.7 %collective-permute-start.24 = (f32[32,512]{1,0:T(8,128)S(1)}, f32[32,512]{1,0:T(8,128)S(1)}, u32[]{:S(2)}, u32[]{:S(2)}) collective-permute-start(f32[32,512]{1,0:T(8,128)S(1)} %add_add_fusion), channel_id=1, source_target_pairs={{0,4},{1,5},{2,6},{3,7},{4,0},{5,1},{6,2},{7,3},{8,12},{9,13},{10,... | collective-permute-start | bytes 196616 | tf_op jit(solution)/shard_map/ppermute | solution.py:41
  142.3 1.6 collective-permute-start.25
  (15 other events, 113.1 us)

commit v3 on v2

--- a/solution.py
+++ b/solution.py
@@ -21,20 +21,22 @@
 HALF = COUNT // 2
 
 
-def permutation(z=0, y=0, x=0, core=0, flip=None):
-    pairs = []
+def permutation(z=0, y=0, x=0, core=0, pairs=None):
+    result = []
     for source in range(128):
         cz, cy, ch, cc, cl = (int(v) for v in np.unravel_index(source, SIZES))
-        cx = ch * 2 + cl
-        cx = (cx + x) % 4 if flip is None else flip[cx]
-        target = ((cz + z) % 4, (cy + y) % 4, cx // 2, (cc + core) % 2, cx % 2)
-        pairs.append((source, int(np.ravel_multi_index(target, SIZES))))
-    return pairs
+        place = {"z": cz, "y": cy, "x": ch * 2 + cl}
+        if pairs is not None:
+            place[pairs[0]] = ((1, 0, 3, 2), (3, 2, 1, 0))[pairs[1]][place[pairs[0]]]
+        cz, cy, cx = (place["z"] + z) % 4, (place["y"] + y) % 4, (place["x"] + x) % 4
+        target = (cz, cy, cx // 2, (cc + core) % 2, cx % 2)
+        result.append((source, int(np.ravel_multi_index(target, SIZES))))
+    return result
 
 
 OTHER_CORE = permutation(core=1)
-PARTNER = permutation(flip=(1, 0, 3, 2))
-WRAP = permutation(flip=(3, 2, 1, 0))
+PARTNER = permutation(pairs=("x", 0))
+WRAP = permutation(pairs=("x", 1))
 
 
 def send(array, pairs):
@@ -78,13 +80,16 @@
         copy.wait()
 
 
-def call(kernel, name, operands, outs, scratch, limit, aliases=None, hbm=False):
+def call(kernel, name, operands, outs, scratch, limit, aliases=None, hbm=False, loose=()):
     anywhere = pl.BlockSpec(memory_space=pl.ANY)
-    far = [pltpu.with_memory_space_constraint(array, pltpu.HBM) for array in operands[1:]]
+    far = [
+        array if number in loose else pltpu.with_memory_space_constraint(array, pltpu.HBM)
+        for number, array in enumerate(operands[1:], 1)
+    ]
     return pl.pallas_call(
         kernel,
         out_shape=[(pltpu.HBM if hbm else jax.ShapeDtypeStruct)(shape, dtype) for shape, dtype in outs],
-        in_specs=[pl.BlockSpec(memory_space=pltpu.SMEM)] + [pl.BlockSpec(memory_space=pltpu.HBM)] * len(far),
+        in_specs=[pl.BlockSpec(memory_space=pltpu.SMEM)] + [anywhere if n in loose else pl.BlockSpec(memory_space=pltpu.HBM) for n in range(1, len(operands))],
         out_specs=[anywhere] * len(outs),
         scratch_shapes=scratch,
         input_output_aliases=aliases or {},
@@ -333,6 +338,27 @@
         ],
         28,
     )
+
+
+def inverse_kernel(gram, inverse):
+    both = jnp.concatenate([gram[...], jnp.eye(64, dtype=F32)], axis=1)
+    rows = lax.broadcasted_iota(jnp.int32, (64, 1), 0)
+    scale = jnp.zeros((64, 1), F32)
+    for j in range(64):
+        pivot = both[j : j + 1, j : j + 1]
+        scale = jnp.where(rows == j, pivot, scale)
+        factor = jnp.where(rows > j, both[:, j : j + 1], 0.0) / pivot
+        both = both - factor * both[j : j + 1, :]
+    inverse[...] = both[:, 64:] / jnp.sqrt(scale)
+
+
+def inverse_part(gram):
+    return pl.pallas_call(
+        inverse_kernel,
+        out_shape=jax.ShapeDtypeStruct((64, 64), F32),
+        cost_estimate=pl.CostEstimate(flops=1024, bytes_accessed=1024, transcendentals=0),
+        name="inverse_part",
+    )(gram)
 
 
 def final_kernel(
@@ -422,6 +448,7 @@
         ],
         44,
         aliases={7: 3},
+        loose=(3, 4, 5, 6),
     )
 
 
@@ -507,64 +534,54 @@
 
     tok_far = send(tok_other, PARTNER)
 
-    hidden_0, weight_0, hidden_1, weight_1, hidden_2, weight_2, weight_3, weight_4 = parcel_part(
-        core_arg,
-        masked_own,
-        hidden_rows,
-        key_weight,
-        [
-            ("hidden", 0, 48),
-            ("weight", 0, 576),
-            ("hidden", 48, 48),
-            ("weight", 576, 768),
-            ("hidden", 96, 32),
-            ("weight", 1344, 512),
-            ("weight", 1856, 1152),
-            ("weight", 3008, 1088),
-        ],
-    )
-    tok_far, hidden_0 = barrier((tok_far, hidden_0))
-    far_hidden_0 = send(hidden_0, PARTNER)
-    far_weight_0 = send(weight_0, WRAP)
+    lots = [("hidden", 0, 16), ("hidden", 16, 80), ("hidden", 96, 32)]
+    first = 0
+    for rows in (448, 1152, 448, 1024, 1024):
+        lots.append(("weight", first, rows))
+        first += rows
+    parcels = parcel_part(core_arg, masked_own, hidden_rows, key_weight, lots)
+    parcels, weights = list(parcels[:3]), list(parcels[3:])
+    tok_far, parcels[0], weights[0], masked_other = barrier((tok_far, parcels[0], weights[0], masked_other))
+    masked_far = send(masked_other, PARTNER)
+    far_hidden = [send(parcels[0], PARTNER)]
+    far_weight = [send(weights[0], WRAP)]
 
     keep, away = left_part(core_arg, err, hidden_rows, terms_t, tok_own, tok_far)
-    keep, away, far_hidden_0, far_weight_0, hidden_1, weight_1, masked_own, masked_other = barrier(
-        (keep, away, far_hidden_0, far_weight_0, hidden_1, weight_1, masked_own, masked_other)
+    keep, away, far_hidden[0], far_weight[0], parcels[1], weights[1], masked_far = barrier(
+        (keep, away, far_hidden[0], far_weight[0], parcels[1], weights[1], masked_far)
     )
     piece = keep + send(away, OTHER_CORE)
-    masked_far = send(masked_other, PARTNER)
-    far_hidden_1 = send(hidden_1, PARTNER)
-    far_weight_1 = send(weight_1, WRAP)
+    far_hidden.append(send(parcels[1], PARTNER))
+    far_weight.append(send(weights[1], WRAP))
+    far_hidden[1], far_weight[1], masked_own = barrier((far_hidden[1], far_weight[1], masked_own))
+    near_other = send(masked_own, OTHER_CORE)
     piece = lax.all_to_all(piece, ("z", "y"), 0, 0, tiled=True)
     piece = jnp.sum(piece, axis=0)
-    piece, far_hidden_1, far_weight_1, masked_far = barrier((piece, far_hidden_1, far_weight_1, masked_far))
+    piece, near_other = barrier((piece, near_other))
     piece = sum_of_four(piece, "x")
 
-    piece, hidden_2, weight_2, masked_own, masked_far = barrier((piece, hidden_2, weight_2, masked_own, masked_far))
-    far_hidden_2 = send(hidden_2, PARTNER)
-    far_weight_2 = send(weight_2, WRAP)
-    near_other = send(masked_own, OTHER_CORE)
+    piece, parcels[2], weights[2], masked_far = barrier((piece, parcels[2], weights[2], masked_far))
+    far_hidden.append(send(parcels[2], PARTNER))
+    far_weight.append(send(weights[2], WRAP))
     far_other = send(masked_far, OTHER_CORE)
     mine = lax.all_to_all(jnp.broadcast_to(piece[None], (16, 64, 256)), ("z", "y"), 0, 0, tiled=True)
-    mine, far_hidden_2, far_weight_2, weight_3, weight_4, near_other, far_other = barrier(
-        (mine, far_hidden_2, far_weight_2, weight_3, weight_4, near_other, far_other)
-    )
-    far_weight_3 = send(weight_3, WRAP)
-    far_weight_4 = send(weight_4, PARTNER)
+    mine, far_hidden[2], far_weight[2], weights[3], weights[4], far_other = barrier(
+        (mine, far_hidden[2], far_weight[2], weights[3], weights[4], far_other)
+    )
+    far_weight.append(send(weights[3], WRAP))
+    far_weight.append(send(weights[4], PARTNER))
     other = send(mine, OTHER_CORE)
 
-    hidden = [hidden_rows, far_hidden_0, far_hidden_1, far_hidden_2]
+    hidden = [hidden_rows, *far_hidden]
     keep, away, gram = right_part(core_arg, mine, other, err, hidden, masked_own, masked_other)
     total = keep + send(away, OTHER_CORE)
     total, gram = barrier((total, gram))
-    factor_low = jnp.linalg.cholesky(gram)
+    inverse = inverse_part(gram)
     total = sum_of_four(total, "y")
-    total, factor_low, far_weight_3, far_weight_4 = barrier((total, factor_low, far_weight_3, far_weight_4))
-    pieces = [far_weight_0, far_weight_1, far_weight_2, far_weight_3, far_weight_4]
-    grad, grad_other = input_part(core_arg, masked_own, near_other, masked_far, far_other, key_weight, pieces)
+    total, inverse, far_weight[3], far_weight[4] = barrier((total, inverse, far_weight[3], far_weight[4]))
+    grad, grad_other = input_part(core_arg, masked_own, near_other, masked_far, far_other, key_weight, far_weight)
     total = sum_of_four(total, "z")
-    total, factor_low, grad_other = barrier((total, factor_low, grad_other))
-    inverse = jax.scipy.linalg.solve_triangular(factor_low, jnp.eye(64, dtype=F32), lower=True)
+    total, grad_other = barrier((total, grad_other))
     grad_far = send(grad_other, OTHER_CORE)
     total = total + send(total, permutation(x=2))
     total_other = send(total, OTHER_CORE)

time: 161 us -> 153 us (0.950)
  other arithmetic: 13.4 us -> 1.25 us
  Pallas kernels: 48.4 us -> 55.9 us
  starting transfers between devices: 49.9 us -> 45.3 us
  waiting for transfers between devices: 43.6 us -> 47 us
    ppermute x27, waiting for transfers between devices: 27.7 us -> 43.2 us  [send(): return lax.ppermute(array, AXES, pairs)]
    all_to_all x1, waiting for transfers between devices: 13.5 us -> 0.01 us  [local(): piece = lax.all_to_all(piece, ('z', 'y'), 0, 0, tiled=True)]
    another operation x5 -> x0, other arithmetic: 11.4 us -> none  [the longest x3 6.52 us: local(): factor_low = jnp.linalg.cholesky(gram)]
    pallas_call x0 -> x1, Pallas kernels: none -> 7.03 us  [inverse_part(): pl.pallas_call(inverse_kernel, out_shape=jax.ShapeDtypeStruct((64, 64), F...]
    ppermute x27, starting transfers between devices: 35.8 us -> 29.8 us  [send(): return lax.ppermute(array, AXES, pairs)]
  transfers between devices with their start and end apart: 29 -> 29, of which waited for: 15 -> 16; matrix products, arithmetic and copies ran while one was open for 8% -> 1% of each run, Pallas kernels for 19% -> 25%
where the time goes in v3:
time: 153 us
  Pallas kernels  55.9 us (37%)
  waiting for transfers between devices  47 us (31%)
  starting transfers between devices  45.3 us (30%)
  local copies, waits for them, and re-layouts  2.14 us (1%)
    pallas_call x6, Pallas kernels, call(): pl.pallas_call(kernel, out_shape=[(pltpu.HBM if hbm else jax.ShapeDtypeSt...  48.8 us
    ppermute x27, waiting for transfers between devices, send(): return lax.ppermute(array, AXES, pairs)  43.2 us
    ppermute x27, starting transfers between devices, send(): return lax.ppermute(array, AXES, pairs)  29.8 us
    all_to_all x1, starting transfers between devices, local(): piece = lax.all_to_all(piece, ('z', 'y'), 0, 0, tiled=True)  7.77 us
    all_to_all x1, starting transfers between devices, local(): lax.all_to_all(jnp.broadcast_to(piece[None], (16, 64, 256)), ('z', 'y'),...  7.77 us
    pallas_call x1, Pallas kernels, inverse_part(): pl.pallas_call(inverse_kernel, out_shape=jax.ShapeDtypeStruct((64, 64), F...  7.03 us
    all_to_all x1, waiting for transfers between devices, local(): lax.all_to_all(jnp.broadcast_to(piece[None], (16, 64, 256)), ('z', 'y'),...  3.81 us
  transfers between devices with their start and end apart: 29, of which 16 were waited for; matrix products, arithmetic and copies ran while one was open for 1% of the time, Pallas kernels for 25%

profile of v3, /device:TPU:1, one launch (start us, length us, event | category | flops | bytes accessed | tf_op | source)
XLA Modules:
  0.0 152.7 jit_solution(6023368630975802696)
XLA Ops:
  0.6 2.3 %token_part.1 = (bf16[128,512]{1,0:T(8,128)(2,1)}, bf16[128,512]{1,0:T(8,128)(2,1)}, f32[64,128]{1,0:T(8,128)}, f32[64,128]{1,0:T(8,128)}, bf16[192,512]{1,0:T(8,128)(2,1)}) custom-call(s32[1]{0:T(128)} %bitcast.2.xl_ref, bf16[256,512]{1,0:T(8,128)(2,1)} %grads.1, s32[1,256]{1,0:T(1,128)} %bitcast.11, f32[64,512]{1,0:T(8,128)} %bitcast.10), custom_call_target="tpu_custom_call" | custom-call | flops 1024 | bytes 1024 | tf_op jit(solution)/shard_map/token_part/pallas_call | solution.py:89
  3.0 2.1 %collective-permute-start = (f32[64,128]{1,0:T(8,128)}, f32[64,128]{1,0:T(8,128)S(1)}, u32[]{:S(2)}, u32[]{:S(2)}) collective-permute-start(f32[64,128]{1,0:T(8,128)} %get-tuple-element.64), channel_id=1, source_target_pairs={{0,1},{1,0},{2,3},{3,2},{4,5},{5,4},{6,7},{7,6},{8,9},{9,8},{10,11... | collective-permute-start | bytes 98312 | tf_op jit(solution)/shard_map/ppermute | solution.py:43
  5.1 5.4 %parcel_part.1 = (bf16[16,8192]{1,0:T(8,128)(2,1)}, bf16[80,8192]{1,0:T(8,128)(2,1)}, bf16[32,8192]{1,0:T(8,128)(2,1)}, bf16[448,512]{1,0:T(8,128)(2,1)}, bf16[1...) custom-call(s32[1]{0:T(128)} %bitcast.core_ref, ...), custom_call_target="tpu_custom_call" | custom-call | flops 1024 | bytes 1024 | tf_op jit(solution)/shard_map/parcel_part/pallas_call | solution.py:89
  10.5 1.9 %collective-permute-start.2 = (bf16[448,512]{1,0:T(8,128)(2,1)}, bf16[448,512]{1,0:T(8,128)(2,1)S(1)}, u32[]{:S(2)}, u32[]{:S(2)}) collective-permute-start(bf16[448,512]{1,0:T(8,128)(2,1)} %get-tuple-element.73), channel_id=1, source_target_pairs={{0,5},{1,4},{2,7},{3,6},{4,1},{5,0},{6,3},{7,2},{8,13},{9,12},{10,... | collective-permute-start | bytes 1376264 | tf_op jit(solution)/shard_map/ppermute | solution.py:43
  12.7 1.2 collective-permute-start.3
  13.9 10.2 %left_part.1 = (f32[16,64,256]{2,1,0:T(8,128)S(1)}, f32[16,64,256]{2,1,0:T(8,128)S(1)}) custom-call(s32[1]{0:T(128)} %bitcast.core_ref, bf16[8192,512]{1,0:T(8,128)(2,1)} %bitcast.7, bf16[128,8192]{1,0:T(8,128)(2,1)} %refs_0_.3, bf16[192,512]{1,0:T(8,128)(2,1)} %get-tuple-element.62.terms_t, f32[64,128]{1,0:T(8,128)} %get-tuple-element.63.tok_own, ...), custom_call_target="tpu_custom_call" | custom-call | flops 1024 | bytes 1024 | tf_op jit(solution)/shard_map/left_part/pallas_call | solution.py:89
  24.2 1.9 %collective-permute-start.6 = (f32[16,64,256]{2,1,0:T(8,128)S(1)}, f32[16,64,256]{2,1,0:T(8,128)S(1)}, u32[]{:S(2)}, u32[]{:S(2)}) collective-permute-start(f32[16,64,256]{2,1,0:T(8,128)S(1)} %get-tuple-element.81), channel_id=1, source_target_pairs={{0,2},{1,3},{2,0},{3,1},{4,6},{5,7},{6,4},{7,5},{8,10},{9,11},{10,... | collective-permute-start | bytes 3145736 | tf_op jit(solution)/shard_map/ppermute | solution.py:43
  26.9 1.4 collective-permute-done.6
  28.3 1.1 add.36
  29.4 7.8 %all-to-all-start = ((f32[16,64,256]{2,1,0:T(8,128)}), f32[16,64,256]{2,1,0:T(8,128)S(1)}, u32[]{:S(2)}, u32[]{:S(2)}) async-start(f32[16,64,256]{2,1,0:T(8,128)} %add.36), calls=%async_computation | async-start | bytes 2097152 | tf_op jit(solution)/shard_map/all_to_all | solution.py:558
  37.2 17.9 %collective-permute-done.5.refs_1_ = bf16[1152,512]{1,0:T(8,128)(2,1)} collective-permute-done((bf16[1152,512]{1,0:T(8,128)(2,1)}, bf16[1152,512]{1,0:T(8,128)(2,1)}, u32[]{:S(2)}, u32[]{:S(2)}) %collective-permute-start.5) | collective-permute-done | bytes 1179680 | tf_op jit(solution)/shard_map/ppermute | solution.py:43
  55.1 1.5 collective-permute-done.4.refs_2_
  60.5 1.0 collective-permute-done.10
  61.6 2.1 %collective-permute-done.9 = f32[64,256]{1,0:T(8,128)S(1)} collective-permute-done((f32[64,256]{1,0:T(8,128)S(1)}, f32[64,256]{1,0:T(8,128)S(1)}, u32[]{:S(2)}, u32[]{:S(2)}) %collective-permute-start.9) | collective-permute-done | bytes 65568 | tf_op jit(solution)/shard_map/ppermute | solution.py:43
  64.6 1.1 broadcast_in_dim.17
  65.7 7.8 %all-to-all-start.1 = ((f32[16,64,256]{2,1,0:T(8,128)}), f32[16,64,256]{2,1,0:T(8,128)S(1)}, u32[]{:S(2)}, u32[]{:S(2)}) async-start(f32[16,64,256]{2,1,0:T(8,128)} %broadcast_in_dim.17), calls=%async_computation.1 | async-start | bytes 2097152 | tf_op jit(solution)/shard_map/all_to_all | solution.py:567
  73.8 1.8 %collective-permute-start.12 = (bf16[448,512]{1,0:T(8,128)(2,1)}, bf16[448,512]{1,0:T(8,128)(2,1)S(1)}, u32[]{:S(2)}, u32[]{:S(2)}) collective-permute-start(bf16[448,512]{1,0:T(8,128)(2,1)} %get-tuple-element.88), channel_id=1, source_target_pairs={{0,5},{1,4},{2,7},{3,6},{4,1},{5,0},{6,3},{7,2},{8,13},{9,12},{10,... | collective-permute-start | bytes 1376264 | tf_op jit(solution)/shard_map/ppermute | solution.py:43
  75.7 2.6 %collective-permute-start.13 = (bf16[128,512]{1,0:T(8,128)(2,1)S(1)}, bf16[128,512]{1,0:T(8,128)(2,1)S(1)}, u32[]{:S(2)}, u32[]{:S(2)}) collective-permute-start(bf16[128,512]{1,0:T(8,128)(2,1)S(1)} %copy-done.12), channel_id=1, source_target_pairs={{0,2},{1,3},{2,0},{3,1},{4,6},{5,7},{6,4},{7,5},{8,10},{9,11},{10,... | collective-permute-start | bytes 393224 | tf_op jit(solution)/shard_map/ppermute | solution.py:43
  79.3 5.3 %collective-permute-done.12.refs_2_ = bf16[448,512]{1,0:T(8,128)(2,1)S(1)} collective-permute-done((bf16[448,512]{1,0:T(8,128)(2,1)}, bf16[448,512]{1,0:T(8,128)(2,1)S(1)}, u32[]{:S(2)}, u32[]{:S(2)}) %collective-permute-start.12) | collective-permute-done | bytes 458784 | tf_op jit(solution)/shard_map/ppermute | solution.py:43
  84.6 3.8 %all-to-all-done.1.mine = f32[16,64,256]{2,1,0:T(8,128)S(1)} async-done(((f32[16,64,256]{2,1,0:T(8,128)}), f32[16,64,256]{2,1,0:T(8,128)S(1)}, u32[]{:S(2)}, u32[]{:S(2)}) %all-to-all-start.1) | async-done | bytes 1048608 | tf_op jit(solution)/shard_map/all_to_all | solution.py:567
  88.5 3.5 %collective-permute-start.14 = (f32[16,64,256]{2,1,0:T(8,128)S(1)}, f32[16,64,256]{2,1,0:T(8,128)S(1)}, u32[]{:S(2)}, u32[]{:S(2)}) collective-permute-start(f32[16,64,256]{2,1,0:T(8,128)S(1)} %all-to-all-done.1.mine), channel_id=1, source_target_pairs={{0,2},{1,3},{2,0},{3,1},{4,6},{5,7},{6,4},{7,5},{8,10},{9,11},{10,... | collective-permute-start | bytes 3145736 | tf_op jit(solution)/shard_map/ppermute | solution.py:43
  92.0 2.0 %collective-permute-start.19 = (bf16[1024,512]{1,0:T(8,128)(2,1)}, bf16[1024,512]{1,0:T(8,128)(2,1)}, u32[]{:S(2)}, u32[]{:S(2)}) collective-permute-start(bf16[1024,512]{1,0:T(8,128)(2,1)} %get-tuple-element.101), channel_id=1, source_target_pairs={{0,5},{1,4},{2,7},{3,6},{4,1},{5,0},{6,3},{7,2},{8,13},{9,12},{10,... | collective-permute-start | bytes 3145736 | tf_op jit(solution)/shard_map/ppermute | solution.py:43
  95.2 8.5 %right_part.1 = (f32[32,512]{1,0:T(8,128)S(1)}, f32[32,512]{1,0:T(8,128)S(1)}, f32[64,64]{1,0:T(8,128)S(1)}) custom-call(s32[1]{0:T(128)} %bitcast.core_ref, f32[16,64,256]{2,1,0:T(8,128)} %copy-done.2, f32[16,64,256]{2,1,0:T(8,128)} %copy-done.4, bf16[8192,512]{1,0:T(8,128)(2,1)} %bitcast.8, bf16[128,512]{1,0:T(8,128)(2,1)} %get-tuple-element.79.after.masked_own.near_own, ...), custom_call_target="tpu_custom_call" | custom-call | flops 1024 | bytes 1024 | tf_op jit(solution)/shard_map/right_part/pallas_call | solution.py:89
  105.3 1.5 collective-permute-start.17
  107.4 7.0 %inverse_part.1.inverse = f32[64,64]{1,0:T(8,128)} custom-call(f32[64,64]{1,0:T(8,128)} %copy-done.1), custom_call_target="tpu_custom_call" | custom-call | flops 1024 | bytes 1024 | tf_op jit(solution)/shard_map/inverse_part/pallas_call | solution.py:356
  114.5 3.8 %collective-permute-done.19.refs_3_ = bf16[1024,512]{1,0:T(8,128)(2,1)} collective-permute-done((bf16[1024,512]{1,0:T(8,128)(2,1)}, bf16[1024,512]{1,0:T(8,128)(2,1)}, u32[]{:S(2)}, u32[]{:S(2)}) %collective-permute-start.19) | collective-permute-done | bytes 1048608 | tf_op jit(solution)/shard_map/ppermute | solution.py:43
  119.0 1.2 collective-permute-start.22
  120.8 6.8 %input_part.1 = (bf16[128,8192]{1,0:T(8,128)(2,1)}, bf16[128,4096]{1,0:T(8,128)(2,1)S(1)}) custom-call(s32[1]{0:T(128)} %bitcast.core_ref, bf16[128,512]{1,0:T(8,128)(2,1)} %get-tuple-element.79.after.masked_own.near_own, bf16[128,512]{1,0:T(8,128)(2,1)} %copy-done.13, bf16[128,512]{1,0:T(8,128)(2,1)} %copy-done.11, bf16[128,512]{1,0:T(8,128)(2,1)} %copy-done.14, ...), custom_call_target="tpu_custom_call" | custom-call | flops 1024 | bytes 1024 | tf_op jit(solution)/shard_map/input_part/pallas_call | solution.py:89
  127.7 2.0 %collective-permute-start.26 = (bf16[128,4096]{1,0:T(8,128)(2,1)S(1)}, bf16[128,4096]{1,0:T(8,128)(2,1)S(1)}, u32[]{:S(2)}, u32[]{:S(2)}) collective-permute-start(bf16[128,4096]{1,0:T(8,128)(2,1)S(1)} %get-tuple-element.114), channel_id=1, source_target_pairs={{0,2},{1,3},{2,0},{3,1},{4,6},{5,7},{6,4},{7,5},{8,10},{9,11},{10,... | collective-permute-start | bytes 3145736 | tf_op jit(solution)/shard_map/ppermute | solution.py:43
  130.1 4.8 %collective-permute-done.24 = f32[32,512]{1,0:T(8,128)S(1)} collective-permute-done((f32[32,512]{1,0:T(8,128)S(1)}, f32[32,512]{1,0:T(8,128)S(1)}, u32[]{:S(2)}, u32[]{:S(2)}) %collective-permute-start.24) | collective-permute-done | bytes 65568 | tf_op jit(solution)/shard_map/ppermute | solution.py:43
  134.9 1.2 collective-permute-start.25
  136.9 15.6 %final_part.1 = (bf16[8192,512]{1,0:T(8,128)(2,1)}, bf16[8192,512]{1,0:T(8,128)(2,1)}, f32[64,512]{1,0:T(8,128)}, bf16[128,8192]{1,0:T(8,128)(2,1)}) custom-call(s32[1]{0:T(128)} %bitcast.core_ref, bf16[128,512]{1,0:T(8,128)(2,1)} %get-tuple-element.79.after.masked_own.near_own, ...), custom_call_target="tpu_custom_call", output_to_operand_aliasing={{3}: (7, {})} | custom-call | flops 1024 | bytes 1024 | tf_op jit(solution)/shard_map/final_part/pallas_call | solution.py:89
  (75 shorter events, 13.5 us)
Async XLA Ops:
  3.0 7.5 %collective-permute-start = (f32[64,128]{1,0:T(8,128)}, f32[64,128]{1,0:T(8,128)S(1)}, u32[]{:S(2)}, u32[]{:S(2)}) collective-permute-start(f32[64,128]{1,0:T(8,128)} %get-tuple-element.64), channel_id=1, source_target_pairs={{0,1},{1,0},{2,3},{3,2},{4,5},{5,4},{6,7},{7,6},{8,9},{9,8},{10,11... | collective-permute-start | bytes 98312 | tf_op jit(solution)/shard_map/ppermute | solution.py:43
  10.5 13.6 %collective-permute-start.2 = (bf16[448,512]{1,0:T(8,128)(2,1)}, bf16[448,512]{1,0:T(8,128)(2,1)S(1)}, u32[]{:S(2)}, u32[]{:S(2)}) collective-permute-start(bf16[448,512]{1,0:T(8,128)(2,1)} %get-tuple-element.73), channel_id=1, source_target_pairs={{0,5},{1,4},{2,7},{3,6},{4,1},{5,0},{6,3},{7,2},{8,13},{9,12},{10,... | collective-permute-start | bytes 1376264 | tf_op jit(solution)/shard_map/ppermute | solution.py:43
  12.4 11.7 %collective-permute-start.1 = (bf16[16,8192]{1,0:T(8,128)(2,1)}, bf16[16,8192]{1,0:T(8,128)(2,1)S(1)}, u32[]{:S(2)}, u32[]{:S(2)}) collective-permute-start(bf16[16,8192]{1,0:T(8,128)(2,1)} %get-tuple-element.72), channel_id=1, source_target_pairs={{0,1},{1,0},{2,3},{3,2},{4,5},{5,4},{6,7},{7,6},{8,9},{9,8},{10,11... | collective-permute-start | bytes 786440 | tf_op jit(solution)/shard_map/ppermute | solution.py:43
  12.7 11.4 %collective-permute-start.3 = (bf16[128,512]{1,0:T(8,128)(2,1)S(1)}, bf16[128,512]{1,0:T(8,128)(2,1)S(1)}, u32[]{:S(2)}, u32[]{:S(2)}) collective-permute-start(bf16[128,512]{1,0:T(8,128)(2,1)S(1)} %copy-done.8), channel_id=1, source_target_pairs={{0,1},{1,0},{2,3},{3,2},{4,5},{5,4},{6,7},{7,6},{8,9},{9,8},{10,11... | collective-permute-start | bytes 393224 | tf_op jit(solution)/shard_map/ppermute | solution.py:43
  24.2 32.4 %copy-start.5 = (bf16[128,512]{1,0:T(8,128)(2,1)S(1)}, bf16[128,512]{1,0:T(8,128)(2,1)}, u32[]{:S(2)}) copy-start(bf16[128,512]{1,0:T(8,128)(2,1)} %get-tuple-element.79.after.masked_own.near_own) | copy-start | bytes 393220
  24.2 4.1 %collective-permute-start.6 = (f32[16,64,256]{2,1,0:T(8,128)S(1)}, f32[16,64,256]{2,1,0:T(8,128)S(1)}, u32[]{:S(2)}, u32[]{:S(2)}) collective-permute-start(f32[16,64,256]{2,1,0:T(8,128)S(1)} %get-tuple-element.81), channel_id=1, source_target_pairs={{0,2},{1,3},{2,0},{3,1},{4,6},{5,7},{6,4},{7,5},{8,10},{9,11},{10,... | collective-permute-start | bytes 3145736 | tf_op jit(solution)/shard_map/ppermute | solution.py:43
  26.0 30.5 %collective-permute-start.4 = (bf16[80,8192]{1,0:T(8,128)(2,1)}, bf16[80,8192]{1,0:T(8,128)(2,1)S(1)}, u32[]{:S(2)}, u32[]{:S(2)}) collective-permute-start(bf16[80,8192]{1,0:T(8,128)(2,1)} %get-tuple-element.77), channel_id=1, source_target_pairs={{0,1},{1,0},{2,3},{3,2},{4,5},{5,4},{6,7},{7,6},{8,9},{9,8},{10,11... | collective-permute-start | bytes 3932168 | tf_op jit(solution)/shard_map/ppermute | solution.py:43
  26.4 28.7 %collective-permute-start.5 = (bf16[1152,512]{1,0:T(8,128)(2,1)}, bf16[1152,512]{1,0:T(8,128)(2,1)}, u32[]{:S(2)}, u32[]{:S(2)}) collective-permute-start(bf16[1152,512]{1,0:T(8,128)(2,1)} %get-tuple-element.78), channel_id=1, source_target_pairs={{0,5},{1,4},{2,7},{3,6},{4,1},{5,0},{6,3},{7,2},{8,13},{9,12},{10,... | collective-permute-start | bytes 3538952 | tf_op jit(solution)/shard_map/ppermute | solution.py:43
  29.4 28.0 %all-to-all-start = ((f32[16,64,256]{2,1,0:T(8,128)}), f32[16,64,256]{2,1,0:T(8,128)S(1)}, u32[]{:S(2)}, u32[]{:S(2)}) async-start(f32[16,64,256]{2,1,0:T(8,128)} %add.36), calls=%async_computation | async-start | bytes 2097152 | tf_op jit(solution)/shard_map/all_to_all | solution.py:558
  37.2 38.4 %copy-start.12 = (bf16[128,512]{1,0:T(8,128)(2,1)S(1)}, bf16[128,512]{1,0:T(8,128)(2,1)}, u32[]{:S(2)}) copy-start(bf16[128,512]{1,0:T(8,128)(2,1)} %copy-done.11) | copy-start | bytes 393220
  56.6 1.9 %collective-permute-start.7 = (bf16[128,512]{1,0:T(8,128)(2,1)S(1)}, bf16[128,512]{1,0:T(8,128)(2,1)S(1)}, u32[]{:S(2)}, u32[]{:S(2)}) collective-permute-start(bf16[128,512]{1,0:T(8,128)(2,1)S(1)} %copy-done.5), channel_id=1, source_target_pairs={{0,2},{1,3},{2,0},{3,1},{4,6},{5,7},{6,4},{7,5},{8,10},{9,11},{10,... | collective-permute-start | bytes 393224 | tf_op jit(solution)/shard_map/ppermute | solution.py:43
  58.4 45.4 %copy-start.13 = (bf16[128,512]{1,0:T(8,128)(2,1)}, bf16[128,512]{1,0:T(8,128)(2,1)S(1)}, u32[]{:S(2)}) copy-start(bf16[128,512]{1,0:T(8,128)(2,1)S(1)} %collective-permute-done.7.near_other) | copy-start | bytes 393220
  58.4 3.1 %collective-permute-start.10 = (f32[64,256]{1,0:T(8,128)S(1)}, f32[64,256]{1,0:T(8,128)S(1)}, u32[]{:S(2)}, u32[]{:S(2)}) collective-permute-start(f32[64,256]{1,0:T(8,128)S(1)} %reduce_sum.9), channel_id=1, source_target_pairs={{0,5},{1,0},{2,7},{3,2},{4,1},{5,4},{6,3},{7,6},{8,13},{9,8},{10,1... | collective-permute-start | bytes 196616 | tf_op jit(solution)/shard_map/ppermute | solution.py:43
  59.3 4.3 %collective-permute-start.9 = (f32[64,256]{1,0:T(8,128)S(1)}, f32[64,256]{1,0:T(8,128)S(1)}, u32[]{:S(2)}, u32[]{:S(2)}) collective-permute-start(f32[64,256]{1,0:T(8,128)S(1)} %reduce_sum.9), channel_id=1, source_target_pairs={{0,1},{1,4},{2,3},{3,6},{4,5},{5,0},{6,7},{7,2},{8,9},{9,12},{10,1... | collective-permute-start | bytes 196616 | tf_op jit(solution)/shard_map/ppermute | solution.py:43
  59.9 4.7 %collective-permute-start.8 = (f32[64,256]{1,0:T(8,128)S(1)}, f32[64,256]{1,0:T(8,128)S(1)}, u32[]{:S(2)}, u32[]{:S(2)}) collective-permute-start(f32[64,256]{1,0:T(8,128)S(1)} %reduce_sum.9), channel_id=1, source_target_pairs={{0,4},{1,5},{2,6},{3,7},{4,0},{5,1},{6,2},{7,3},{8,12},{9,13},{10,... | collective-permute-start | bytes 196616 | tf_op jit(solution)/shard_map/ppermute | solution.py:43
  65.7 22.8 %all-to-all-start.1 = ((f32[16,64,256]{2,1,0:T(8,128)}), f32[16,64,256]{2,1,0:T(8,128)S(1)}, u32[]{:S(2)}, u32[]{:S(2)}) async-start(f32[16,64,256]{2,1,0:T(8,128)} %broadcast_in_dim.17), calls=%async_computation.1 | async-start | bytes 2097152 | tf_op jit(solution)/shard_map/all_to_all | solution.py:567
  73.5 11.2 %collective-permute-start.11 = (bf16[32,8192]{1,0:T(8,128)(2,1)S(1)}, bf16[32,8192]{1,0:T(8,128)(2,1)S(1)}, u32[]{:S(2)}, u32[]{:S(2)}) collective-permute-start(bf16[32,8192]{1,0:T(8,128)(2,1)S(1)} %copy-done.16), channel_id=1, source_target_pairs={{0,1},{1,0},{2,3},{3,2},{4,5},{5,4},{6,7},{7,6},{8,9},{9,8},{10,11... | collective-permute-start | bytes 1572872 | tf_op jit(solution)/shard_map/ppermute | solution.py:43
  73.8 10.8 %collective-permute-start.12 = (bf16[448,512]{1,0:T(8,128)(2,1)}, bf16[448,512]{1,0:T(8,128)(2,1)S(1)}, u32[]{:S(2)}, u32[]{:S(2)}) collective-permute-start(bf16[448,512]{1,0:T(8,128)(2,1)} %get-tuple-element.88), channel_id=1, source_target_pairs={{0,5},{1,4},{2,7},{3,6},{4,1},{5,0},{6,3},{7,2},{8,13},{9,12},{10,... | collective-permute-start | bytes 1376264 | tf_op jit(solution)/shard_map/ppermute | solution.py:43
  75.7 3.6 %collective-permute-start.13 = (bf16[128,512]{1,0:T(8,128)(2,1)S(1)}, bf16[128,512]{1,0:T(8,128)(2,1)S(1)}, u32[]{:S(2)}, u32[]{:S(2)}) collective-permute-start(bf16[128,512]{1,0:T(8,128)(2,1)S(1)} %copy-done.12), channel_id=1, source_target_pairs={{0,2},{1,3},{2,0},{3,1},{4,6},{5,7},{6,4},{7,5},{8,10},{9,11},{10,... | collective-permute-start | bytes 393224 | tf_op jit(solution)/shard_map/ppermute | solution.py:43
  88.5 5.8 %collective-permute-start.14 = (f32[16,64,256]{2,1,0:T(8,128)S(1)}, f32[16,64,256]{2,1,0:T(8,128)S(1)}, u32[]{:S(2)}, u32[]{:S(2)}) collective-permute-start(f32[16,64,256]{2,1,0:T(8,128)S(1)} %all-to-all-done.1.mine), channel_id=1, source_target_pairs={{0,2},{1,3},{2,0},{3,1},{4,6},{5,7},{6,4},{7,5},{8,10},{9,11},{10,... | collective-permute-start | bytes 3145736 | tf_op jit(solution)/shard_map/ppermute | solution.py:43
  92.0 26.3 %collective-permute-start.19 = (bf16[1024,512]{1,0:T(8,128)(2,1)}, bf16[1024,512]{1,0:T(8,128)(2,1)}, u32[]{:S(2)}, u32[]{:S(2)}) collective-permute-start(bf16[1024,512]{1,0:T(8,128)(2,1)} %get-tuple-element.101), channel_id=1, source_target_pairs={{0,5},{1,4},{2,7},{3,6},{4,1},{5,0},{6,3},{7,2},{8,13},{9,12},{10,... | collective-permute-start | bytes 3145736 | tf_op jit(solution)/shard_map/ppermute | solution.py:43
  94.0 24.8 %collective-permute-start.20 = (bf16[1024,512]{1,0:T(8,128)(2,1)}, bf16[1024,512]{1,0:T(8,128)(2,1)}, u32[]{:S(2)}, u32[]{:S(2)}) collective-permute-start(bf16[1024,512]{1,0:T(8,128)(2,1)} %get-tuple-element.102), channel_id=1, source_target_pairs={{0,1},{1,0},{2,3},{3,2},{4,5},{5,4},{6,7},{7,6},{8,9},{9,8},{10,11... | collective-permute-start | bytes 3145736 | tf_op jit(solution)/shard_map/ppermute | solution.py:43
  103.8 1.4 collective-permute-start.15
  105.2 9.2 %collective-permute-start.18 = (f32[32,512]{1,0:T(8,128)S(1)}, f32[32,512]{1,0:T(8,128)S(1)}, u32[]{:S(2)}, u32[]{:S(2)}) collective-permute-start(f32[32,512]{1,0:T(8,128)S(1)} %add.40), channel_id=1, source_target_pairs={{0,24},{1,25},{2,26},{3,27},{4,28},{5,29},{6,30},{7,31},{8,0},{9,1... | collective-permute-start | bytes 196616 | tf_op jit(solution)/shard_map/ppermute | solution.py:43
  105.3 9.1 %collective-permute-start.17 = (f32[32,512]{1,0:T(8,128)S(1)}, f32[32,512]{1,0:T(8,128)S(1)}, u32[]{:S(2)}, u32[]{:S(2)}) collective-permute-start(f32[32,512]{1,0:T(8,128)S(1)} %add.40), channel_id=1, source_target_pairs={{0,8},{1,9},{2,10},{3,11},{4,12},{5,13},{6,14},{7,15},{8,16},{9,17... | collective-permute-start | bytes 196616 | tf_op jit(solution)/shard_map/ppermute | solution.py:43
  106.8 7.7 %collective-permute-start.16 = (f32[32,512]{1,0:T(8,128)S(1)}, f32[32,512]{1,0:T(8,128)S(1)}, u32[]{:S(2)}, u32[]{:S(2)}) collective-permute-start(f32[32,512]{1,0:T(8,128)S(1)} %add.40), channel_id=1, source_target_pairs={{0,16},{1,17},{2,18},{3,19},{4,20},{5,21},{6,22},{7,23},{8,24},{9,... | collective-permute-start | bytes 196616 | tf_op jit(solution)/shard_map/ppermute | solution.py:43
  118.8 8.8 %collective-permute-start.23 = (f32[32,512]{1,0:T(8,128)S(1)}, f32[32,512]{1,0:T(8,128)S(1)}, u32[]{:S(2)}, u32[]{:S(2)}) collective-permute-start(f32[32,512]{1,0:T(8,128)S(1)} %add_add_fusion.1), channel_id=1, source_target_pairs={{0,96},{1,97},{2,98},{3,99},{4,100},{5,101},{6,102},{7,103},{8,104... | collective-permute-start | bytes 196616 | tf_op jit(solution)/shard_map/ppermute | solution.py:43
  119.0 8.6 %collective-permute-start.22 = (f32[32,512]{1,0:T(8,128)S(1)}, f32[32,512]{1,0:T(8,128)S(1)}, u32[]{:S(2)}, u32[]{:S(2)}) collective-permute-start(f32[32,512]{1,0:T(8,128)S(1)} %add_add_fusion.1), channel_id=1, source_target_pairs={{0,32},{1,33},{2,34},{3,35},{4,36},{5,37},{6,38},{7,39},{8,40},{9,... | collective-permute-start | bytes 196616 | tf_op jit(solution)/shard_map/ppermute | solution.py:43
  120.2 7.4 %collective-permute-start.21 = (f32[32,512]{1,0:T(8,128)S(1)}, f32[32,512]{1,0:T(8,128)S(1)}, u32[]{:S(2)}, u32[]{:S(2)}) collective-permute-start(f32[32,512]{1,0:T(8,128)S(1)} %add_add_fusion.1), channel_id=1, source_target_pairs={{0,64},{1,65},{2,66},{3,67},{4,68},{5,69},{6,70},{7,71},{8,72},{9,... | collective-permute-start | bytes 196616 | tf_op jit(solution)/shard_map/ppermute | solution.py:43
  127.7 9.3 %collective-permute-start.26 = (bf16[128,4096]{1,0:T(8,128)(2,1)S(1)}, bf16[128,4096]{1,0:T(8,128)(2,1)S(1)}, u32[]{:S(2)}, u32[]{:S(2)}) collective-permute-start(bf16[128,4096]{1,0:T(8,128)(2,1)S(1)} %get-tuple-element.114), channel_id=1, source_target_pairs={{0,2},{1,3},{2,0},{3,1},{4,6},{5,7},{6,4},{7,5},{8,10},{9,11},{10,... | collective-permute-start | bytes 3145736 | tf_op jit(solution)/shard_map/ppermute | solution.py:43
  129.7 5.2 %collective-permute-start.24 = (f32[32,512]{1,0:T(8,128)S(1)}, f32[32,512]{1,0:T(8,128)S(1)}, u32[]{:S(2)}, u32[]{:S(2)}) collective-permute-start(f32[32,512]{1,0:T(8,128)S(1)} %add_add_fusion), channel_id=1, source_target_pairs={{0,4},{1,5},{2,6},{3,7},{4,0},{5,1},{6,2},{7,3},{8,12},{9,13},{10,... | collective-permute-start | bytes 196616 | tf_op jit(solution)/shard_map/ppermute | solution.py:43
  134.9 2.1 %collective-permute-start.25 = (f32[32,512]{1,0:T(8,128)S(1)}, f32[32,512]{1,0:T(8,128)S(1)}, u32[]{:S(2)}, u32[]{:S(2)}) collective-permute-start(f32[32,512]{1,0:T(8,128)S(1)} %add.47.total), channel_id=1, source_target_pairs={{0,2},{1,3},{2,0},{3,1},{4,6},{5,7},{6,4},{7,5},{8,10},{9,11},{10,... | collective-permute-start | bytes 196616 | tf_op jit(solution)/shard_map/ppermute | solution.py:43
  (14 other events, 134.9 us)

commit v4 on v3

--- a/solution.py
+++ b/solution.py
@@ -337,6 +337,7 @@
             pltpu.SemaphoreType.DMA((COUNT, len(hidden))),
         ],
         28,
+        loose=(9,),
     )
 
 
@@ -393,8 +394,8 @@
     coefficients = lax.dot_general(
         v_inv[...], v_factor[...], (((0,), (0,)), ((), ())), precision=HIGHEST, preferred_element_type=F32
     )
-    y1, y2, y3 = kernel_split3(coefficients)
-    ys = jnp.concatenate([y1, y1, y1, y2, y2, y3], axis=0)
+    y1, y2, _ = kernel_split3(coefficients)
+    ys = jnp.concatenate([y1, y1, y2, y2], axis=0)
     stores = [pltpu.make_async_copy(v_factor, factor, sems.at[5])]
     stores[0].start()
     for j in range(COUNT):
@@ -404,8 +405,8 @@
             start(loads[j + AHEAD])
         elif j + AHEAD == COUNT:
             grad_in.start()
-        l1, l2, l3 = kernel_split3(jnp.concatenate([v_left[place, 0], v_left[place, 1]], axis=1))
-        estimate = dot(jnp.concatenate([l1, l2, l3, l1, l2, l1], axis=0), ys, (0, 0))
+        l1, l2, _ = kernel_split3(jnp.concatenate([v_left[place, 0], v_left[place, 1]], axis=1))
+        estimate = dot(jnp.concatenate([l1, l2, l1, l2], axis=0), ys, (0, 0))
         merged = dot(v_hid[place], v_masked[...], (0, 0)) * (1.0 / 16.0) + v_err[place].astype(F32)
         slot = j % SLOTS
         if j >= SLOTS:
@@ -448,7 +449,7 @@
         ],
         44,
         aliases={7: 3},
-        loose=(3, 4, 5, 6),
+        loose=(3, 4, 5, 6, 14),
     )
 
 
@@ -534,21 +535,20 @@
 
     tok_far = send(tok_other, PARTNER)
 
-    lots = [("hidden", 0, 16), ("hidden", 16, 80), ("hidden", 96, 32)]
+    lots = [("hidden", 0, 32), ("hidden", 32, 64), ("hidden", 96, 32)]
     first = 0
-    for rows in (448, 1152, 448, 1024, 1024):
+    for rows in (512, 1024, 512, 1024, 1024):
         lots.append(("weight", first, rows))
         first += rows
     parcels = parcel_part(core_arg, masked_own, hidden_rows, key_weight, lots)
     parcels, weights = list(parcels[:3]), list(parcels[3:])
-    tok_far, parcels[0], weights[0], masked_other = barrier((tok_far, parcels[0], weights[0], masked_other))
-    masked_far = send(masked_other, PARTNER)
+    tok_far, parcels[0], weights[0] = barrier((tok_far, parcels[0], weights[0]))
     far_hidden = [send(parcels[0], PARTNER)]
     far_weight = [send(weights[0], WRAP)]
 
     keep, away = left_part(core_arg, err, hidden_rows, terms_t, tok_own, tok_far)
-    keep, away, far_hidden[0], far_weight[0], parcels[1], weights[1], masked_far = barrier(
-        (keep, away, far_hidden[0], far_weight[0], parcels[1], weights[1], masked_far)
+    keep, away, far_hidden[0], far_weight[0], parcels[1], weights[1] = barrier(
+        (keep, away, far_hidden[0], far_weight[0], parcels[1], weights[1])
     )
     piece = keep + send(away, OTHER_CORE)
     far_hidden.append(send(parcels[1], PARTNER))
@@ -560,17 +560,19 @@
     piece, near_other = barrier((piece, near_other))
     piece = sum_of_four(piece, "x")
 
-    piece, parcels[2], weights[2], masked_far = barrier((piece, parcels[2], weights[2], masked_far))
+    piece, parcels[2], weights[2], weights[3], weights[4], masked_other = barrier(
+        (piece, parcels[2], weights[2], weights[3], weights[4], masked_other)
+    )
+    masked_far = send(masked_other, PARTNER)
     far_hidden.append(send(parcels[2], PARTNER))
     far_weight.append(send(weights[2], WRAP))
-    far_other = send(masked_far, OTHER_CORE)
     mine = lax.all_to_all(jnp.broadcast_to(piece[None], (16, 64, 256)), ("z", "y"), 0, 0, tiled=True)
-    mine, far_hidden[2], far_weight[2], weights[3], weights[4], far_other = barrier(
-        (mine, far_hidden[2], far_weight[2], weights[3], weights[4], far_other)
-    )
+    mine, far_hidden[2], far_weight[2], masked_far = barrier((mine, far_hidden[2], far_weight[2], masked_far))
     far_weight.append(send(weights[3], WRAP))
     far_weight.append(send(weights[4], PARTNER))
+    far_other = send(masked_far, OTHER_CORE)
     other = send(mine, OTHER_CORE)
+    other, far_other = barrier((other, far_other))
 
     hidden = [hidden_rows, *far_hidden]
     keep, away, gram = right_part(core_arg, mine, other, err, hidden, masked_own, masked_other)

time: 153 us -> 150 us (0.980)
  waiting for transfers between devices: 47 us -> 42.3 us
  starting transfers between devices: 45.3 us -> 49.5 us
  Pallas kernels: 55.9 us -> 53.6 us
    all_to_all x1, waiting for transfers between devices: 3.81 us -> 0.3 us  [local(): lax.all_to_all(jnp.broadcast_to(piece[None], (16, 64, 256)), ('z', 'y'),...]
    ppermute x27, starting transfers between devices: 29.8 us -> 32.9 us  [send(): return lax.ppermute(array, AXES, pairs)]
    pallas_call x6, Pallas kernels: 48.8 us -> 46.6 us  [call(): pl.pallas_call(kernel, out_shape=[(pltpu.HBM if hbm else jax.ShapeDtypeSt...]
    ppermute x27, waiting for transfers between devices: 43.2 us -> 41.4 us  [send(): return lax.ppermute(array, AXES, pairs)]
  transfers between devices with their start and end apart: 29 -> 29, of which waited for: 16 -> 13; matrix products, arithmetic and copies ran while one was open for 1% -> 1% of each run, Pallas kernels for 25% -> 25%
where the time goes in v4:
time: 150 us
  Pallas kernels  53.6 us (36%)
  starting transfers between devices  49.5 us (33%)
  waiting for transfers between devices  42.3 us (28%)
  local copies, waits for them, and re-layouts  2.13 us (1%)
    pallas_call x6, Pallas kernels, call(): pl.pallas_call(kernel, out_shape=[(pltpu.HBM if hbm else jax.ShapeDtypeSt...  46.6 us
    ppermute x27, waiting for transfers between devices, send(): return lax.ppermute(array, AXES, pairs)  41.4 us
    ppermute x27, starting transfers between devices, send(): return lax.ppermute(array, AXES, pairs)  32.9 us
    all_to_all x1, starting transfers between devices, local(): lax.all_to_all(jnp.broadcast_to(piece[None], (16, 64, 256)), ('z', 'y'),...  8.89 us
    all_to_all x1, starting transfers between devices, local(): piece = lax.all_to_all(piece, ('z', 'y'), 0, 0, tiled=True)  7.77 us
    pallas_call x1, Pallas kernels, inverse_part(): pl.pallas_call(inverse_kernel, out_shape=jax.ShapeDtypeStruct((64, 64), F...  7.03 us
  transfers between devices with their start and end apart: 29, of which 13 were waited for; matrix products, arithmetic and copies ran while one was open for 1% of the time, Pallas kernels for 25%

profile of v4, /device:TPU:1, one launch (start us, length us, event | category | flops | bytes accessed | tf_op | source)
XLA Modules:
  0.0 149.9 jit_solution(15025161097430463796)
XLA Ops:
  0.6 2.3 %token_part.1 = (bf16[128,512]{1,0:T(8,128)(2,1)}, bf16[128,512]{1,0:T(8,128)(2,1)}, f32[64,128]{1,0:T(8,128)}, f32[64,128]{1,0:T(8,128)}, bf16[192,512]{1,0:T(8,128)(2,1)}) custom-call(s32[1]{0:T(128)} %bitcast.2.xl_ref, bf16[256,512]{1,0:T(8,128)(2,1)} %grads.1, s32[1,256]{1,0:T(1,128)} %bitcast.11, f32[64,512]{1,0:T(8,128)} %bitcast.10), custom_call_target="tpu_custom_call" | custom-call | flops 1024 | bytes 1024 | tf_op jit(solution)/shard_map/token_part/pallas_call | solution.py:89
  3.0 2.1 %collective-permute-start = (f32[64,128]{1,0:T(8,128)}, f32[64,128]{1,0:T(8,128)S(1)}, u32[]{:S(2)}, u32[]{:S(2)}) collective-permute-start(f32[64,128]{1,0:T(8,128)} %get-tuple-element.64), channel_id=1, source_target_pairs={{0,1},{1,0},{2,3},{3,2},{4,5},{5,4},{6,7},{7,6},{8,9},{9,8},{10,11... | collective-permute-start | bytes 98312 | tf_op jit(solution)/shard_map/ppermute | solution.py:43
  5.1 5.4 %parcel_part.1 = (bf16[32,8192]{1,0:T(8,128)(2,1)}, bf16[64,8192]{1,0:T(8,128)(2,1)}, bf16[32,8192]{1,0:T(8,128)(2,1)}, bf16[512,512]{1,0:T(8,128)(2,1)}, bf16[1...) custom-call(s32[1]{0:T(128)} %bitcast.core_ref, ...), custom_call_target="tpu_custom_call" | custom-call | flops 1024 | bytes 1024 | tf_op jit(solution)/shard_map/parcel_part/pallas_call | solution.py:89
  10.6 2.7 %collective-permute-start.2 = (bf16[512,512]{1,0:T(8,128)(2,1)}, bf16[512,512]{1,0:T(8,128)(2,1)S(1)}, u32[]{:S(2)}, u32[]{:S(2)}) collective-permute-start(bf16[512,512]{1,0:T(8,128)(2,1)} %get-tuple-element.72), channel_id=1, source_target_pairs={{0,5},{1,4},{2,7},{3,6},{4,1},{5,0},{6,3},{7,2},{8,13},{9,12},{10,... | collective-permute-start | bytes 1572872 | tf_op jit(solution)/shard_map/ppermute | solution.py:43
  13.4 10.2 %left_part.1 = (f32[16,64,256]{2,1,0:T(8,128)S(1)}, f32[16,64,256]{2,1,0:T(8,128)S(1)}) custom-call(s32[1]{0:T(128)} %bitcast.core_ref, bf16[8192,512]{1,0:T(8,128)(2,1)} %bitcast.7, bf16[128,8192]{1,0:T(8,128)(2,1)} %refs_0_.3, bf16[192,512]{1,0:T(8,128)(2,1)} %get-tuple-element.62.terms_t, f32[64,128]{1,0:T(8,128)} %get-tuple-element.63.tok_own, ...), custom_call_target="tpu_custom_call" | custom-call | flops 1024 | bytes 1024 | tf_op jit(solution)/shard_map/left_part/pallas_call | solution.py:89
  24.2 2.2 %collective-permute-start.5 = (f32[16,64,256]{2,1,0:T(8,128)S(1)}, f32[16,64,256]{2,1,0:T(8,128)S(1)}, u32[]{:S(2)}, u32[]{:S(2)}) collective-permute-start(f32[16,64,256]{2,1,0:T(8,128)S(1)} %get-tuple-element.79), channel_id=1, source_target_pairs={{0,2},{1,3},{2,0},{3,1},{4,6},{5,7},{6,4},{7,5},{8,10},{9,11},{10,... | collective-permute-start | bytes 3145736 | tf_op jit(solution)/shard_map/ppermute | solution.py:43
  26.6 2.5 %collective-permute-start.4 = (bf16[1024,512]{1,0:T(8,128)(2,1)}, bf16[1024,512]{1,0:T(8,128)(2,1)}, u32[]{:S(2)}, u32[]{:S(2)}) collective-permute-start(bf16[1024,512]{1,0:T(8,128)(2,1)} %get-tuple-element.76), channel_id=1, source_target_pairs={{0,5},{1,4},{2,7},{3,6},{4,1},{5,0},{6,3},{7,2},{8,13},{9,12},{10,... | collective-permute-start | bytes 3145736 | tf_op jit(solution)/shard_map/ppermute | solution.py:43
  29.1 1.1 add.36
  30.3 7.8 %all-to-all-start = ((f32[16,64,256]{2,1,0:T(8,128)}), f32[16,64,256]{2,1,0:T(8,128)S(1)}, u32[]{:S(2)}, u32[]{:S(2)}) async-start(f32[16,64,256]{2,1,0:T(8,128)} %add.36), calls=%async_computation | async-start | bytes 2097152 | tf_op jit(solution)/shard_map/all_to_all | solution.py:558
  38.0 13.6 %collective-permute-done.3.refs_2_ = bf16[64,8192]{1,0:T(8,128)(2,1)S(1)} collective-permute-done((bf16[64,8192]{1,0:T(8,128)(2,1)}, bf16[64,8192]{1,0:T(8,128)(2,1)S(1)}, u32[]{:S(2)}, u32[]{:S(2)}) %collective-permute-start.3) | collective-permute-done | bytes 1048608 | tf_op jit(solution)/shard_map/ppermute | solution.py:43
  52.6 1.1 collective-permute-start.6
  54.7 2.5 %collective-permute-start.9 = (f32[64,256]{1,0:T(8,128)S(1)}, f32[64,256]{1,0:T(8,128)S(1)}, u32[]{:S(2)}, u32[]{:S(2)}) collective-permute-start(f32[64,256]{1,0:T(8,128)S(1)} %reduce_sum.9), channel_id=1, source_target_pairs={{0,5},{1,0},{2,7},{3,2},{4,1},{5,4},{6,3},{7,6},{8,13},{9,8},{10,1... | collective-permute-start | bytes 196616 | tf_op jit(solution)/shard_map/ppermute | solution.py:43
  57.2 1.4 collective-permute-start.7
  58.7 3.6 %collective-permute-done.8 = f32[64,256]{1,0:T(8,128)S(1)} collective-permute-done((f32[64,256]{1,0:T(8,128)S(1)}, f32[64,256]{1,0:T(8,128)S(1)}, u32[]{:S(2)}, u32[]{:S(2)}) %collective-permute-start.8) | collective-permute-done | bytes 65568 | tf_op jit(solution)/shard_map/ppermute | solution.py:43
  63.4 8.9 %all-to-all-start.1 = ((f32[16,64,256]{2,1,0:T(8,128)}), f32[16,64,256]{2,1,0:T(8,128)S(1)}, u32[]{:S(2)}, u32[]{:S(2)}) async-start(f32[16,64,256]{2,1,0:T(8,128)} %broadcast_in_dim.17), calls=%async_computation.1 | async-start | bytes 2097152 | tf_op jit(solution)/shard_map/all_to_all | solution.py:569
  72.3 1.2 collective-permute-start.11
  74.3 13.3 %collective-permute-done.12.far_own = bf16[128,512]{1,0:T(8,128)(2,1)S(1)} collective-permute-done((bf16[128,512]{1,0:T(8,128)(2,1)S(1)}, bf16[128,512]{1,0:T(8,128)(2,1)S(1)}, u32[]{:S(2)}, u32[]{:S(2)}) %collective-permute-start.12) | collective-permute-done | bytes 131104 | tf_op jit(solution)/shard_map/ppermute | solution.py:43
  87.9 2.9 %collective-permute-start.13 = (f32[16,64,256]{2,1,0:T(8,128)S(1)}, f32[16,64,256]{2,1,0:T(8,128)S(1)}, u32[]{:S(2)}, u32[]{:S(2)}) collective-permute-start(f32[16,64,256]{2,1,0:T(8,128)S(1)} %all-to-all-done.1.mine), channel_id=1, source_target_pairs={{0,2},{1,3},{2,0},{3,1},{4,6},{5,7},{6,4},{7,5},{8,10},{9,11},{10,... | collective-permute-start | bytes 3145736 | tf_op jit(solution)/shard_map/ppermute | solution.py:43
  92.2 1.1 collective-permute-done.14.far_other
  94.3 8.3 %right_part.1 = (f32[32,512]{1,0:T(8,128)S(1)}, f32[32,512]{1,0:T(8,128)S(1)}, f32[64,64]{1,0:T(8,128)S(1)}) custom-call(s32[1]{0:T(128)} %bitcast.core_ref, f32[16,64,256]{2,1,0:T(8,128)} %copy-done.2, f32[16,64,256]{2,1,0:T(8,128)} %copy-done.4, bf16[8192,512]{1,0:T(8,128)(2,1)} %bitcast.8, bf16[128,512]{1,0:T(8,128)(2,1)} %get-tuple-element.77.after.masked_own.near_own, ...), custom_call_target="tpu_custom_call" | custom-call | flops 1024 | bytes 1024 | tf_op jit(solution)/shard_map/right_part/pallas_call | solution.py:89
  104.1 1.6 %collective-permute-start.18 = (f32[32,512]{1,0:T(8,128)S(1)}, f32[32,512]{1,0:T(8,128)S(1)}, u32[]{:S(2)}, u32[]{:S(2)}) collective-permute-start(f32[32,512]{1,0:T(8,128)S(1)} %add.40), channel_id=1, source_target_pairs={{0,24},{1,25},{2,26},{3,27},{4,28},{5,29},{6,30},{7,31},{8,0},{9,1... | collective-permute-start | bytes 196616 | tf_op jit(solution)/shard_map/ppermute | solution.py:43
  105.6 1.8 %collective-permute-start.16 = (f32[32,512]{1,0:T(8,128)S(1)}, f32[32,512]{1,0:T(8,128)S(1)}, u32[]{:S(2)}, u32[]{:S(2)}) collective-permute-start(f32[32,512]{1,0:T(8,128)S(1)} %add.40), channel_id=1, source_target_pairs={{0,16},{1,17},{2,18},{3,19},{4,20},{5,21},{6,22},{7,23},{8,24},{9,... | collective-permute-start | bytes 196616 | tf_op jit(solution)/shard_map/ppermute | solution.py:43
  107.4 7.0 %inverse_part.1.inverse = f32[64,64]{1,0:T(8,128)} custom-call(f32[64,64]{1,0:T(8,128)} %copy-done.1), custom_call_target="tpu_custom_call" | custom-call | flops 1024 | bytes 1024 | tf_op jit(solution)/shard_map/inverse_part/pallas_call | solution.py:357
  114.5 2.6 %collective-permute-done.19.refs_3_ = bf16[1024,512]{1,0:T(8,128)(2,1)} collective-permute-done((bf16[1024,512]{1,0:T(8,128)(2,1)}, bf16[1024,512]{1,0:T(8,128)(2,1)}, u32[]{:S(2)}, u32[]{:S(2)}) %collective-permute-start.19) | collective-permute-done | bytes 1048608 | tf_op jit(solution)/shard_map/ppermute | solution.py:43
  117.1 1.4 collective-permute-start.23
  118.6 1.7 %collective-permute-start.21 = (f32[32,512]{1,0:T(8,128)S(1)}, f32[32,512]{1,0:T(8,128)S(1)}, u32[]{:S(2)}, u32[]{:S(2)}) collective-permute-start(f32[32,512]{1,0:T(8,128)S(1)} %add_add_fusion.1), channel_id=1, source_target_pairs={{0,64},{1,65},{2,66},{3,67},{4,68},{5,69},{6,70},{7,71},{8,72},{9,... | collective-permute-start | bytes 196616 | tf_op jit(solution)/shard_map/ppermute | solution.py:43
  120.3 6.8 %input_part.1 = (bf16[128,8192]{1,0:T(8,128)(2,1)}, bf16[128,4096]{1,0:T(8,128)(2,1)S(1)}) custom-call(s32[1]{0:T(128)} %bitcast.core_ref, bf16[128,512]{1,0:T(8,128)(2,1)} %get-tuple-element.77.after.masked_own.near_own, bf16[128,512]{1,0:T(8,128)(2,1)} %copy-done.9, bf16[128,512]{1,0:T(8,128)(2,1)} %copy-done.10, bf16[128,512]{1,0:T(8,128)(2,1)} %copy-done.11, ...), custom_call_target="tpu_custom_call" | custom-call | flops 1024 | bytes 1024 | tf_op jit(solution)/shard_map/input_part/pallas_call | solution.py:89
  127.2 1.8 %collective-permute-start.26 = (bf16[128,4096]{1,0:T(8,128)(2,1)S(1)}, bf16[128,4096]{1,0:T(8,128)(2,1)S(1)}, u32[]{:S(2)}, u32[]{:S(2)}) collective-permute-start(bf16[128,4096]{1,0:T(8,128)(2,1)S(1)} %get-tuple-element.114), channel_id=1, source_target_pairs={{0,2},{1,3},{2,0},{3,1},{4,6},{5,7},{6,4},{7,5},{8,10},{9,11},{10,... | collective-permute-start | bytes 3145736 | tf_op jit(solution)/shard_map/ppermute | solution.py:43
  128.9 1.7 %collective-permute-start.24 = (f32[32,512]{1,0:T(8,128)S(1)}, f32[32,512]{1,0:T(8,128)S(1)}, u32[]{:S(2)}, u32[]{:S(2)}) collective-permute-start(f32[32,512]{1,0:T(8,128)S(1)} %add_add_fusion), channel_id=1, source_target_pairs={{0,4},{1,5},{2,6},{3,7},{4,0},{5,1},{6,2},{7,3},{8,12},{9,13},{10,... | collective-permute-start | bytes 196616 | tf_op jit(solution)/shard_map/ppermute | solution.py:43
  130.7 3.4 %collective-permute-done.24 = f32[32,512]{1,0:T(8,128)S(1)} collective-permute-done((f32[32,512]{1,0:T(8,128)S(1)}, f32[32,512]{1,0:T(8,128)S(1)}, u32[]{:S(2)}, u32[]{:S(2)}) %collective-permute-start.24) | collective-permute-done | bytes 65568 | tf_op jit(solution)/shard_map/ppermute | solution.py:43
  134.1 1.2 collective-permute-start.25
  136.2 13.5 %final_part.1 = (bf16[8192,512]{1,0:T(8,128)(2,1)}, bf16[8192,512]{1,0:T(8,128)(2,1)}, f32[64,512]{1,0:T(8,128)}, bf16[128,8192]{1,0:T(8,128)(2,1)}) custom-call(s32[1]{0:T(128)} %bitcast.core_ref, bf16[128,512]{1,0:T(8,128)(2,1)} %get-tuple-element.77.after.masked_own.near_own, ...), custom_call_target="tpu_custom_call", output_to_operand_aliasing={{3}: (7, {})} | custom-call | flops 1024 | bytes 1024 | tf_op jit(solution)/shard_map/final_part/pallas_call | solution.py:89
  (67 shorter events, 10.0 us)
Async XLA Ops:
  3.0 7.6 %collective-permute-start = (f32[64,128]{1,0:T(8,128)}, f32[64,128]{1,0:T(8,128)S(1)}, u32[]{:S(2)}, u32[]{:S(2)}) collective-permute-start(f32[64,128]{1,0:T(8,128)} %get-tuple-element.64), channel_id=1, source_target_pairs={{0,1},{1,0},{2,3},{3,2},{4,5},{5,4},{6,7},{7,6},{8,9},{9,8},{10,11... | collective-permute-start | bytes 98312 | tf_op jit(solution)/shard_map/ppermute | solution.py:43
  10.5 13.1 %collective-permute-start.1 = (bf16[32,8192]{1,0:T(8,128)(2,1)}, bf16[32,8192]{1,0:T(8,128)(2,1)S(1)}, u32[]{:S(2)}, u32[]{:S(2)}) collective-permute-start(bf16[32,8192]{1,0:T(8,128)(2,1)} %get-tuple-element.71), channel_id=1, source_target_pairs={{0,1},{1,0},{2,3},{3,2},{4,5},{5,4},{6,7},{7,6},{8,9},{9,8},{10,11... | collective-permute-start | bytes 1572872 | tf_op jit(solution)/shard_map/ppermute | solution.py:43
  10.6 13.6 %collective-permute-start.2 = (bf16[512,512]{1,0:T(8,128)(2,1)}, bf16[512,512]{1,0:T(8,128)(2,1)S(1)}, u32[]{:S(2)}, u32[]{:S(2)}) collective-permute-start(bf16[512,512]{1,0:T(8,128)(2,1)} %get-tuple-element.72), channel_id=1, source_target_pairs={{0,5},{1,4},{2,7},{3,6},{4,1},{5,0},{6,3},{7,2},{8,13},{9,12},{10,... | collective-permute-start | bytes 1572872 | tf_op jit(solution)/shard_map/ppermute | solution.py:43
  13.4 60.2 %copy-start.7 = (bf16[128,512]{1,0:T(8,128)(2,1)S(1)}, bf16[128,512]{1,0:T(8,128)(2,1)}, u32[]{:S(2)}) copy-start(bf16[128,512]{1,0:T(8,128)(2,1)} %get-tuple-element.86.masked_other) | copy-start | bytes 393220
  23.6 69.7 %copy-start.6 = (bf16[32,8192]{1,0:T(8,128)(2,1)}, bf16[32,8192]{1,0:T(8,128)(2,1)S(1)}, u32[]{:S(2)}) copy-start(bf16[32,8192]{1,0:T(8,128)(2,1)S(1)} %collective-permute-done.1.refs_1_) | copy-start | bytes 1572868
  24.2 4.9 %collective-permute-start.5 = (f32[16,64,256]{2,1,0:T(8,128)S(1)}, f32[16,64,256]{2,1,0:T(8,128)S(1)}, u32[]{:S(2)}, u32[]{:S(2)}) collective-permute-start(f32[16,64,256]{2,1,0:T(8,128)S(1)} %get-tuple-element.79), channel_id=1, source_target_pairs={{0,2},{1,3},{2,0},{3,1},{4,6},{5,7},{6,4},{7,5},{8,10},{9,11},{10,... | collective-permute-start | bytes 3145736 | tf_op jit(solution)/shard_map/ppermute | solution.py:43
  26.5 25.1 %collective-permute-start.3 = (bf16[64,8192]{1,0:T(8,128)(2,1)}, bf16[64,8192]{1,0:T(8,128)(2,1)S(1)}, u32[]{:S(2)}, u32[]{:S(2)}) collective-permute-start(bf16[64,8192]{1,0:T(8,128)(2,1)} %get-tuple-element.75), channel_id=1, source_target_pairs={{0,1},{1,0},{2,3},{3,2},{4,5},{5,4},{6,7},{7,6},{8,9},{9,8},{10,11... | collective-permute-start | bytes 3145736 | tf_op jit(solution)/shard_map/ppermute | solution.py:43
  26.6 26.0 %collective-permute-start.4 = (bf16[1024,512]{1,0:T(8,128)(2,1)}, bf16[1024,512]{1,0:T(8,128)(2,1)}, u32[]{:S(2)}, u32[]{:S(2)}) collective-permute-start(bf16[1024,512]{1,0:T(8,128)(2,1)} %get-tuple-element.76), channel_id=1, source_target_pairs={{0,5},{1,4},{2,7},{3,6},{4,1},{5,0},{6,3},{7,2},{8,13},{9,12},{10,... | collective-permute-start | bytes 3145736 | tf_op jit(solution)/shard_map/ppermute | solution.py:43
  30.3 24.1 %all-to-all-start = ((f32[16,64,256]{2,1,0:T(8,128)}), f32[16,64,256]{2,1,0:T(8,128)S(1)}, u32[]{:S(2)}, u32[]{:S(2)}) async-start(f32[16,64,256]{2,1,0:T(8,128)} %add.36), calls=%async_computation | async-start | bytes 2097152 | tf_op jit(solution)/shard_map/all_to_all | solution.py:558
  52.6 2.1 %collective-permute-start.6 = (bf16[128,512]{1,0:T(8,128)(2,1)S(1)}, bf16[128,512]{1,0:T(8,128)(2,1)S(1)}, u32[]{:S(2)}, u32[]{:S(2)}) collective-permute-start(bf16[128,512]{1,0:T(8,128)(2,1)S(1)} %copy-done.5), channel_id=1, source_target_pairs={{0,2},{1,3},{2,0},{3,1},{4,6},{5,7},{6,4},{7,5},{8,10},{9,11},{10,... | collective-permute-start | bytes 393224 | tf_op jit(solution)/shard_map/ppermute | solution.py:43
  54.7 47.9 %copy-start.9 = (bf16[128,512]{1,0:T(8,128)(2,1)}, bf16[128,512]{1,0:T(8,128)(2,1)S(1)}, u32[]{:S(2)}) copy-start(bf16[128,512]{1,0:T(8,128)(2,1)S(1)} %collective-permute-done.6.near_other) | copy-start | bytes 393220
  54.7 3.9 %collective-permute-start.9 = (f32[64,256]{1,0:T(8,128)S(1)}, f32[64,256]{1,0:T(8,128)S(1)}, u32[]{:S(2)}, u32[]{:S(2)}) collective-permute-start(f32[64,256]{1,0:T(8,128)S(1)} %reduce_sum.9), channel_id=1, source_target_pairs={{0,5},{1,0},{2,7},{3,2},{4,1},{5,4},{6,3},{7,6},{8,13},{9,8},{10,1... | collective-permute-start | bytes 196616 | tf_op jit(solution)/shard_map/ppermute | solution.py:43
  57.2 5.0 %collective-permute-start.8 = (f32[64,256]{1,0:T(8,128)S(1)}, f32[64,256]{1,0:T(8,128)S(1)}, u32[]{:S(2)}, u32[]{:S(2)}) collective-permute-start(f32[64,256]{1,0:T(8,128)S(1)} %reduce_sum.9), channel_id=1, source_target_pairs={{0,1},{1,4},{2,3},{3,6},{4,5},{5,0},{6,7},{7,2},{8,9},{9,12},{10,1... | collective-permute-start | bytes 196616 | tf_op jit(solution)/shard_map/ppermute | solution.py:43
  57.2 5.0 %collective-permute-start.7 = (f32[64,256]{1,0:T(8,128)S(1)}, f32[64,256]{1,0:T(8,128)S(1)}, u32[]{:S(2)}, u32[]{:S(2)}) collective-permute-start(f32[64,256]{1,0:T(8,128)S(1)} %reduce_sum.9), channel_id=1, source_target_pairs={{0,4},{1,5},{2,6},{3,7},{4,0},{5,1},{6,2},{7,3},{8,12},{9,13},{10,... | collective-permute-start | bytes 196616 | tf_op jit(solution)/shard_map/ppermute | solution.py:43
  63.4 24.6 %all-to-all-start.1 = ((f32[16,64,256]{2,1,0:T(8,128)}), f32[16,64,256]{2,1,0:T(8,128)S(1)}, u32[]{:S(2)}, u32[]{:S(2)}) async-start(f32[16,64,256]{2,1,0:T(8,128)} %broadcast_in_dim.17), calls=%async_computation.1 | async-start | bytes 2097152 | tf_op jit(solution)/shard_map/all_to_all | solution.py:569
  72.2 15.4 %collective-permute-start.10 = (bf16[32,8192]{1,0:T(8,128)(2,1)}, bf16[32,8192]{1,0:T(8,128)(2,1)S(1)}, u32[]{:S(2)}, u32[]{:S(2)}) collective-permute-start(bf16[32,8192]{1,0:T(8,128)(2,1)} %get-tuple-element.88), channel_id=1, source_target_pairs={{0,1},{1,0},{2,3},{3,2},{4,5},{5,4},{6,7},{7,6},{8,9},{9,8},{10,11... | collective-permute-start | bytes 1572872 | tf_op jit(solution)/shard_map/ppermute | solution.py:43
  72.3 15.3 %collective-permute-start.11 = (bf16[512,512]{1,0:T(8,128)(2,1)}, bf16[512,512]{1,0:T(8,128)(2,1)}, u32[]{:S(2)}, u32[]{:S(2)}) collective-permute-start(bf16[512,512]{1,0:T(8,128)(2,1)} %get-tuple-element.89), channel_id=1, source_target_pairs={{0,5},{1,4},{2,7},{3,6},{4,1},{5,0},{6,3},{7,2},{8,13},{9,12},{10,... | collective-permute-start | bytes 1572872 | tf_op jit(solution)/shard_map/ppermute | solution.py:43
  73.6 14.0 %collective-permute-start.12 = (bf16[128,512]{1,0:T(8,128)(2,1)S(1)}, bf16[128,512]{1,0:T(8,128)(2,1)S(1)}, u32[]{:S(2)}, u32[]{:S(2)}) collective-permute-start(bf16[128,512]{1,0:T(8,128)(2,1)S(1)} %copy-done.7), channel_id=1, source_target_pairs={{0,1},{1,0},{2,3},{3,2},{4,5},{5,4},{6,7},{7,6},{8,9},{9,8},{10,11... | collective-permute-start | bytes 393224 | tf_op jit(solution)/shard_map/ppermute | solution.py:43
  87.9 5.4 %collective-permute-start.13 = (f32[16,64,256]{2,1,0:T(8,128)S(1)}, f32[16,64,256]{2,1,0:T(8,128)S(1)}, u32[]{:S(2)}, u32[]{:S(2)}) collective-permute-start(f32[16,64,256]{2,1,0:T(8,128)S(1)} %all-to-all-done.1.mine), channel_id=1, source_target_pairs={{0,2},{1,3},{2,0},{3,1},{4,6},{5,7},{6,4},{7,5},{8,10},{9,11},{10,... | collective-permute-start | bytes 3145736 | tf_op jit(solution)/shard_map/ppermute | solution.py:43
  90.8 26.3 %collective-permute-start.19 = (bf16[1024,512]{1,0:T(8,128)(2,1)}, bf16[1024,512]{1,0:T(8,128)(2,1)}, u32[]{:S(2)}, u32[]{:S(2)}) collective-permute-start(bf16[1024,512]{1,0:T(8,128)(2,1)} %get-tuple-element.101), channel_id=1, source_target_pairs={{0,5},{1,4},{2,7},{3,6},{4,1},{5,0},{6,3},{7,2},{8,13},{9,12},{10,... | collective-permute-start | bytes 3145736 | tf_op jit(solution)/shard_map/ppermute | solution.py:43
  91.9 25.2 %collective-permute-start.20 = (bf16[1024,512]{1,0:T(8,128)(2,1)}, bf16[1024,512]{1,0:T(8,128)(2,1)}, u32[]{:S(2)}, u32[]{:S(2)}) collective-permute-start(bf16[1024,512]{1,0:T(8,128)(2,1)} %get-tuple-element.102), channel_id=1, source_target_pairs={{0,1},{1,0},{2,3},{3,2},{4,5},{5,4},{6,7},{7,6},{8,9},{9,8},{10,11... | collective-permute-start | bytes 3145736 | tf_op jit(solution)/shard_map/ppermute | solution.py:43
  91.9 1.4 collective-permute-start.14
  102.7 1.4 collective-permute-start.15
  104.1 10.4 %collective-permute-start.18 = (f32[32,512]{1,0:T(8,128)S(1)}, f32[32,512]{1,0:T(8,128)S(1)}, u32[]{:S(2)}, u32[]{:S(2)}) collective-permute-start(f32[32,512]{1,0:T(8,128)S(1)} %add.40), channel_id=1, source_target_pairs={{0,24},{1,25},{2,26},{3,27},{4,28},{5,29},{6,30},{7,31},{8,0},{9,1... | collective-permute-start | bytes 196616 | tf_op jit(solution)/shard_map/ppermute | solution.py:43
  105.6 8.8 %collective-permute-start.17 = (f32[32,512]{1,0:T(8,128)S(1)}, f32[32,512]{1,0:T(8,128)S(1)}, u32[]{:S(2)}, u32[]{:S(2)}) collective-permute-start(f32[32,512]{1,0:T(8,128)S(1)} %add.40), channel_id=1, source_target_pairs={{0,8},{1,9},{2,10},{3,11},{4,12},{5,13},{6,14},{7,15},{8,16},{9,17... | collective-permute-start | bytes 196616 | tf_op jit(solution)/shard_map/ppermute | solution.py:43
  105.6 8.8 %collective-permute-start.16 = (f32[32,512]{1,0:T(8,128)S(1)}, f32[32,512]{1,0:T(8,128)S(1)}, u32[]{:S(2)}, u32[]{:S(2)}) collective-permute-start(f32[32,512]{1,0:T(8,128)S(1)} %add.40), channel_id=1, source_target_pairs={{0,16},{1,17},{2,18},{3,19},{4,20},{5,21},{6,22},{7,23},{8,24},{9,... | collective-permute-start | bytes 196616 | tf_op jit(solution)/shard_map/ppermute | solution.py:43
  117.1 10.0 %collective-permute-start.23 = (f32[32,512]{1,0:T(8,128)S(1)}, f32[32,512]{1,0:T(8,128)S(1)}, u32[]{:S(2)}, u32[]{:S(2)}) collective-permute-start(f32[32,512]{1,0:T(8,128)S(1)} %add_add_fusion.1), channel_id=1, source_target_pairs={{0,96},{1,97},{2,98},{3,99},{4,100},{5,101},{6,102},{7,103},{8,104... | collective-permute-start | bytes 196616 | tf_op jit(solution)/shard_map/ppermute | solution.py:43
  118.6 8.6 %collective-permute-start.22 = (f32[32,512]{1,0:T(8,128)S(1)}, f32[32,512]{1,0:T(8,128)S(1)}, u32[]{:S(2)}, u32[]{:S(2)}) collective-permute-start(f32[32,512]{1,0:T(8,128)S(1)} %add_add_fusion.1), channel_id=1, source_target_pairs={{0,32},{1,33},{2,34},{3,35},{4,36},{5,37},{6,38},{7,39},{8,40},{9,... | collective-permute-start | bytes 196616 | tf_op jit(solution)/shard_map/ppermute | solution.py:43
  118.6 8.5 %collective-permute-start.21 = (f32[32,512]{1,0:T(8,128)S(1)}, f32[32,512]{1,0:T(8,128)S(1)}, u32[]{:S(2)}, u32[]{:S(2)}) collective-permute-start(f32[32,512]{1,0:T(8,128)S(1)} %add_add_fusion.1), channel_id=1, source_target_pairs={{0,64},{1,65},{2,66},{3,67},{4,68},{5,69},{6,70},{7,71},{8,72},{9,... | collective-permute-start | bytes 196616 | tf_op jit(solution)/shard_map/ppermute | solution.py:43
  127.2 9.0 %collective-permute-start.26 = (bf16[128,4096]{1,0:T(8,128)(2,1)S(1)}, bf16[128,4096]{1,0:T(8,128)(2,1)S(1)}, u32[]{:S(2)}, u32[]{:S(2)}) collective-permute-start(bf16[128,4096]{1,0:T(8,128)(2,1)S(1)} %get-tuple-element.114), channel_id=1, source_target_pairs={{0,2},{1,3},{2,0},{3,1},{4,6},{5,7},{6,4},{7,5},{8,10},{9,11},{10,... | collective-permute-start | bytes 3145736 | tf_op jit(solution)/shard_map/ppermute | solution.py:43
  128.9 5.2 %collective-permute-start.24 = (f32[32,512]{1,0:T(8,128)S(1)}, f32[32,512]{1,0:T(8,128)S(1)}, u32[]{:S(2)}, u32[]{:S(2)}) collective-permute-start(f32[32,512]{1,0:T(8,128)S(1)} %add_add_fusion), channel_id=1, source_target_pairs={{0,4},{1,5},{2,6},{3,7},{4,0},{5,1},{6,2},{7,3},{8,12},{9,13},{10,... | collective-permute-start | bytes 196616 | tf_op jit(solution)/shard_map/ppermute | solution.py:43
  134.1 2.1 %collective-permute-start.25 = (f32[32,512]{1,0:T(8,128)S(1)}, f32[32,512]{1,0:T(8,128)S(1)}, u32[]{:S(2)}, u32[]{:S(2)}) collective-permute-start(f32[32,512]{1,0:T(8,128)S(1)} %add.47.total), channel_id=1, source_target_pairs={{0,2},{1,3},{2,0},{3,1},{4,6},{5,7},{6,4},{7,5},{8,10},{9,11},{10,... | collective-permute-start | bytes 196616 | tf_op jit(solution)/shard_map/ppermute | solution.py:43
  (10 other events, 180.8 us)

commit v5 on v4

--- a/solution.py
+++ b/solution.py
@@ -199,7 +199,7 @@
         if kind == "hidden":
             source = hidden.at[pl.ds(first, rows), :]
         else:
-            source = key_weight.at[pl.ds(pl.multiple_of(core_ref[0] * 4096 + first, 64), rows), :]
+            source = key_weight.at[pl.ds(pl.multiple_of(core_ref[0] * 4096 + first, 32), rows), :]
         picks.append(pltpu.make_async_copy(source, v_parcels[k], sems.at[0, k]))
         drops.append(pltpu.make_async_copy(v_parcels[k], parcels[k], sems.at[1, k]))
     start(picks)
@@ -537,7 +537,7 @@
 
     lots = [("hidden", 0, 32), ("hidden", 32, 64), ("hidden", 96, 32)]
     first = 0
-    for rows in (512, 1024, 512, 1024, 1024):
+    for rows in (512, 1024, 544, 992, 1024):
         lots.append(("weight", first, rows))
         first += rows
     parcels = parcel_part(core_arg, masked_own, hidden_rows, key_weight, lots)

time: 150 us -> 151 us (level)
  starting transfers between devices: 49.5 us -> 53.5 us
  waiting for transfers between devices: 42.3 us -> 39 us
    ppermute x27, starting transfers between devices: 32.9 us -> 36.9 us  [send(): return lax.ppermute(array, AXES, pairs)]
    ppermute x27, waiting for transfers between devices: 41.4 us -> 37.8 us  [send(): return lax.ppermute(array, AXES, pairs)]
  transfers between devices with their start and end apart: 29 -> 29, of which waited for: 13 -> 12; matrix products, arithmetic and copies ran while one was open for 1% -> 1% of each run, Pallas kernels for 25% -> 25%
where the time goes in v5:
time: 151 us
  Pallas kernels  53.7 us (36%)
  starting transfers between devices  53.5 us (35%)
  waiting for transfers between devices  39 us (26%)
  local copies, waits for them, and re-layouts  2.11 us (1%)
    pallas_call x6, Pallas kernels, call(): pl.pallas_call(kernel, out_shape=[(pltpu.HBM if hbm else jax.ShapeDtypeSt...  46.6 us
    ppermute x27, waiting for transfers between devices, send(): return lax.ppermute(array, AXES, pairs)  37.8 us
    ppermute x27, starting transfers between devices, send(): return lax.ppermute(array, AXES, pairs)  36.9 us
    all_to_all x1, starting transfers between devices, local(): lax.all_to_all(jnp.broadcast_to(piece[None], (16, 64, 256)), ('z', 'y'),...  8.89 us
    all_to_all x1, starting transfers between devices, local(): piece = lax.all_to_all(piece, ('z', 'y'), 0, 0, tiled=True)  7.77 us
    pallas_call x1, Pallas kernels, inverse_part(): pl.pallas_call(inverse_kernel, out_shape=jax.ShapeDtypeStruct((64, 64), F...  7.03 us
  transfers between devices with their start and end apart: 29, of which 12 were waited for; matrix products, arithmetic and copies ran while one was open for 1% of the time, Pallas kernels for 25%

profile of v5, /device:TPU:1, one launch (start us, length us, event | category | flops | bytes accessed | tf_op | source)
XLA Modules:
  0.0 150.6 jit_solution(12430015133363463304)
XLA Ops:
  0.6 2.3 %token_part.1 = (bf16[128,512]{1,0:T(8,128)(2,1)}, bf16[128,512]{1,0:T(8,128)(2,1)}, f32[64,128]{1,0:T(8,128)}, f32[64,128]{1,0:T(8,128)}, bf16[192,512]{1,0:T(8,128)(2,1)}) custom-call(s32[1]{0:T(128)} %bitcast.2.xl_ref, bf16[256,512]{1,0:T(8,128)(2,1)} %grads.1, s32[1,256]{1,0:T(1,128)} %bitcast.11, f32[64,512]{1,0:T(8,128)} %bitcast.10), custom_call_target="tpu_custom_call" | custom-call | flops 1024 | bytes 1024 | tf_op jit(solution)/shard_map/token_part/pallas_call | solution.py:89
  3.0 2.1 %collective-permute-start = (f32[64,128]{1,0:T(8,128)}, f32[64,128]{1,0:T(8,128)S(1)}, u32[]{:S(2)}, u32[]{:S(2)}) collective-permute-start(f32[64,128]{1,0:T(8,128)} %get-tuple-element.64), channel_id=1, source_target_pairs={{0,1},{1,0},{2,3},{3,2},{4,5},{5,4},{6,7},{7,6},{8,9},{9,8},{10,11... | collective-permute-start | bytes 98312 | tf_op jit(solution)/shard_map/ppermute | solution.py:43
  5.1 5.5 %parcel_part.1 = (bf16[32,8192]{1,0:T(8,128)(2,1)}, bf16[64,8192]{1,0:T(8,128)(2,1)}, bf16[32,8192]{1,0:T(8,128)(2,1)}, bf16[512,512]{1,0:T(8,128)(2,1)}, bf16[1...) custom-call(s32[1]{0:T(128)} %bitcast.core_ref, ...), custom_call_target="tpu_custom_call" | custom-call | flops 1024 | bytes 1024 | tf_op jit(solution)/shard_map/parcel_part/pallas_call | solution.py:89
  10.7 2.7 %collective-permute-start.2 = (bf16[512,512]{1,0:T(8,128)(2,1)}, bf16[512,512]{1,0:T(8,128)(2,1)S(1)}, u32[]{:S(2)}, u32[]{:S(2)}) collective-permute-start(bf16[512,512]{1,0:T(8,128)(2,1)} %get-tuple-element.72), channel_id=1, source_target_pairs={{0,5},{1,4},{2,7},{3,6},{4,1},{5,0},{6,3},{7,2},{8,13},{9,12},{10,... | collective-permute-start | bytes 1572872 | tf_op jit(solution)/shard_map/ppermute | solution.py:43
  13.4 10.2 %left_part.1 = (f32[16,64,256]{2,1,0:T(8,128)S(1)}, f32[16,64,256]{2,1,0:T(8,128)S(1)}) custom-call(s32[1]{0:T(128)} %bitcast.core_ref, bf16[8192,512]{1,0:T(8,128)(2,1)} %bitcast.7, bf16[128,8192]{1,0:T(8,128)(2,1)} %refs_0_.3, bf16[192,512]{1,0:T(8,128)(2,1)} %get-tuple-element.62.terms_t, f32[64,128]{1,0:T(8,128)} %get-tuple-element.63.tok_own, ...), custom_call_target="tpu_custom_call" | custom-call | flops 1024 | bytes 1024 | tf_op jit(solution)/shard_map/left_part/pallas_call | solution.py:89
  24.3 2.2 %collective-permute-start.5 = (f32[16,64,256]{2,1,0:T(8,128)S(1)}, f32[16,64,256]{2,1,0:T(8,128)S(1)}, u32[]{:S(2)}, u32[]{:S(2)}) collective-permute-start(f32[16,64,256]{2,1,0:T(8,128)S(1)} %get-tuple-element.79), channel_id=1, source_target_pairs={{0,2},{1,3},{2,0},{3,1},{4,6},{5,7},{6,4},{7,5},{8,10},{9,11},{10,... | collective-permute-start | bytes 3145736 | tf_op jit(solution)/shard_map/ppermute | solution.py:43
  26.7 2.5 %collective-permute-start.4 = (bf16[1024,512]{1,0:T(8,128)(2,1)}, bf16[1024,512]{1,0:T(8,128)(2,1)}, u32[]{:S(2)}, u32[]{:S(2)}) collective-permute-start(bf16[1024,512]{1,0:T(8,128)(2,1)} %get-tuple-element.76), channel_id=1, source_target_pairs={{0,5},{1,4},{2,7},{3,6},{4,1},{5,0},{6,3},{7,2},{8,13},{9,12},{10,... | collective-permute-start | bytes 3145736 | tf_op jit(solution)/shard_map/ppermute | solution.py:43
  29.2 1.1 add.36
  30.3 7.8 %all-to-all-start = ((f32[16,64,256]{2,1,0:T(8,128)}), f32[16,64,256]{2,1,0:T(8,128)S(1)}, u32[]{:S(2)}, u32[]{:S(2)}) async-start(f32[16,64,256]{2,1,0:T(8,128)} %add.36), calls=%async_computation | async-start | bytes 2097152 | tf_op jit(solution)/shard_map/all_to_all | solution.py:558
  38.1 13.6 %collective-permute-done.3.refs_2_ = bf16[64,8192]{1,0:T(8,128)(2,1)S(1)} collective-permute-done((bf16[64,8192]{1,0:T(8,128)(2,1)}, bf16[64,8192]{1,0:T(8,128)(2,1)S(1)}, u32[]{:S(2)}, u32[]{:S(2)}) %collective-permute-start.3) | collective-permute-done | bytes 1048608 | tf_op jit(solution)/shard_map/ppermute | solution.py:43
  52.7 1.1 collective-permute-start.6
  54.8 2.5 %collective-permute-start.9 = (f32[64,256]{1,0:T(8,128)S(1)}, f32[64,256]{1,0:T(8,128)S(1)}, u32[]{:S(2)}, u32[]{:S(2)}) collective-permute-start(f32[64,256]{1,0:T(8,128)S(1)} %reduce_sum.9), channel_id=1, source_target_pairs={{0,5},{1,0},{2,7},{3,2},{4,1},{5,4},{6,3},{7,6},{8,13},{9,8},{10,1... | collective-permute-start | bytes 196616 | tf_op jit(solution)/shard_map/ppermute | solution.py:43
  57.3 1.4 collective-permute-start.7
  58.7 3.6 %collective-permute-done.8 = f32[64,256]{1,0:T(8,128)S(1)} collective-permute-done((f32[64,256]{1,0:T(8,128)S(1)}, f32[64,256]{1,0:T(8,128)S(1)}, u32[]{:S(2)}, u32[]{:S(2)}) %collective-permute-start.8) | collective-permute-done | bytes 65568 | tf_op jit(solution)/shard_map/ppermute | solution.py:43
  63.4 8.9 %all-to-all-start.1 = ((f32[16,64,256]{2,1,0:T(8,128)}), f32[16,64,256]{2,1,0:T(8,128)S(1)}, u32[]{:S(2)}, u32[]{:S(2)}) async-start(f32[16,64,256]{2,1,0:T(8,128)} %broadcast_in_dim.17), calls=%async_computation.1 | async-start | bytes 2097152 | tf_op jit(solution)/shard_map/all_to_all | solution.py:569
  72.3 1.2 collective-permute-start.11
  73.5 1.5 collective-permute-start.12
  75.0 12.4 %collective-permute-done.12.far_own = bf16[128,512]{1,0:T(8,128)(2,1)S(1)} collective-permute-done((bf16[128,512]{1,0:T(8,128)(2,1)S(1)}, bf16[128,512]{1,0:T(8,128)(2,1)S(1)}, u32[]{:S(2)}, u32[]{:S(2)}) %collective-permute-start.12) | collective-permute-done | bytes 131104 | tf_op jit(solution)/shard_map/ppermute | solution.py:43
  88.0 3.0 %collective-permute-start.13 = (f32[16,64,256]{2,1,0:T(8,128)S(1)}, f32[16,64,256]{2,1,0:T(8,128)S(1)}, u32[]{:S(2)}, u32[]{:S(2)}) collective-permute-start(f32[16,64,256]{2,1,0:T(8,128)S(1)} %all-to-all-done.1.mine), channel_id=1, source_target_pairs={{0,2},{1,3},{2,0},{3,1},{4,6},{5,7},{6,4},{7,5},{8,10},{9,11},{10,... | collective-permute-start | bytes 3145736 | tf_op jit(solution)/shard_map/ppermute | solution.py:43
  91.0 1.5 %collective-permute-start.19 = (bf16[992,512]{1,0:T(8,128)(2,1)}, bf16[992,512]{1,0:T(8,128)(2,1)}, u32[]{:S(2)}, u32[]{:S(2)}) collective-permute-start(bf16[992,512]{1,0:T(8,128)(2,1)} %get-tuple-element.101), channel_id=1, source_target_pairs={{0,5},{1,4},{2,7},{3,6},{4,1},{5,0},{6,3},{7,2},{8,13},{9,12},{10,... | collective-permute-start | bytes 3047432 | tf_op jit(solution)/shard_map/ppermute | solution.py:43
  95.2 8.3 %right_part.1 = (f32[32,512]{1,0:T(8,128)S(1)}, f32[32,512]{1,0:T(8,128)S(1)}, f32[64,64]{1,0:T(8,128)S(1)}) custom-call(s32[1]{0:T(128)} %bitcast.core_ref, f32[16,64,256]{2,1,0:T(8,128)} %copy-done.2, f32[16,64,256]{2,1,0:T(8,128)} %copy-done.4, bf16[8192,512]{1,0:T(8,128)(2,1)} %bitcast.8, bf16[128,512]{1,0:T(8,128)(2,1)} %get-tuple-element.77.after.masked_own.near_own, ...), custom_call_target="tpu_custom_call" | custom-call | flops 1024 | bytes 1024 | tf_op jit(solution)/shard_map/right_part/pallas_call | solution.py:89
  104.9 2.6 %collective-permute-start.18 = (f32[32,512]{1,0:T(8,128)S(1)}, f32[32,512]{1,0:T(8,128)S(1)}, u32[]{:S(2)}, u32[]{:S(2)}) collective-permute-start(f32[32,512]{1,0:T(8,128)S(1)} %add.40), channel_id=1, source_target_pairs={{0,24},{1,25},{2,26},{3,27},{4,28},{5,29},{6,30},{7,31},{8,0},{9,1... | collective-permute-start | bytes 196616 | tf_op jit(solution)/shard_map/ppermute | solution.py:43
  107.5 1.8 %collective-permute-start.16 = (f32[32,512]{1,0:T(8,128)S(1)}, f32[32,512]{1,0:T(8,128)S(1)}, u32[]{:S(2)}, u32[]{:S(2)}) collective-permute-start(f32[32,512]{1,0:T(8,128)S(1)} %add.40), channel_id=1, source_target_pairs={{0,16},{1,17},{2,18},{3,19},{4,20},{5,21},{6,22},{7,23},{8,24},{9,... | collective-permute-start | bytes 196616 | tf_op jit(solution)/shard_map/ppermute | solution.py:43
  109.2 7.0 %inverse_part.1.inverse = f32[64,64]{1,0:T(8,128)} custom-call(f32[64,64]{1,0:T(8,128)} %copy-done.1), custom_call_target="tpu_custom_call" | custom-call | flops 1024 | bytes 1024 | tf_op jit(solution)/shard_map/inverse_part/pallas_call | solution.py:357
  116.3 2.5 %collective-permute-start.23 = (f32[32,512]{1,0:T(8,128)S(1)}, f32[32,512]{1,0:T(8,128)S(1)}, u32[]{:S(2)}, u32[]{:S(2)}) collective-permute-start(f32[32,512]{1,0:T(8,128)S(1)} %add_add_fusion.1), channel_id=1, source_target_pairs={{0,96},{1,97},{2,98},{3,99},{4,100},{5,101},{6,102},{7,103},{8,104... | collective-permute-start | bytes 196616 | tf_op jit(solution)/shard_map/ppermute | solution.py:43
  118.8 1.8 %collective-permute-start.21 = (f32[32,512]{1,0:T(8,128)S(1)}, f32[32,512]{1,0:T(8,128)S(1)}, u32[]{:S(2)}, u32[]{:S(2)}) collective-permute-start(f32[32,512]{1,0:T(8,128)S(1)} %add_add_fusion.1), channel_id=1, source_target_pairs={{0,64},{1,65},{2,66},{3,67},{4,68},{5,69},{6,70},{7,71},{8,72},{9,... | collective-permute-start | bytes 196616 | tf_op jit(solution)/shard_map/ppermute | solution.py:43
  120.6 6.8 %input_part.1 = (bf16[128,8192]{1,0:T(8,128)(2,1)}, bf16[128,4096]{1,0:T(8,128)(2,1)S(1)}) custom-call(s32[1]{0:T(128)} %bitcast.core_ref, bf16[128,512]{1,0:T(8,128)(2,1)} %get-tuple-element.77.after.masked_own.near_own, bf16[128,512]{1,0:T(8,128)(2,1)} %copy-done.9, bf16[128,512]{1,0:T(8,128)(2,1)} %copy-done.10, bf16[128,512]{1,0:T(8,128)(2,1)} %copy-done.11, ...), custom_call_target="tpu_custom_call" | custom-call | flops 1024 | bytes 1024 | tf_op jit(solution)/shard_map/input_part/pallas_call | solution.py:89
  127.4 2.2 %collective-permute-start.26 = (bf16[128,4096]{1,0:T(8,128)(2,1)S(1)}, bf16[128,4096]{1,0:T(8,128)(2,1)S(1)}, u32[]{:S(2)}, u32[]{:S(2)}) collective-permute-start(bf16[128,4096]{1,0:T(8,128)(2,1)S(1)} %get-tuple-element.114), channel_id=1, source_target_pairs={{0,2},{1,3},{2,0},{3,1},{4,6},{5,7},{6,4},{7,5},{8,10},{9,11},{10,... | collective-permute-start | bytes 3145736 | tf_op jit(solution)/shard_map/ppermute | solution.py:43
  129.6 1.7 %collective-permute-start.24 = (f32[32,512]{1,0:T(8,128)S(1)}, f32[32,512]{1,0:T(8,128)S(1)}, u32[]{:S(2)}, u32[]{:S(2)}) collective-permute-start(f32[32,512]{1,0:T(8,128)S(1)} %add_add_fusion), channel_id=1, source_target_pairs={{0,4},{1,5},{2,6},{3,7},{4,0},{5,1},{6,2},{7,3},{8,12},{9,13},{10,... | collective-permute-start | bytes 196616 | tf_op jit(solution)/shard_map/ppermute | solution.py:43
  131.3 3.4 %collective-permute-done.24 = f32[32,512]{1,0:T(8,128)S(1)} collective-permute-done((f32[32,512]{1,0:T(8,128)S(1)}, f32[32,512]{1,0:T(8,128)S(1)}, u32[]{:S(2)}, u32[]{:S(2)}) %collective-permute-start.24) | collective-permute-done | bytes 65568 | tf_op jit(solution)/shard_map/ppermute | solution.py:43
  134.8 1.2 collective-permute-start.25
  136.8 13.6 %final_part.1 = (bf16[8192,512]{1,0:T(8,128)(2,1)}, bf16[8192,512]{1,0:T(8,128)(2,1)}, f32[64,512]{1,0:T(8,128)}, bf16[128,8192]{1,0:T(8,128)(2,1)}) custom-call(s32[1]{0:T(128)} %bitcast.core_ref, bf16[128,512]{1,0:T(8,128)(2,1)} %get-tuple-element.77.after.masked_own.near_own, ...), custom_call_target="tpu_custom_call", output_to_operand_aliasing={{3}: (7, {})} | custom-call | flops 1024 | bytes 1024 | tf_op jit(solution)/shard_map/final_part/pallas_call | solution.py:89
  (67 shorter events, 9.6 us)
Async XLA Ops:
  3.0 7.6 %collective-permute-start = (f32[64,128]{1,0:T(8,128)}, f32[64,128]{1,0:T(8,128)S(1)}, u32[]{:S(2)}, u32[]{:S(2)}) collective-permute-start(f32[64,128]{1,0:T(8,128)} %get-tuple-element.64), channel_id=1, source_target_pairs={{0,1},{1,0},{2,3},{3,2},{4,5},{5,4},{6,7},{7,6},{8,9},{9,8},{10,11... | collective-permute-start | bytes 98312 | tf_op jit(solution)/shard_map/ppermute | solution.py:43
  10.6 13.1 %collective-permute-start.1 = (bf16[32,8192]{1,0:T(8,128)(2,1)}, bf16[32,8192]{1,0:T(8,128)(2,1)S(1)}, u32[]{:S(2)}, u32[]{:S(2)}) collective-permute-start(bf16[32,8192]{1,0:T(8,128)(2,1)} %get-tuple-element.71), channel_id=1, source_target_pairs={{0,1},{1,0},{2,3},{3,2},{4,5},{5,4},{6,7},{7,6},{8,9},{9,8},{10,11... | collective-permute-start | bytes 1572872 | tf_op jit(solution)/shard_map/ppermute | solution.py:43
  10.7 13.6 %collective-permute-start.2 = (bf16[512,512]{1,0:T(8,128)(2,1)}, bf16[512,512]{1,0:T(8,128)(2,1)S(1)}, u32[]{:S(2)}, u32[]{:S(2)}) collective-permute-start(bf16[512,512]{1,0:T(8,128)(2,1)} %get-tuple-element.72), channel_id=1, source_target_pairs={{0,5},{1,4},{2,7},{3,6},{4,1},{5,0},{6,3},{7,2},{8,13},{9,12},{10,... | collective-permute-start | bytes 1572872 | tf_op jit(solution)/shard_map/ppermute | solution.py:43
  13.4 60.1 %copy-start.7 = (bf16[128,512]{1,0:T(8,128)(2,1)S(1)}, bf16[128,512]{1,0:T(8,128)(2,1)}, u32[]{:S(2)}) copy-start(bf16[128,512]{1,0:T(8,128)(2,1)} %get-tuple-element.86.masked_other) | copy-start | bytes 393220
  23.6 70.5 %copy-start.6 = (bf16[32,8192]{1,0:T(8,128)(2,1)}, bf16[32,8192]{1,0:T(8,128)(2,1)S(1)}, u32[]{:S(2)}) copy-start(bf16[32,8192]{1,0:T(8,128)(2,1)S(1)} %collective-permute-done.1.refs_1_) | copy-start | bytes 1572868
  24.3 4.9 %collective-permute-start.5 = (f32[16,64,256]{2,1,0:T(8,128)S(1)}, f32[16,64,256]{2,1,0:T(8,128)S(1)}, u32[]{:S(2)}, u32[]{:S(2)}) collective-permute-start(f32[16,64,256]{2,1,0:T(8,128)S(1)} %get-tuple-element.79), channel_id=1, source_target_pairs={{0,2},{1,3},{2,0},{3,1},{4,6},{5,7},{6,4},{7,5},{8,10},{9,11},{10,... | collective-permute-start | bytes 3145736 | tf_op jit(solution)/shard_map/ppermute | solution.py:43
  26.5 25.1 %collective-permute-start.3 = (bf16[64,8192]{1,0:T(8,128)(2,1)}, bf16[64,8192]{1,0:T(8,128)(2,1)S(1)}, u32[]{:S(2)}, u32[]{:S(2)}) collective-permute-start(bf16[64,8192]{1,0:T(8,128)(2,1)} %get-tuple-element.75), channel_id=1, source_target_pairs={{0,1},{1,0},{2,3},{3,2},{4,5},{5,4},{6,7},{7,6},{8,9},{9,8},{10,11... | collective-permute-start | bytes 3145736 | tf_op jit(solution)/shard_map/ppermute | solution.py:43
  26.7 26.0 %collective-permute-start.4 = (bf16[1024,512]{1,0:T(8,128)(2,1)}, bf16[1024,512]{1,0:T(8,128)(2,1)}, u32[]{:S(2)}, u32[]{:S(2)}) collective-permute-start(bf16[1024,512]{1,0:T(8,128)(2,1)} %get-tuple-element.76), channel_id=1, source_target_pairs={{0,5},{1,4},{2,7},{3,6},{4,1},{5,0},{6,3},{7,2},{8,13},{9,12},{10,... | collective-permute-start | bytes 3145736 | tf_op jit(solution)/shard_map/ppermute | solution.py:43
  30.3 24.1 %all-to-all-start = ((f32[16,64,256]{2,1,0:T(8,128)}), f32[16,64,256]{2,1,0:T(8,128)S(1)}, u32[]{:S(2)}, u32[]{:S(2)}) async-start(f32[16,64,256]{2,1,0:T(8,128)} %add.36), calls=%async_computation | async-start | bytes 2097152 | tf_op jit(solution)/shard_map/all_to_all | solution.py:558
  52.7 2.1 %collective-permute-start.6 = (bf16[128,512]{1,0:T(8,128)(2,1)S(1)}, bf16[128,512]{1,0:T(8,128)(2,1)S(1)}, u32[]{:S(2)}, u32[]{:S(2)}) collective-permute-start(bf16[128,512]{1,0:T(8,128)(2,1)S(1)} %copy-done.5), channel_id=1, source_target_pairs={{0,2},{1,3},{2,0},{3,1},{4,6},{5,7},{6,4},{7,5},{8,10},{9,11},{10,... | collective-permute-start | bytes 393224 | tf_op jit(solution)/shard_map/ppermute | solution.py:43
  54.8 48.7 %copy-start.9 = (bf16[128,512]{1,0:T(8,128)(2,1)}, bf16[128,512]{1,0:T(8,128)(2,1)S(1)}, u32[]{:S(2)}) copy-start(bf16[128,512]{1,0:T(8,128)(2,1)S(1)} %collective-permute-done.6.near_other) | copy-start | bytes 393220
  54.8 3.9 %collective-permute-start.9 = (f32[64,256]{1,0:T(8,128)S(1)}, f32[64,256]{1,0:T(8,128)S(1)}, u32[]{:S(2)}, u32[]{:S(2)}) collective-permute-start(f32[64,256]{1,0:T(8,128)S(1)} %reduce_sum.9), channel_id=1, source_target_pairs={{0,5},{1,0},{2,7},{3,2},{4,1},{5,4},{6,3},{7,6},{8,13},{9,8},{10,1... | collective-permute-start | bytes 196616 | tf_op jit(solution)/shard_map/ppermute | solution.py:43
  57.3 5.0 %collective-permute-start.8 = (f32[64,256]{1,0:T(8,128)S(1)}, f32[64,256]{1,0:T(8,128)S(1)}, u32[]{:S(2)}, u32[]{:S(2)}) collective-permute-start(f32[64,256]{1,0:T(8,128)S(1)} %reduce_sum.9), channel_id=1, source_target_pairs={{0,1},{1,4},{2,3},{3,6},{4,5},{5,0},{6,7},{7,2},{8,9},{9,12},{10,1... | collective-permute-start | bytes 196616 | tf_op jit(solution)/shard_map/ppermute | solution.py:43
  57.3 5.0 %collective-permute-start.7 = (f32[64,256]{1,0:T(8,128)S(1)}, f32[64,256]{1,0:T(8,128)S(1)}, u32[]{:S(2)}, u32[]{:S(2)}) collective-permute-start(f32[64,256]{1,0:T(8,128)S(1)} %reduce_sum.9), channel_id=1, source_target_pairs={{0,4},{1,5},{2,6},{3,7},{4,0},{5,1},{6,2},{7,3},{8,12},{9,13},{10,... | collective-permute-start | bytes 196616 | tf_op jit(solution)/shard_map/ppermute | solution.py:43
  63.4 24.6 %all-to-all-start.1 = ((f32[16,64,256]{2,1,0:T(8,128)}), f32[16,64,256]{2,1,0:T(8,128)S(1)}, u32[]{:S(2)}, u32[]{:S(2)}) async-start(f32[16,64,256]{2,1,0:T(8,128)} %broadcast_in_dim.17), calls=%async_computation.1 | async-start | bytes 2097152 | tf_op jit(solution)/shard_map/all_to_all | solution.py:569
  72.3 15.1 %collective-permute-start.11 = (bf16[544,512]{1,0:T(8,128)(2,1)}, bf16[544,512]{1,0:T(8,128)(2,1)}, u32[]{:S(2)}, u32[]{:S(2)}) collective-permute-start(bf16[544,512]{1,0:T(8,128)(2,1)} %get-tuple-element.89), channel_id=1, source_target_pairs={{0,5},{1,4},{2,7},{3,6},{4,1},{5,0},{6,3},{7,2},{8,13},{9,12},{10,... | collective-permute-start | bytes 1671176 | tf_op jit(solution)/shard_map/ppermute | solution.py:43
  73.5 13.9 %collective-permute-start.10 = (bf16[32,8192]{1,0:T(8,128)(2,1)}, bf16[32,8192]{1,0:T(8,128)(2,1)S(1)}, u32[]{:S(2)}, u32[]{:S(2)}) collective-permute-start(bf16[32,8192]{1,0:T(8,128)(2,1)} %get-tuple-element.88), channel_id=1, source_target_pairs={{0,1},{1,0},{2,3},{3,2},{4,5},{5,4},{6,7},{7,6},{8,9},{9,8},{10,11... | collective-permute-start | bytes 1572872 | tf_op jit(solution)/shard_map/ppermute | solution.py:43
  73.5 13.9 %collective-permute-start.12 = (bf16[128,512]{1,0:T(8,128)(2,1)S(1)}, bf16[128,512]{1,0:T(8,128)(2,1)S(1)}, u32[]{:S(2)}, u32[]{:S(2)}) collective-permute-start(bf16[128,512]{1,0:T(8,128)(2,1)S(1)} %copy-done.7), channel_id=1, source_target_pairs={{0,1},{1,0},{2,3},{3,2},{4,5},{5,4},{6,7},{7,6},{8,9},{9,8},{10,11... | collective-permute-start | bytes 393224 | tf_op jit(solution)/shard_map/ppermute | solution.py:43
  88.0 6.2 %collective-permute-start.13 = (f32[16,64,256]{2,1,0:T(8,128)S(1)}, f32[16,64,256]{2,1,0:T(8,128)S(1)}, u32[]{:S(2)}, u32[]{:S(2)}) collective-permute-start(f32[16,64,256]{2,1,0:T(8,128)S(1)} %all-to-all-done.1.mine), channel_id=1, source_target_pairs={{0,2},{1,3},{2,0},{3,1},{4,6},{5,7},{6,4},{7,5},{8,10},{9,11},{10,... | collective-permute-start | bytes 3145736 | tf_op jit(solution)/shard_map/ppermute | solution.py:43
  91.0 25.3 %collective-permute-start.20 = (bf16[1024,512]{1,0:T(8,128)(2,1)}, bf16[1024,512]{1,0:T(8,128)(2,1)}, u32[]{:S(2)}, u32[]{:S(2)}) collective-permute-start(bf16[1024,512]{1,0:T(8,128)(2,1)} %get-tuple-element.102), channel_id=1, source_target_pairs={{0,1},{1,0},{2,3},{3,2},{4,5},{5,4},{6,7},{7,6},{8,9},{9,8},{10,11... | collective-permute-start | bytes 3145736 | tf_op jit(solution)/shard_map/ppermute | solution.py:43
  91.0 25.3 %collective-permute-start.19 = (bf16[992,512]{1,0:T(8,128)(2,1)}, bf16[992,512]{1,0:T(8,128)(2,1)}, u32[]{:S(2)}, u32[]{:S(2)}) collective-permute-start(bf16[992,512]{1,0:T(8,128)(2,1)} %get-tuple-element.101), channel_id=1, source_target_pairs={{0,5},{1,4},{2,7},{3,6},{4,1},{5,0},{6,3},{7,2},{8,13},{9,12},{10,... | collective-permute-start | bytes 3047432 | tf_op jit(solution)/shard_map/ppermute | solution.py:43
  92.5 1.6 %collective-permute-start.14 = (bf16[128,512]{1,0:T(8,128)(2,1)S(1)}, bf16[128,512]{1,0:T(8,128)(2,1)S(1)}, u32[]{:S(2)}, u32[]{:S(2)}) collective-permute-start(bf16[128,512]{1,0:T(8,128)(2,1)S(1)} %collective-permute-done.12.far_own), channel_id=1, source_target_pairs={{0,2},{1,3},{2,0},{3,1},{4,6},{5,7},{6,4},{7,5},{8,10},{9,11},{10,... | collective-permute-start | bytes 393224 | tf_op jit(solution)/shard_map/ppermute | solution.py:43
  103.5 1.3 collective-permute-start.15
  104.9 11.4 %collective-permute-start.18 = (f32[32,512]{1,0:T(8,128)S(1)}, f32[32,512]{1,0:T(8,128)S(1)}, u32[]{:S(2)}, u32[]{:S(2)}) collective-permute-start(f32[32,512]{1,0:T(8,128)S(1)} %add.40), channel_id=1, source_target_pairs={{0,24},{1,25},{2,26},{3,27},{4,28},{5,29},{6,30},{7,31},{8,0},{9,1... | collective-permute-start | bytes 196616 | tf_op jit(solution)/shard_map/ppermute | solution.py:43
  107.5 8.8 %collective-permute-start.17 = (f32[32,512]{1,0:T(8,128)S(1)}, f32[32,512]{1,0:T(8,128)S(1)}, u32[]{:S(2)}, u32[]{:S(2)}) collective-permute-start(f32[32,512]{1,0:T(8,128)S(1)} %add.40), channel_id=1, source_target_pairs={{0,8},{1,9},{2,10},{3,11},{4,12},{5,13},{6,14},{7,15},{8,16},{9,17... | collective-permute-start | bytes 196616 | tf_op jit(solution)/shard_map/ppermute | solution.py:43
  107.5 8.8 %collective-permute-start.16 = (f32[32,512]{1,0:T(8,128)S(1)}, f32[32,512]{1,0:T(8,128)S(1)}, u32[]{:S(2)}, u32[]{:S(2)}) collective-permute-start(f32[32,512]{1,0:T(8,128)S(1)} %add.40), channel_id=1, source_target_pairs={{0,16},{1,17},{2,18},{3,19},{4,20},{5,21},{6,22},{7,23},{8,24},{9,... | collective-permute-start | bytes 196616 | tf_op jit(solution)/shard_map/ppermute | solution.py:43
  116.3 11.0 %collective-permute-start.23 = (f32[32,512]{1,0:T(8,128)S(1)}, f32[32,512]{1,0:T(8,128)S(1)}, u32[]{:S(2)}, u32[]{:S(2)}) collective-permute-start(f32[32,512]{1,0:T(8,128)S(1)} %add_add_fusion.1), channel_id=1, source_target_pairs={{0,96},{1,97},{2,98},{3,99},{4,100},{5,101},{6,102},{7,103},{8,104... | collective-permute-start | bytes 196616 | tf_op jit(solution)/shard_map/ppermute | solution.py:43
  118.8 8.6 %collective-permute-start.22 = (f32[32,512]{1,0:T(8,128)S(1)}, f32[32,512]{1,0:T(8,128)S(1)}, u32[]{:S(2)}, u32[]{:S(2)}) collective-permute-start(f32[32,512]{1,0:T(8,128)S(1)} %add_add_fusion.1), channel_id=1, source_target_pairs={{0,32},{1,33},{2,34},{3,35},{4,36},{5,37},{6,38},{7,39},{8,40},{9,... | collective-permute-start | bytes 196616 | tf_op jit(solution)/shard_map/ppermute | solution.py:43
  118.8 8.6 %collective-permute-start.21 = (f32[32,512]{1,0:T(8,128)S(1)}, f32[32,512]{1,0:T(8,128)S(1)}, u32[]{:S(2)}, u32[]{:S(2)}) collective-permute-start(f32[32,512]{1,0:T(8,128)S(1)} %add_add_fusion.1), channel_id=1, source_target_pairs={{0,64},{1,65},{2,66},{3,67},{4,68},{5,69},{6,70},{7,71},{8,72},{9,... | collective-permute-start | bytes 196616 | tf_op jit(solution)/shard_map/ppermute | solution.py:43
  127.4 9.4 %collective-permute-start.26 = (bf16[128,4096]{1,0:T(8,128)(2,1)S(1)}, bf16[128,4096]{1,0:T(8,128)(2,1)S(1)}, u32[]{:S(2)}, u32[]{:S(2)}) collective-permute-start(bf16[128,4096]{1,0:T(8,128)(2,1)S(1)} %get-tuple-element.114), channel_id=1, source_target_pairs={{0,2},{1,3},{2,0},{3,1},{4,6},{5,7},{6,4},{7,5},{8,10},{9,11},{10,... | collective-permute-start | bytes 3145736 | tf_op jit(solution)/shard_map/ppermute | solution.py:43
  129.6 5.2 %collective-permute-start.24 = (f32[32,512]{1,0:T(8,128)S(1)}, f32[32,512]{1,0:T(8,128)S(1)}, u32[]{:S(2)}, u32[]{:S(2)}) collective-permute-start(f32[32,512]{1,0:T(8,128)S(1)} %add_add_fusion), channel_id=1, source_target_pairs={{0,4},{1,5},{2,6},{3,7},{4,0},{5,1},{6,2},{7,3},{8,12},{9,13},{10,... | collective-permute-start | bytes 196616 | tf_op jit(solution)/shard_map/ppermute | solution.py:43
  134.8 2.1 %collective-permute-start.25 = (f32[32,512]{1,0:T(8,128)S(1)}, f32[32,512]{1,0:T(8,128)S(1)}, u32[]{:S(2)}, u32[]{:S(2)}) collective-permute-start(f32[32,512]{1,0:T(8,128)S(1)} %add.47.total), channel_id=1, source_target_pairs={{0,2},{1,3},{2,0},{3,1},{4,6},{5,7},{6,4},{7,5},{8,10},{9,11},{10,... | collective-permute-start | bytes 196616 | tf_op jit(solution)/shard_map/ppermute | solution.py:43
  (10 other events, 181.1 us)
